TPU v7x, 512 devices: a whole 4x4x16 slice. The times are simulated.
512 devices in a mesh: stream: 32 (over z, core), gy: 4 (over y), gz: 4 (over x).
Axes of the slice: x: 4, y: 4, z: 16, core: 2. Of those that a mesh axis runs over, the one named last changes fastest.
Arguments:
- right_side: bfloat16 [32, 4, 4, 625, 768], P('stream', 'gy', 'gz'), may hold values from -6 to 6
- inverse: bfloat16 [32, 4, 4, 625, 625], P('stream', 'gy', 'gz'), may hold values from -0.3 to 1.3
- coupling: bfloat16 [32, 4, 4, 6, 625, 125], P('stream', 'gy', 'gz'), may hold values from -0.2593839 to 0.2593839
- initial_guess: bfloat16 [32, 4, 4, 625, 768], P('stream', 'gy', 'gz'), may hold values from -6 to 6
- face_order: int32 [32, 4, 4, 6, 125], P('stream', 'gy', 'gz'), may hold values from 0 to 124, each once within a row
Outputs:
- updated: bfloat16 [32, 4, 4, 625, 768], P('stream', 'gy', 'gz')
Inputs may be any that keep to these rules, and one draw needn't show every extreme that they name: `face_order`: each element's row of each face is a permutation of 0 to 124.
All inputs are finite; a program needn't handle non-finite values.
Results may differ from a plain program's by a relative error of at most 0.0049.
Values may be sent and summed in bfloat16 or wider, within the bound.
No kernel may reach another device: no remote copies, remote signals or barrier semaphores. Data moves between devices by JAX's collectives and lax.ppermute only.
A program may use at most 64 MiB of HBM per device.

v0:
```python
import jax
import jax.numpy as jnp
from jax import lax
from jax.sharding import PartitionSpec as P

NODE = 5
VARS = 5


def passed_along(value, axis, steps):
    count = lax.axis_size(axis)
    leading, last = (max(0, -steps), min(count, count - steps))
    return lax.ppermute(value, axis, [(source, source + steps) for source in range(leading, last)])


def with_halo(block, sides, width):
    for axis, dim in sides:
        count = lax.axis_size(axis)
        forward = [(i, i + 1) for i in range(count - 1)]
        backward = [(target, source) for source, target in forward]
        low = lax.ppermute(
            lax.slice_in_dim(block, block.shape[dim] - width, None, axis=dim), axis, forward
        )
        high = lax.ppermute(lax.slice_in_dim(block, 0, width, axis=dim), axis, backward)
        block = jnp.concatenate([low, block, high], axis=dim)
    return block


def entering(value, axis, join, neutral):
    count, mine = (lax.axis_size(axis), lax.axis_index(axis))
    pieces = jax.tree.map(lambda part: lax.all_gather(part, axis), value)
    subtotal = jax.tree.map(
        lambda part, zero: jnp.full_like(part, 0) + jnp.asarray(zero, part.dtype), value, neutral
    )

    def turn(position, subtotal):
        longer = join(subtotal, jax.tree.map(lambda part: part[position], pieces))
        return jax.tree.map(lambda new, old: jnp.where(position < mine, new, old), longer, subtotal)

    return lax.fori_loop(0, count - 1, turn, subtotal)


def face_trace(values, which, side):
    shaped = values.reshape(values.shape[:-2] + (VARS, NODE, NODE, NODE, values.shape[-1]))
    picked = lax.index_in_dim(shaped, side, shaped.ndim - 4 + which, keepdims=False)
    return picked.reshape(values.shape[:-2] + (VARS * NODE * NODE, values.shape[-1]))


def on_device(right_side, inverse, coupling, initial_guess, face_order):
    highest = lax.Precision.HIGHEST
    guess_block = initial_guess[0, 0, 0]
    couple_block = coupling[0, 0, 0]
    order_block = face_order[0, 0, 0]
    inverse_block = inverse[0, 0, 0]
    downstream = passed_along(face_trace(guess_block, 0, 0), "stream", -1)
    padded = with_halo(initial_guess, (("gy", 1), ("gz", 2)), 1)
    lower_y = face_trace(padded[0, 0, 1], 1, NODE - 1)
    upper_y = face_trace(padded[0, 2, 1], 1, 0)
    lower_z = face_trace(padded[0, 1, 0], 2, NODE - 1)
    upper_z = face_trace(padded[0, 1, 2], 2, 0)
    stacked = jnp.stack([downstream, lower_y, upper_y, lower_z, upper_z])
    permuted = jnp.take_along_axis(stacked, order_block[1:, :, None], axis=1)
    pulled = jnp.einsum(
        "frt,ftc->rc", couple_block[1:], permuted, preferred_element_type=jnp.float32
    )
    residual_part = (right_side[0, 0, 0].astype(jnp.float32) - pulled).astype(jnp.bfloat16)
    solved = jnp.dot(inverse_block, residual_part, preferred_element_type=jnp.float32)
    upstream_gain = jnp.dot(inverse_block, couple_block[0], preferred_element_type=jnp.float32)
    trace_count = order_block.shape[1]
    selector = (
        order_block[0][:, None] == jnp.arange(trace_count, dtype=jnp.int32)[None, :]
    ).astype(jnp.float32)
    transfer_map = -jnp.dot(face_trace(upstream_gain, 0, NODE - 1), selector, precision=highest)
    offset = face_trace(solved, 0, NODE - 1)

    def compose(earlier, later):
        joined_map = jnp.dot(later[0], earlier[0], precision=highest)
        joined_offset = later[1] + jnp.dot(later[0], earlier[1], precision=highest)
        return (joined_map, joined_offset)

    neutral = (jnp.eye(trace_count, dtype=jnp.float32), jnp.zeros_like(offset))
    prefix = entering((transfer_map, offset), "stream", compose, neutral)
    arrived = jnp.take(prefix[1], order_block[0], axis=0)
    updated = solved - jnp.dot(upstream_gain, arrived, precision=highest)
    return updated.astype(jnp.bfloat16)[None, None, None]


def solution(mesh):
    return jax.shard_map(
        on_device,
        mesh=mesh,
        in_specs=(
            P("stream", "gy", "gz", None, None),
            P("stream", "gy", "gz", None, None),
            P("stream", "gy", "gz", None, None, None),
            P("stream", "gy", "gz", None, None),
            P("stream", "gy", "gz", None, None),
        ),
        out_specs=P("stream", "gy", "gz", None, None),
        check_vma=False,
    )
```

profile of v0, /device:TPU:24, one launch (start us, length us, event | category | flops | bytes accessed | tf_op | source)
XLA Modules:
  0.0 285.5 jit_solution(6721090218992465643)
XLA Ops:
  8.0 4.6 %collective-permute-start.2 = (bf16[1,1,1,625,768]{4,3,2,1,0:T(8,128)(2,1)}, bf16[1,1,1,625,768]{4,3,2,1,0:T(8,128)(2,1)S(1)}, u32[]{:S(2)}, u32[]{:S(2)}) collective-permute-start(bf16[1,1,1,625,768]{4,3,2,1,0:T(8,128)(2,1)} %param.10), channel_id=1, source_target_pairs={{4,0},{8,4},{12,8},{5,1},{9,5},{13,9},{6,2},{10,6},{14,10},{7,3},{... | collective-permute-start | bytes 2880008 | tf_op jit(solution)/shard_map/ppermute | solution.py:24
  15.7 16.4 %collective-permute-done.1 = bf16[1,1,1,625,768]{4,3,2,1,0:T(8,128)(2,1)} collective-permute-done((bf16[1,1,1,625,768]{4,3,2,1,0:T(8,128)(2,1)}, bf16[1,1,1,625,768]{4,3,2,1,0:T(8,128)(2,1)}, u32[]{:S(2)}, u32[]{:S(2)}) %collective-permute-start.1) | collective-permute-done | bytes 960032 | tf_op jit(solution)/shard_map/ppermute | solution.py:21
  32.1 2.2 constant_dynamic-update-slice_fusion.2
  36.5 5.0 %collective-permute-start.3 = (bf16[1,3,1,625,768]{4,3,2,1,0:T(8,128)(2,1)}, bf16[1,3,1,625,768]{4,3,2,1,0:T(8,128)(2,1)}, u32[]{:S(2)}, u32[]{:S(2)}) collective-permute-start(bf16[1,3,1,625,768]{4,3,2,1,0:T(8,128)(2,1)} %constant_dynamic-update-slice_fusion), channel_id=1, source_target_pairs={{0,1},{1,2},{2,3},{4,5},{5,6},{6,7},{8,9},{9,10},{10,11},{12,13},{... | collective-permute-start | bytes 8640008 | tf_op jit(solution)/shard_map/ppermute | solution.py:21
  43.7 1.5 reshape_squeeze.21
  47.8 1.9 collective-permute-done
  49.7 2.9 %reshape_squeeze.23 = bf16[5,5,5,5,768]{4,3,2,1,0:T(8,128)(2,1)} reshape(bf16[1,1,1,625,768]{4,3,2,1,0:T(8,128)(2,1)} %collective-permute-done.1) | data formatting | bytes 1920000 | tf_op jit(solution)/shard_map/reshape;squeeze | solution.py:44
  54.4 1.5 reshape_squeeze.24
  57.1 44.5 %collective-permute-done.3 = bf16[1,3,1,625,768]{4,3,2,1,0:T(8,128)(2,1)} collective-permute-done((bf16[1,3,1,625,768]{4,3,2,1,0:T(8,128)(2,1)}, bf16[1,3,1,625,768]{4,3,2,1,0:T(8,128)(2,1)}, u32[]{:S(2)}, u32[]{:S(2)}) %collective-permute-start.3) | collective-permute-done | bytes 2880032 | tf_op jit(solution)/shard_map/ppermute | solution.py:21
  104.4 2.6 slice_reduce_fusion.1
  111.1 2.4 slice_reduce_fusion
  113.7 9.0 %gather_fusion.1 = bf16[625,768]{1,0:T(8,128)(2,1)S(1)} fusion(bf16[5,125,768]{2,1,0:T(8,128)(2,1)S(1)} %constant_dynamic-update-slice_fusion.3, s32[625]{0:T(1024)S(1)} %reshape.108), kind=kCustom, calls=%fused_computation.1 | custom fusion | bytes 1925000 | tf_op jit(solution)/shard_map/jit(take_along_axis)/gather | solution.py:62
  123.9 4.5 %convolution_bitcast_fusion = f32[625,768]{1,0:T(8,128)S(1)} fusion(bf16[5,125,768]{2,1,0:T(8,128)(2,1)} %reshape.111, pred[5,125]{1,0:T(8,128)(4,1)S(1)} %compare_and_fusion, bf16[1,1,1,625,768]{4,3,2,1,0:T(8,128)(2,1)} %param.7, bf16[1,1,1,625,625]{4,3,2,1,0:T(8,128)(2,1)S(1)} %copy-done, bf16[1,1,1,6,625,125]{5,4,3,2,1,0:T(8,128)(2,1)} %param.9), kind=kOutput, calls=%fused_computation.14 | convolution fusion | flops 1201920000 | bytes 5464627 | tf_op jit(solution)/shard_map/dot_general | solution.py:67
  128.4 1.9 reshape.97
  132.7 91.0 %all-gather.5.cloned.1.call-done = f32[32,125,768]{2,1,0:T(8,128)} async-done(((f32[1,125,768]{2,1,0:T(8,128)}), f32[32,125,768]{2,1,0:T(8,128)}) %all-gather.5.cloned.1.call-update) | async-done | bytes 12288016 | tf_op jit(solution)/shard_map/all_gather | solution.py:31
  223.7 49.6 %while.14 = (s32[]{:T(128)}, f32[125,768]{1,0:T(8,128)S(1)}, s32[]{:T(128)}, f32[32,125,768]{2,1,0:T(8,128)}, f32[32,125,125]{2,1,0:T(8,128)}, /*index=5*/s32[]{:T(128)}, s32[]{:T(128)}) while((s32[]{:T(128)}, f32[125,768]{1,0:T(8,128)S(1)}, s32[]{:T(128)}, f32[32,125,768]{2,1,0:T(8,128)}, f32[32,125,125]{2,1,0:T(8,128)}, ...), condition=%wide.region_1.2_spmd.clone, body=%wide.region_0.0_spmd.clone.sunk | while | flops 144384000 | bytes 2399839 | solution.py:40
  223.7 1.5 fusion.46
  225.3 1.5 fusion.46
  226.9 1.5 fusion.46
  228.5 1.5 fusion.46
  231.7 1.5 fusion.46
  234.9 1.5 fusion.46
  273.3 1.5 gather_fusion
  274.8 3.8 %fusion.9 = bf16[1,1,1,625,768]{4,3,2,1,0:T(8,128)(2,1)} fusion(f32[625,768]{1,0:T(8,128)S(1)} %convolution_bitcast_fusion, f32[625,125]{1,0:T(8,128)S(1)} %fusion.16, f32[125,768]{1,0:T(8,128)} %gather_fusion, pred[125]{0:T(512)(128)(4,1)S(1)} %compare_and_fusion.1), kind=kOutput, calls=%fused_computation.15 | convolution fusion | flops 721056000 | bytes 3576625 | tf_op jit(solution)/shard_map/dot_general | solution.py:84
  (112 shorter events, 64.0 us)
Async XLA Ops:
  6.5 6.0 %copy-start = (bf16[1,1,1,625,625]{4,3,2,1,0:T(8,128)(2,1)S(1)}, bf16[1,1,1,625,625]{4,3,2,1,0:T(8,128)(2,1)}, u32[]{:S(2)}) copy-start(bf16[1,1,1,625,625]{4,3,2,1,0:T(8,128)(2,1)} %param.8) | copy-start | bytes 2343754
  6.5 27.8 %copy-start.1 = (bf16[1,1,1,625,768]{4,3,2,1,0:T(8,128)(2,1)S(1)}, bf16[1,1,1,625,768]{4,3,2,1,0:T(8,128)(2,1)}, u32[]{:S(2)}) copy-start(bf16[1,1,1,625,768]{4,3,2,1,0:T(8,128)(2,1)} %param.10) | copy-start | bytes 2880004
  6.5 126.2 %all-gather.7.cloned.1.call-start = ((), (), s32[]{:S(2)}) async-start(), calls=%async_computation.1 | async-start | bytes 2162688 | tf_op jit(solution)/shard_map/all_gather | solution.py:31
  6.5 25.6 %collective-permute-start.1 = (bf16[1,1,1,625,768]{4,3,2,1,0:T(8,128)(2,1)}, bf16[1,1,1,625,768]{4,3,2,1,0:T(8,128)(2,1)}, u32[]{:S(2)}, u32[]{:S(2)}) collective-permute-start(bf16[1,1,1,625,768]{4,3,2,1,0:T(8,128)(2,1)} %param.10), channel_id=1, source_target_pairs={{0,4},{4,8},{8,12},{1,5},{5,9},{9,13},{2,6},{6,10},{10,14},{3,7},{... | collective-permute-start | bytes 2880008 | tf_op jit(solution)/shard_map/ppermute | solution.py:21
  8.0 27.4 %collective-permute-start.2 = (bf16[1,1,1,625,768]{4,3,2,1,0:T(8,128)(2,1)}, bf16[1,1,1,625,768]{4,3,2,1,0:T(8,128)(2,1)S(1)}, u32[]{:S(2)}, u32[]{:S(2)}) collective-permute-start(bf16[1,1,1,625,768]{4,3,2,1,0:T(8,128)(2,1)} %param.10), channel_id=1, source_target_pairs={{4,0},{8,4},{12,8},{5,1},{9,5},{13,9},{6,2},{10,6},{14,10},{7,3},{... | collective-permute-start | bytes 2880008 | tf_op jit(solution)/shard_map/ppermute | solution.py:24
  34.3 7.1 %copy-start.3 = (s32[1,1,1,6,125]{4,2,3,1,0:T(1,128)S(1)}, s32[1,1,1,6,125]{4,2,3,1,0:T(1,128)}, u32[]{:S(2)}) copy-start(s32[1,1,1,6,125]{4,2,3,1,0:T(1,128)} %param.11) | copy-start | bytes 9004
  36.5 65.2 %collective-permute-start.3 = (bf16[1,3,1,625,768]{4,3,2,1,0:T(8,128)(2,1)}, bf16[1,3,1,625,768]{4,3,2,1,0:T(8,128)(2,1)}, u32[]{:S(2)}, u32[]{:S(2)}) collective-permute-start(bf16[1,3,1,625,768]{4,3,2,1,0:T(8,128)(2,1)} %constant_dynamic-update-slice_fusion), channel_id=1, source_target_pairs={{0,1},{1,2},{2,3},{4,5},{5,6},{6,7},{8,9},{9,10},{10,11},{12,13},{... | collective-permute-start | bytes 8640008 | tf_op jit(solution)/shard_map/ppermute | solution.py:21
  41.5 6.3 %slice-start = ((s32[1,1,1,6,125]{4,2,3,1,0:T(1,128)}), s32[1,1,1,5,125]{4,2,3,1,0:T(1,128)S(1)}, s32[]{:S(2)}) async-start(s32[1,1,1,6,125]{4,2,3,1,0:T(1,128)} %param.11), calls=%async_computation.2 | async-start | bytes 5120 | tf_op jit(solution)/shard_map/slice | solution.py:62
  42.4 181.3 %all-gather.5.cloned.1.call-start = ((), (), s32[]{:S(2)}) async-start(), calls=%async_computation | async-start | bytes 12976128 | tf_op jit(solution)/shard_map/all_gather | solution.py:31
  42.4 65.9 %collective-permute-start.4 = (bf16[1,3,1,625,768]{4,3,2,1,0:T(8,128)(2,1)}, bf16[1,3,1,625,768]{4,3,2,1,0:T(8,128)(2,1)}, u32[]{:S(2)}, u32[]{:S(2)}) collective-permute-start(bf16[1,3,1,625,768]{4,3,2,1,0:T(8,128)(2,1)} %constant_dynamic-update-slice_fusion), channel_id=1, source_target_pairs={{1,0},{2,1},{3,2},{5,4},{6,5},{7,6},{9,8},{10,9},{11,10},{13,12},{... | collective-permute-start | bytes 8640008 | tf_op jit(solution)/shard_map/ppermute | solution.py:24
  46.4 3.3 %collective-permute-start = (bf16[125,768]{1,0:T(8,128)(2,1)S(1)}, bf16[125,768]{1,0:T(8,128)(2,1)S(1)}, u32[]{:S(2)}, u32[]{:S(2)}) collective-permute-start(bf16[125,768]{1,0:T(8,128)(2,1)S(1)} %reshape_squeeze.22), channel_id=1, source_target_pairs={{16,0},{32,16},{48,32},{64,48},{80,64},{96,80},{112,96},{128,112},... | collective-permute-start | bytes 576008 | tf_op jit(solution)/shard_map/ppermute | solution.py:13
  54.4 2.6 copy-start.2
Sparse Core Ops, SparseCore 0:
  42.5 74.0 all-gather.6
  132.8 90.8 all-gather.4
where the time goes:
time: 288 us; the launch traced here: 285 us
  waiting for transfers between devices  155 us (54%)
  matrix products  58.1 us (20%)
  local copies, waits for them, and re-layouts  43.7 us (15%)
  starting transfers between devices  13.7 us (5%)
  between operations  13.6 us (5%)
    all_gather x2, waiting for transfers between devices, entering(): pieces = jax.tree.map(lambda part: lax.all_gather(part, axis), value)  91 us
    ppermute x2, waiting for transfers between devices, with_halo(): lax.ppermute(lax.slice_in_dim(block, block.shape[dim] - width, None, axis...  61 us
    dot_general x31, matrix products, compose(): joined_offset = later[1] + jnp.dot(later[0], earlier[1], precision=highest)  47.6 us
    gather x3, local copies, waits for them, and re-layouts, on_device(): permuted = jnp.take_along_axis(stacked, order_block[1:, :, None], axis=1)  10.3 us
    another operation x5, local copies, waits for them, and re-layouts, face_trace(): values.reshape(values.shape[:-2] + (VARS, NODE, NODE, NODE, values.shape[...  9.03 us
    unnamed x19, local copies, waits for them, and re-layouts  7.56 us
    ppermute x2, starting transfers between devices, with_halo(): lax.ppermute(lax.slice_in_dim(block, block.shape[dim] - width, None, axis...  6.42 us
    slice x3, local copies, waits for them, and re-layouts, face_trace(): lax.index_in_dim(shaped, side, shaped.ndim - 4 + which, keepdims=False)  6.1 us
  transfers between devices with their start and end apart: 7, of which 5 were waited for; matrix products, arithmetic and copies ran while one was open for 16% of the time, Pallas kernels for 0%

commit v1 on v0

v1 whole, which is shorter than its diff:
```python
import jax
import jax.numpy as jnp
from jax import lax
from jax.experimental import pallas as pl
from jax.experimental.pallas import tpu as pltpu
from jax.sharding import PartitionSpec as P

NODE = 5
TRACE = 125
WIDE = 128
FACES = 5
GROUP = 8
f32, bf16 = jnp.float32, jnp.bfloat16
WIRE = f32
GRANT = 40 * 1024 * 1024


def params(*semantics):
    return pltpu.CompilerParams(vmem_limit_bytes=GRANT, dimension_semantics=semantics or None)


def dot(left, right, contract=(1, 0)):
    dims = (((contract[0],), (contract[1],)), ((), ()))
    return lax.dot_general(left, right, dims, preferred_element_type=f32)


def halves(value):
    high = value.astype(bf16)
    return high, (value - high.astype(f32)).astype(bf16)


def split_left(value):
    high, low = halves(value)
    return jnp.concatenate([high, low, high], axis=1)


def split_right(value, axis):
    high, low = halves(value)
    return jnp.concatenate([high, high, low], axis=axis)


def trace_rows(which, side):
    at = lax.broadcasted_iota(jnp.int32, (WIDE, 1), 0)
    var = (at * 41) >> 10
    rest = at - 25 * var
    slow = (rest * 13) >> 6
    fast = rest - 5 * slow
    place = [side, slow, fast]
    if which == 1:
        place = [slow, side, fast]
    if which == 2:
        place = [slow, fast, side]
    row = var * 125 + place[0] * 25 + place[1] * 5 + place[2]
    row = jnp.where(at < TRACE, row, -1)
    column = lax.broadcasted_iota(jnp.int32, (WIDE, 625), 1)
    return (row == column).astype(f32).astype(bf16)


SENT = ((0, 0), (1, NODE - 1), (1, 0), (2, NODE - 1), (2, 0))


def traces_kernel(guess, *outs):
    for (which, side), out in zip(SENT, outs):
        out[...] = dot(trace_rows(which, side), guess[...]).astype(bf16)


def maps_kernel(inverse, coupling, order, couple_out, gain_out, inverse_out, map_out):
    node = lax.broadcasted_iota(jnp.int32, (WIDE, TRACE), 0)

    def permuted(face):
        pick = (node == order[face : face + 1, :]).astype(f32).astype(bf16)
        return dot(coupling[face], pick, (1, 1)).astype(bf16)

    for face in range(1, 6):
        couple_out[:, (face - 1) * WIDE : face * WIDE] = permuted(face)
    first = permuted(0)
    gain_out[...] = split_left(dot(inverse[...], first))
    picked = dot(trace_rows(0, NODE - 1), inverse[...]).astype(bf16)
    inverse_out[...] = picked
    map_out[...] = -dot(picked, first).T


def offset_kernel(right_side, couple, t1, t2, t3, t4, t5, inverse, maps, residual_out, send_out):
    traces = jnp.concatenate([t[...] for t in (t1, t2, t3, t4, t5)], axis=0)
    pulled = dot(couple[...], traces)
    residual = (right_side[...].astype(f32) - pulled).astype(bf16)
    residual_out[...] = residual
    offset = dot(inverse[...], residual).T
    part = send_out.shape[1] - WIDE
    for at in range(send_out.shape[0]):
        send_out[at, :part, :] = offset[at * part : (at + 1) * part].astype(WIRE)
        send_out[at, part:, :] = maps[...].astype(WIRE)


def scan_kernel(received, states_out, last_out):
    count, rows, _ = received.shape
    part = rows - WIDE
    state = received[0].astype(f32)
    for at in range(1, count):
        states_out[at - 1] = state
        step = received[at].astype(f32)
        moved = dot(split_left(state), split_right(step[part:], 0))
        state = jnp.concatenate([moved[:part] + step[:part], moved[part:]], axis=0)
    last_out[...] = state.astype(WIRE)


def prefix_kernel(group, totals, states, out):
    count, part, _ = out.shape
    entering = jnp.zeros((part, WIDE), f32)
    for at in range(totals.shape[0] - 1):
        total = totals[at].astype(f32)
        longer = total[:part]
        if at > 0:
            longer = longer + dot(split_left(entering), split_right(total[part:], 0))
        entering = jnp.where(at < group[0], longer, entering)
    out[0] = entering.astype(WIRE)
    left = split_left(entering)
    for at in range(1, count):
        state = states[at - 1]
        moved = dot(left, split_right(state[part:], 0))
        out[at] = (state[:part] + moved).astype(WIRE)


def update_kernel(inverse, residual, gain, arrived, out):
    solved = dot(inverse[...], residual[...])
    moved = dot(gain[...], split_right(arrived[...].astype(f32), 1), (1, 1))
    out[...] = (solved - moved).astype(bf16)


def on_device(right_side, inverse, coupling, initial_guess, face_order):
    rows, width = right_side.shape[-2:]
    right_side, inverse, guess = right_side[0, 0, 0], inverse[0, 0, 0], initial_guess[0, 0, 0]
    coupling, order = coupling[0, 0, 0], face_order[0, 0, 0]
    count = lax.axis_size("stream")
    groups = count // GROUP
    part = width // GROUP
    near = [[g * GROUP + i for i in range(GROUP)] for g in range(groups)]
    far = [[g * GROUP + i for g in range(groups)] for i in range(GROUP)]

    def whole(*shape):
        return pl.BlockSpec(shape, lambda *_: (0,) * len(shape))

    def columns(size, block):
        return pl.BlockSpec((size, block), lambda i: (0, i))

    traces = pl.pallas_call(
        traces_kernel,
        grid=(3,),
        in_specs=[columns(rows, width // 3)],
        out_specs=[columns(WIDE, width // 3)] * FACES,
        out_shape=[jax.ShapeDtypeStruct((WIDE, width), bf16)] * FACES,
        compiler_params=params("arbitrary"),
        name="face_traces",
    )(guess)

    def shifted(value, axis, step):
        size = lax.axis_size(axis)
        pairs = [(i, i + step) for i in range(size) if 0 <= i + step < size]
        return lax.ppermute(value, axis, pairs)

    moves = (("stream", -1), ("gy", 1), ("gy", -1), ("gz", 1), ("gz", -1))
    halos = [shifted(value, axis, step) for value, (axis, step) in zip(traces, moves)]

    couple, gain, picked, maps = pl.pallas_call(
        maps_kernel,
        out_shape=[
            jax.ShapeDtypeStruct((rows, FACES * WIDE), bf16),
            jax.ShapeDtypeStruct((rows, 3 * WIDE), bf16),
            jax.ShapeDtypeStruct((WIDE, rows), bf16),
            jax.ShapeDtypeStruct((WIDE, WIDE), f32),
        ],
        compiler_params=params(),
        name="element_maps",
    )(inverse, coupling, order)

    block = width // 2
    residual, sent = pl.pallas_call(
        offset_kernel,
        grid=(2,),
        in_specs=[columns(rows, block), whole(rows, FACES * WIDE)]
        + [columns(WIDE, block)] * FACES
        + [whole(WIDE, rows), whole(WIDE, WIDE)],
        out_specs=[
            columns(rows, block),
            pl.BlockSpec((GROUP // 2, part + WIDE, WIDE), lambda i: (i, 0, 0)),
        ],
        out_shape=[
            jax.ShapeDtypeStruct((rows, width), bf16),
            jax.ShapeDtypeStruct((GROUP, part + WIDE, WIDE), WIRE),
        ],
        compiler_params=params("arbitrary"),
        name="residual_offset",
    )(right_side, couple, *halos, picked, maps)

    received = lax.all_to_all(sent, "stream", 0, 0, tiled=True, axis_index_groups=near)
    states, last = pl.pallas_call(
        scan_kernel,
        out_shape=[
            jax.ShapeDtypeStruct((GROUP - 1, part + WIDE, WIDE), f32),
            jax.ShapeDtypeStruct((part + WIDE, WIDE), WIRE),
        ],
        compiler_params=params(),
        name="group_scan",
    )(received)

    totals = lax.all_gather(last, "stream", axis_index_groups=far)
    group = (lax.axis_index("stream") // GROUP).astype(jnp.int32).reshape(1)
    entering = pl.pallas_call(
        prefix_kernel,
        in_specs=[
            pl.BlockSpec(memory_space=pltpu.SMEM),
            pl.BlockSpec(memory_space=pltpu.VMEM),
            pl.BlockSpec(memory_space=pltpu.VMEM),
        ],
        out_shape=jax.ShapeDtypeStruct((GROUP, part, WIDE), WIRE),
        compiler_params=params(),
        name="group_prefix",
    )(group, totals, states)
    arrived = lax.all_to_all(entering, "stream", 0, 0, tiled=True, axis_index_groups=near)

    updated = pl.pallas_call(
        update_kernel,
        grid=(3,),
        in_specs=[
            whole(rows, rows),
            columns(rows, width // 3),
            whole(rows, 3 * WIDE),
            pl.BlockSpec((width // 3, WIDE), lambda i: (i, 0)),
        ],
        out_specs=columns(rows, width // 3),
        out_shape=jax.ShapeDtypeStruct((rows, width), bf16),
        compiler_params=params("arbitrary"),
        name="update",
    )(inverse, residual, gain, arrived.reshape(width, WIDE))
    return updated[None, None, None]


def solution(mesh):
    return jax.shard_map(
        on_device,
        mesh=mesh,
        in_specs=(
            P("stream", "gy", "gz", None, None),
            P("stream", "gy", "gz", None, None),
            P("stream", "gy", "gz", None, None, None),
            P("stream", "gy", "gz", None, None),
            P("stream", "gy", "gz", None, None),
        ),
        out_specs=P("stream", "gy", "gz", None, None),
        check_vma=False,
    )
```

time: 288 us -> 107 us (0.37)
  waiting for transfers between devices: 155 us -> 29.1 us
  matrix products: 58.1 us -> 0 us
  blocking collectives: 0 us -> 46.7 us
  local copies, waits for them, and re-layouts: 43.7 us -> 3.4 us
  between operations: 13.6 us -> 0.15 us
  Pallas kernels: 0 us -> 8.95 us
  starting transfers between devices: 13.7 us -> 17.9 us
    all_gather x2 -> x0, waiting for transfers between devices: 91 us -> none  [entering(): pieces = jax.tree.map(lambda part: lax.all_gather(part, axis), value)]
    ppermute x5, waiting for transfers between devices: 64.2 us -> 5.32 us  [shifted(): return lax.ppermute(value, axis, pairs)]
    dot_general x35 -> x0, matrix products: 58.1 us -> none  [the longest x31 47.6 us: compose(): joined_offset = later[1] + jnp.dot(later[0], earlier[1], precision=highest)]
    all_gather x0 -> x1, blocking collectives: none -> 31.7 us  [on_device(): totals = lax.all_gather(last, 'stream', axis_index_groups=far)]
    all_to_all x0 -> x1, waiting for transfers between devices: none -> 23.8 us  [on_device(): lax.all_to_all(sent, 'stream', 0, 0, tiled=True, axis_index_groups=near)]
    all_to_all x0 -> x1, blocking collectives: none -> 14.9 us  [on_device(): lax.all_to_all(entering, 'stream', 0, 0, tiled=True, axis_index_groups=near)]
    gather x4 -> x0, local copies, waits for them, and re-layouts: 11.8 us -> none  [the longest x3 10.3 us: on_device(): permuted = jnp.take_along_axis(stacked, order_block[1:, :, None], axis=1)]
    another operation x13 -> x0, local copies, waits for them, and re-layouts: 10.9 us -> none  [the longest x5 9.03 us: face_trace(): values.reshape(values.shape[:-2] + (VARS, NODE, NODE, NODE, values.shape[...]
  transfers between devices with their start and end apart: 7 -> 6, of which waited for: 5 -> 3; matrix products, arithmetic and copies ran while one was open for 16% -> 0% of each run, Pallas kernels for 0% -> 1%
where the time goes in v1:
time: 107 us; the launch traced here: 106 us
  blocking collectives  46.7 us (44%)
  waiting for transfers between devices  29.1 us (27%)
  starting transfers between devices  17.9 us (17%)
  Pallas kernels  8.95 us (8%)
  local copies, waits for them, and re-layouts  3.4 us (3%)
    all_gather x1, blocking collectives, on_device(): totals = lax.all_gather(last, 'stream', axis_index_groups=far)  31.7 us
    all_to_all x1, waiting for transfers between devices, on_device(): lax.all_to_all(sent, 'stream', 0, 0, tiled=True, axis_index_groups=near)  23.8 us
    all_to_all x1, blocking collectives, on_device(): lax.all_to_all(entering, 'stream', 0, 0, tiled=True, axis_index_groups=near)  14.9 us
    ppermute x5, starting transfers between devices, shifted(): return lax.ppermute(value, axis, pairs)  12 us
    all_to_all x1, starting transfers between devices, on_device(): lax.all_to_all(sent, 'stream', 0, 0, tiled=True, axis_index_groups=near)  5.9 us
    ppermute x5, waiting for transfers between devices, shifted(): return lax.ppermute(value, axis, pairs)  5.32 us
    unnamed x13, local copies, waits for them, and re-layouts  3.4 us
    pallas_call x1, Pallas kernels, on_device(): pl.pallas_call(update_kernel, grid=(3,), in_specs=[whole(rows, rows), col...  2.67 us
  transfers between devices with their start and end apart: 6, of which 3 were waited for; matrix products, arithmetic and copies ran while one was open for 0% of the time, Pallas kernels for 1%

profile of v1, /device:TPU:24, one launch (start us, length us, event | category | flops | bytes accessed | tf_op | source)
XLA Modules:
  0.0 106.2 jit_solution(15892285378150530936)
XLA Ops:
  0.0 1.3 %copy-done.2 = bf16[1,1,1,625,768]{4,3,2,1,0:T(8,128)(2,1)S(1)} copy-done((bf16[1,1,1,625,768]{4,3,2,1,0:T(8,128)(2,1)S(1)}, bf16[1,1,1,625,768]{4,3,2,1,0:T(8,128)(2,1)}, u32[]{:S(2)}) %copy-start.2) | copy-done | bytes 960024
  1.3 1.5 %face_traces.1 = (bf16[128,768]{1,0:T(8,128)(2,1)S(1)}, bf16[128,768]{1,0:T(8,128)(2,1)S(1)}, bf16[128,768]{1,0:T(8,128)(2,1)S(1)}, bf16[128,768]{1,0:T(8,128)(2,1)S(1)}, bf16[128,768]{1,0:T(8,128)(2,1)S(1)}) custom-call(bf16[625,768]{1,0:T(8,128)(2,1)S(1)} %bitcast.16), custom_call_target="tpu_custom_call" | custom-call | tf_op jit(solution)/shard_map/face_traces/pallas_call | solution.py:146
  2.8 0.0 copy-start.1
  2.8 1.4 %collective-permute-start = (bf16[128,768]{1,0:T(8,128)(2,1)S(1)}, bf16[128,768]{1,0:T(8,128)(2,1)S(1)}, u32[]{:S(2)}, u32[]{:S(2)}) collective-permute-start(bf16[128,768]{1,0:T(8,128)(2,1)S(1)} %get-tuple-element.19), channel_id=1, source_target_pairs={{16,0},{32,16},{48,32},{64,48},{80,64},{96,80},{112,96},{128,112},... | collective-permute-start | bytes 589832 | tf_op jit(solution)/shard_map/ppermute | solution.py:159
  4.2 1.3 %collective-permute-start.1 = (bf16[128,768]{1,0:T(8,128)(2,1)S(1)}, bf16[128,768]{1,0:T(8,128)(2,1)S(1)}, u32[]{:S(2)}, u32[]{:S(2)}) collective-permute-start(bf16[128,768]{1,0:T(8,128)(2,1)S(1)} %get-tuple-element.20), channel_id=1, source_target_pairs={{0,4},{4,8},{8,12},{1,5},{5,9},{9,13},{2,6},{6,10},{10,14},{3,7},{... | collective-permute-start | bytes 589832 | tf_op jit(solution)/shard_map/ppermute | solution.py:159
  5.5 4.6 %collective-permute-start.2 = (bf16[128,768]{1,0:T(8,128)(2,1)S(1)}, bf16[128,768]{1,0:T(8,128)(2,1)S(1)}, u32[]{:S(2)}, u32[]{:S(2)}) collective-permute-start(bf16[128,768]{1,0:T(8,128)(2,1)S(1)} %get-tuple-element.21), channel_id=1, source_target_pairs={{4,0},{8,4},{12,8},{5,1},{9,5},{13,9},{6,2},{10,6},{14,10},{7,3},{... | collective-permute-start | bytes 589832 | tf_op jit(solution)/shard_map/ppermute | solution.py:159
  10.1 3.4 %collective-permute-start.3 = (bf16[128,768]{1,0:T(8,128)(2,1)S(1)}, bf16[128,768]{1,0:T(8,128)(2,1)S(1)}, u32[]{:S(2)}, u32[]{:S(2)}) collective-permute-start(bf16[128,768]{1,0:T(8,128)(2,1)S(1)} %get-tuple-element.22), channel_id=1, source_target_pairs={{0,1},{1,2},{2,3},{4,5},{5,6},{6,7},{8,9},{9,10},{10,11},{12,13},{... | collective-permute-start | bytes 589832 | tf_op jit(solution)/shard_map/ppermute | solution.py:159
  13.5 1.3 %collective-permute-start.4 = (bf16[128,768]{1,0:T(8,128)(2,1)S(1)}, bf16[128,768]{1,0:T(8,128)(2,1)S(1)}, u32[]{:S(2)}, u32[]{:S(2)}) collective-permute-start(bf16[128,768]{1,0:T(8,128)(2,1)S(1)} %get-tuple-element.23), channel_id=1, source_target_pairs={{1,0},{2,1},{3,2},{5,4},{6,5},{7,6},{9,8},{10,9},{11,10},{13,12},{... | collective-permute-start | bytes 589832 | tf_op jit(solution)/shard_map/ppermute | solution.py:159
  14.8 0.0 copy-start.3
  14.8 1.2 %copy-done.3 = bf16[1,1,1,6,625,125]{5,4,3,2,1,0:T(8,128)(2,1)S(1)} copy-done((bf16[1,1,1,6,625,125]{5,4,3,2,1,0:T(8,128)(2,1)S(1)}, bf16[1,1,1,6,625,125]{5,4,3,2,1,0:T(8,128)(2,1)}, u32[]{:S(2)}) %copy-start.3) | copy-done | bytes 937524
  16.0 1.1 %element_maps.1 = (bf16[625,640]{1,0:T(8,128)(2,1)S(1)}, bf16[625,384]{1,0:T(8,128)(2,1)S(1)}, bf16[128,625]{1,0:T(8,128)(2,1)S(1)}, f32[128,128]{1,0:T(8,128)S(1)}) custom-call(bf16[625,625]{1,0:T(8,128)(2,1)S(1)} %bitcast.11, bf16[6,625,125]{2,1,0:T(8,128)(2,1)S(1)} %bitcast.17, s32[6,125]{1,0:T(8,128)S(1)} %bitcast.18), custom_call_target="tpu_custom_call" | custom-call | tf_op jit(solution)/shard_map/element_maps/pallas_call | solution.py:164
  17.1 0.0 collective-permute-done.t1
  17.2 1.2 %collective-permute-done.3.t4 = bf16[128,768]{1,0:T(8,128)(2,1)S(1)} collective-permute-done((bf16[128,768]{1,0:T(8,128)(2,1)S(1)}, bf16[128,768]{1,0:T(8,128)(2,1)S(1)}, u32[]{:S(2)}, u32[]{:S(2)}) %collective-permute-start.3) | collective-permute-done | bytes 196640 | tf_op jit(solution)/shard_map/ppermute | solution.py:159
  18.4 4.1 %collective-permute-done.4.t5 = bf16[128,768]{1,0:T(8,128)(2,1)S(1)} collective-permute-done((bf16[128,768]{1,0:T(8,128)(2,1)S(1)}, bf16[128,768]{1,0:T(8,128)(2,1)S(1)}, u32[]{:S(2)}, u32[]{:S(2)}) %collective-permute-start.4) | collective-permute-done | bytes 196640 | tf_op jit(solution)/shard_map/ppermute | solution.py:159
  22.5 2.1 %residual_offset.1 = (bf16[625,768]{1,0:T(8,128)(2,1)S(1)}, f32[8,224,128]{2,1,0:T(8,128)S(1)}) custom-call(bf16[625,768]{1,0:T(8,128)(2,1)S(1)} %bitcast.15, bf16[625,640]{1,0:T(8,128)(2,1)S(1)} %get-tuple-element.18.couple, bf16[128,768]{1,0:T(8,128)(2,1)S(1)} %collective-permute-done.t1, bf16[128,768]{1,0:T(8,128)(2,1)S(1)} %collective-permute-done.1.t2, ...), custom_call_target="tpu_custom_call" | custom-call | tf_op jit(solution)/shard_map/residual_offset/pallas_call | solution.py:177
  24.6 0.0 copy-start.4
  24.7 0.9 copy-done.4
  25.6 5.9 %all-to-all-start = ((f32[8,224,128]{2,1,0:T(8,128)}), f32[8,224,128]{2,1,0:T(8,128)S(1)}, u32[]{:S(2)}, u32[]{:S(2)}) async-start(f32[8,224,128]{2,1,0:T(8,128)} %copy-done.4), calls=%async_computation | async-start | bytes 1835008 | tf_op jit(solution)/shard_map/all_to_all | solution.py:195
  31.5 23.8 %all-to-all-done.received = f32[8,224,128]{2,1,0:T(8,128)S(1)} async-done(((f32[8,224,128]{2,1,0:T(8,128)}), f32[8,224,128]{2,1,0:T(8,128)S(1)}, u32[]{:S(2)}, u32[]{:S(2)}) %all-to-all-start) | async-done | bytes 917536 | tf_op jit(solution)/shard_map/all_to_all | solution.py:195
  55.3 1.0 group_scan.1
  56.2 31.7 %all-gather = f32[896,128]{1,0:T(8,128)S(1)} all-gather(f32[224,128]{1,0:T(8,128)S(1)} %get-tuple-element.29), channel_id=2, replica_groups={{0,128,256,384},{16,144,272,400},{32,160,288,416},{48,176,304,432},{64,..., dimensions={0}, use_global_device_ids=true | all-gather | bytes 573440 | tf_op jit(solution)/shard_map/all_gather | solution.py:206
  88.0 0.6 group_prefix.1
  88.5 14.9 %all_to_all.10 = f32[8,96,128]{2,1,0:T(8,128)S(1)} all-to-all(f32[8,96,128]{2,1,0:T(8,128)S(1)} %group_prefix.1), channel_id=1, replica_groups={{0,16,32,48,64,80,96,112},{128,144,160,176,192,208,224,240},{256,272,28..., dimensions={0} | all-to-all | bytes 786432 | tf_op jit(solution)/shard_map/all_to_all | solution.py:219
  103.5 2.7 %update.1 = bf16[625,768]{1,0:T(8,128)(2,1)} custom-call(bf16[625,625]{1,0:T(8,128)(2,1)S(1)} %bitcast.12, bf16[625,768]{1,0:T(8,128)(2,1)S(1)} %get-tuple-element.26.residual, bf16[625,384]{1,0:T(8,128)(2,1)S(1)} %get-tuple-element.27.gain, f32[768,128]{1,0:T(8,128)S(1)} %bitcast.14), custom_call_target="tpu_custom_call" | custom-call | tf_op jit(solution)/shard_map/update/pallas_call | solution.py:221
  (9 shorter events, 0.0 us)
Async XLA Ops:
  0.0 14.8 %copy-start = (bf16[1,1,1,625,625]{4,3,2,1,0:T(8,128)(2,1)S(1)}, bf16[1,1,1,625,625]{4,3,2,1,0:T(8,128)(2,1)}, u32[]{:S(2)}) copy-start(bf16[1,1,1,625,625]{4,3,2,1,0:T(8,128)(2,1)} %param.6) | copy-start | bytes 2343754
  0.0 1.3 %copy-start.2 = (bf16[1,1,1,625,768]{4,3,2,1,0:T(8,128)(2,1)S(1)}, bf16[1,1,1,625,768]{4,3,2,1,0:T(8,128)(2,1)}, u32[]{:S(2)}) copy-start(bf16[1,1,1,625,768]{4,3,2,1,0:T(8,128)(2,1)} %param.8) | copy-start | bytes 2880004
  1.3 13.5 %copy-start.5 = (s32[1,1,1,6,125]{4,2,3,1,0:T(1,128)S(1)}, s32[1,1,1,6,125]{4,2,3,1,0:T(1,128)}, u32[]{:S(2)}) copy-start(s32[1,1,1,6,125]{4,2,3,1,0:T(1,128)} %param.9) | copy-start | bytes 9004
  2.8 19.7 %copy-start.1 = (bf16[1,1,1,625,768]{4,3,2,1,0:T(8,128)(2,1)S(1)}, bf16[1,1,1,625,768]{4,3,2,1,0:T(8,128)(2,1)}, u32[]{:S(2)}) copy-start(bf16[1,1,1,625,768]{4,3,2,1,0:T(8,128)(2,1)} %param.5) | copy-start | bytes 2880004
  2.8 14.4 %collective-permute-start = (bf16[128,768]{1,0:T(8,128)(2,1)S(1)}, bf16[128,768]{1,0:T(8,128)(2,1)S(1)}, u32[]{:S(2)}, u32[]{:S(2)}) collective-permute-start(bf16[128,768]{1,0:T(8,128)(2,1)S(1)} %get-tuple-element.19), channel_id=1, source_target_pairs={{16,0},{32,16},{48,32},{64,48},{80,64},{96,80},{112,96},{128,112},... | collective-permute-start | bytes 589832 | tf_op jit(solution)/shard_map/ppermute | solution.py:159
  4.2 12.9 %collective-permute-start.1 = (bf16[128,768]{1,0:T(8,128)(2,1)S(1)}, bf16[128,768]{1,0:T(8,128)(2,1)S(1)}, u32[]{:S(2)}, u32[]{:S(2)}) collective-permute-start(bf16[128,768]{1,0:T(8,128)(2,1)S(1)} %get-tuple-element.20), channel_id=1, source_target_pairs={{0,4},{4,8},{8,12},{1,5},{5,9},{9,13},{2,6},{6,10},{10,14},{3,7},{... | collective-permute-start | bytes 589832 | tf_op jit(solution)/shard_map/ppermute | solution.py:159
  5.5 11.6 %collective-permute-start.2 = (bf16[128,768]{1,0:T(8,128)(2,1)S(1)}, bf16[128,768]{1,0:T(8,128)(2,1)S(1)}, u32[]{:S(2)}, u32[]{:S(2)}) collective-permute-start(bf16[128,768]{1,0:T(8,128)(2,1)S(1)} %get-tuple-element.21), channel_id=1, source_target_pairs={{4,0},{8,4},{12,8},{5,1},{9,5},{13,9},{6,2},{10,6},{14,10},{7,3},{... | collective-permute-start | bytes 589832 | tf_op jit(solution)/shard_map/ppermute | solution.py:159
  10.1 8.3 %collective-permute-start.3 = (bf16[128,768]{1,0:T(8,128)(2,1)S(1)}, bf16[128,768]{1,0:T(8,128)(2,1)S(1)}, u32[]{:S(2)}, u32[]{:S(2)}) collective-permute-start(bf16[128,768]{1,0:T(8,128)(2,1)S(1)} %get-tuple-element.22), channel_id=1, source_target_pairs={{0,1},{1,2},{2,3},{4,5},{5,6},{6,7},{8,9},{9,10},{10,11},{12,13},{... | collective-permute-start | bytes 589832 | tf_op jit(solution)/shard_map/ppermute | solution.py:159
  13.5 9.0 %collective-permute-start.4 = (bf16[128,768]{1,0:T(8,128)(2,1)S(1)}, bf16[128,768]{1,0:T(8,128)(2,1)S(1)}, u32[]{:S(2)}, u32[]{:S(2)}) collective-permute-start(bf16[128,768]{1,0:T(8,128)(2,1)S(1)} %get-tuple-element.23), channel_id=1, source_target_pairs={{1,0},{2,1},{3,2},{5,4},{6,5},{7,6},{9,8},{10,9},{11,10},{13,12},{... | collective-permute-start | bytes 589832 | tf_op jit(solution)/shard_map/ppermute | solution.py:159
  14.8 1.2 %copy-start.3 = (bf16[1,1,1,6,625,125]{5,4,3,2,1,0:T(8,128)(2,1)S(1)}, bf16[1,1,1,6,625,125]{5,4,3,2,1,0:T(8,128)(2,1)}, u32[]{:S(2)}) copy-start(bf16[1,1,1,6,625,125]{5,4,3,2,1,0:T(8,128)(2,1)} %param.7) | copy-start | bytes 2812504
  24.6 0.9 copy-start.4
  25.6 29.7 %all-to-all-start = ((f32[8,224,128]{2,1,0:T(8,128)}), f32[8,224,128]{2,1,0:T(8,128)S(1)}, u32[]{:S(2)}, u32[]{:S(2)}) async-start(f32[8,224,128]{2,1,0:T(8,128)} %copy-done.4), calls=%async_computation | async-start | bytes 1835008 | tf_op jit(solution)/shard_map/all_to_all | solution.py:195

commit v2 on v1

v2 whole, which is shorter than its diff:
```python
import jax
import jax.numpy as jnp
from jax import lax
from jax.experimental import pallas as pl
from jax.experimental.pallas import tpu as pltpu
from jax.sharding import PartitionSpec as P

NODE = 5
TRACE = 125
WIDE = 128
FACES = 5
GROUP = 8
f32, bf16 = jnp.float32, jnp.bfloat16
WIRE = jnp.int16
GRANT = 40 * 1024 * 1024


def params():
    return pltpu.CompilerParams(vmem_limit_bytes=GRANT)


def dot(left, right, contract=(1, 0)):
    dims = (((contract[0],), (contract[1],)), ((), ()))
    return lax.dot_general(left, right, dims, preferred_element_type=f32)


def halves(value):
    high = value.astype(bf16)
    return high, (value - high.astype(f32)).astype(bf16)


def split_left(value):
    high, low = halves(value)
    return jnp.concatenate([high, low, high], axis=1)


def split_right(value, axis):
    high, low = halves(value)
    return jnp.concatenate([high, high, low], axis=axis)


def coded(value):
    lane = lax.broadcasted_iota(jnp.int32, value.shape, 1)
    top = jnp.max(jnp.abs(value), axis=1, keepdims=True)
    power = jnp.minimum(jnp.ceil(jnp.log2(jnp.maximum(top, 1e-30))), 127.0)
    fraction = jnp.round(value * jnp.exp2(13.9 - power))
    return jnp.where(lane == WIDE - 1, power, fraction).astype(jnp.int32).astype(WIRE)


def decoded(block):
    value = block.astype(jnp.int32).astype(f32)
    lane = lax.broadcasted_iota(jnp.int32, value.shape, 1)
    power = value[:, WIDE - 1 :]
    return jnp.where(lane == WIDE - 1, 0.0, value * jnp.exp2(power - 13.9))


def trace_rows(which, side):
    at = lax.broadcasted_iota(jnp.int32, (WIDE, 1), 0)
    var = (at * 41) >> 10
    rest = at - 25 * var
    slow = (rest * 13) >> 6
    fast = rest - 5 * slow
    place = [side, slow, fast]
    if which == 1:
        place = [slow, side, fast]
    if which == 2:
        place = [slow, fast, side]
    row = var * 125 + place[0] * 25 + place[1] * 5 + place[2]
    row = jnp.where(at < TRACE, row, -1)
    column = lax.broadcasted_iota(jnp.int32, (WIDE, 625), 1)
    return (row == column).astype(f32).astype(bf16)


SENT = ((0, 0), (1, NODE - 1), (1, 0), (2, NODE - 1), (2, 0))


def traces_kernel(guess, *refs):
    outs, (held, sems) = refs[:FACES], refs[FACES:]
    block = WIDE * 2
    cuts = [slice(at, at + block) for at in range(0, held.shape[1], block)]
    copies = [
        pltpu.make_async_copy(guess.at[:, cut], held.at[:, cut], sems.at[at])
        for at, cut in enumerate(cuts)
    ]
    for copy in copies:
        copy.start()
    picks = [trace_rows(which, side) for which, side in SENT]
    for copy, cut in zip(copies, cuts):
        copy.wait()
        for pick, out in zip(picks, outs):
            out[:, cut] = dot(pick, held[:, cut]).astype(bf16)


def maps_kernel(inverse, coupling, order, couple_out, gain_out, inverse_out, map_out):
    node = lax.broadcasted_iota(jnp.int32, (WIDE, TRACE), 0)

    def permuted(face):
        pick = (node == order[face : face + 1, :]).astype(f32).astype(bf16)
        return dot(coupling[face], pick, (1, 1)).astype(bf16)

    for face in range(1, 6):
        couple_out[:, (face - 1) * WIDE : face * WIDE] = permuted(face)
    first = permuted(0)
    gain_out[...] = split_left(dot(inverse[...], first))
    picked = dot(trace_rows(0, NODE - 1), inverse[...]).astype(bf16)
    inverse_out[...] = picked
    map_out[...] = -dot(picked, first).T


def offset_kernel(right_side, couple, t1, t2, t3, t4, t5, inverse, maps, residual_out, send_out):
    count, rows, _ = send_out.shape
    part = rows - WIDE
    step = coded(maps[...])
    for start in range(0, count, count // 2):
        cut = slice(start * part, (start + count // 2) * part)
        traces = jnp.concatenate([t[:, cut] for t in (t1, t2, t3, t4, t5)], axis=0)
        pulled = dot(couple[...], traces)
        residual = (right_side[:, cut].astype(f32) - pulled).astype(bf16)
        residual_out[:, cut] = residual
        offset = coded(dot(inverse[...], residual).T)
        for at in range(count // 2):
            send_out[start + at, :part, :] = offset[at * part : (at + 1) * part]
            send_out[start + at, part:, :] = step


def scan_kernel(received, states_out, total_out):
    count, rows, _ = received.shape
    part = rows - WIDE
    state = decoded(received[0])
    for at in range(1, count):
        states_out[at - 1] = state
        step = decoded(received[at])
        moved = dot(split_left(state), split_right(step[part:], 0))
        state = jnp.concatenate([moved[:part] + step[:part], moved[part:]], axis=0)
    states_out[count - 1] = state
    total_out[...] = coded(state[:part])


def passing_kernel(entering, last, out):
    part = out.shape[0]
    moved = dot(split_left(decoded(entering[...])), split_right(last[0, part:], 0))
    out[...] = coded(last[0, :part] + moved)


def prefix_kernel(*refs):
    entries, states, out = refs[:-2], refs[-2], refs[-1]
    count, part, _ = out.shape
    entering = sum(decoded(entry[...]) for entry in entries)
    out[0] = coded(entering)
    left = split_left(entering)
    for at in range(1, count):
        state = states[at - 1]
        moved = dot(left, split_right(state[part:], 0))
        out[at] = coded(state[:part] + moved)


def update_kernel(inverse, residual, gain, arrived, out, held, sems):
    block = WIDE * 2
    copies = []
    for at, start in enumerate(range(0, held.shape[1], block)):
        cut = slice(start, start + block)
        moved = dot(gain[...], split_right(decoded(arrived[cut, :]), 1), (1, 1))
        held[:, cut] = (dot(inverse[...], residual[:, cut]) - moved).astype(bf16)
        copies.append(pltpu.make_async_copy(held.at[:, cut], out.at[:, cut], sems.at[at]))
        copies[-1].start()
    for copy in copies:
        copy.wait()


def on_device(right_side, inverse, coupling, initial_guess, face_order):
    rows, width = right_side.shape[-2:]
    right_side, inverse, guess = right_side[0, 0, 0], inverse[0, 0, 0], initial_guess[0, 0, 0]
    coupling, order = coupling[0, 0, 0], face_order[0, 0, 0]
    count = lax.axis_size("stream")
    groups = count // GROUP
    part = width // GROUP
    near = [[g * GROUP + i for i in range(GROUP)] for g in range(groups)]

    outer = pl.BlockSpec(memory_space=pltpu.HBM)
    blocks = width // (2 * WIDE)

    traces = pl.pallas_call(
        traces_kernel,
        in_specs=[outer],
        out_shape=[jax.ShapeDtypeStruct((WIDE, width), bf16)] * FACES,
        scratch_shapes=[pltpu.VMEM((rows, width), bf16), pltpu.SemaphoreType.DMA((blocks,))],
        compiler_params=params(),
        name="face_traces",
    )(guess)

    def shifted(value, axis, step):
        size = lax.axis_size(axis)
        pairs = [(i, i + step) for i in range(size) if 0 <= i + step < size]
        return lax.ppermute(value, axis, pairs)

    moves = (("stream", -1), ("gy", 1), ("gy", -1), ("gz", 1), ("gz", -1))
    halos = [shifted(value, axis, step) for value, (axis, step) in zip(traces, moves)]

    couple, gain, picked, maps = pl.pallas_call(
        maps_kernel,
        out_shape=[
            jax.ShapeDtypeStruct((rows, FACES * WIDE), bf16),
            jax.ShapeDtypeStruct((rows, 3 * WIDE), bf16),
            jax.ShapeDtypeStruct((WIDE, rows), bf16),
            jax.ShapeDtypeStruct((WIDE, WIDE), f32),
        ],
        compiler_params=params(),
        name="element_maps",
    )(inverse, coupling, order)

    residual, sent = pl.pallas_call(
        offset_kernel,
        out_shape=[
            jax.ShapeDtypeStruct((rows, width), bf16),
            jax.ShapeDtypeStruct((GROUP, part + WIDE, WIDE), WIRE),
        ],
        compiler_params=params(),
        name="residual_offset",
    )(right_side, couple, *halos, picked, maps)

    received = lax.all_to_all(sent, "stream", 0, 0, tiled=True, axis_index_groups=near)
    states, total = pl.pallas_call(
        scan_kernel,
        out_shape=[
            jax.ShapeDtypeStruct((GROUP, part + WIDE, WIDE), f32),
            jax.ShapeDtypeStruct((part, WIDE), WIRE),
        ],
        compiler_params=params(),
        name="group_scan",
    )(received)

    entries = []
    for g in range(groups - 1):
        pairs = [(g * GROUP + i, (g + 1) * GROUP + i) for i in range(GROUP)]
        entries.append(lax.ppermute(total, "stream", pairs))
        if g < groups - 2:
            total = pl.pallas_call(
                passing_kernel,
                grid=(1,),
                in_specs=[
                    pl.BlockSpec((part, WIDE), lambda i: (0, 0)),
                    pl.BlockSpec((1, part + WIDE, WIDE), lambda i: (GROUP - 1, 0, 0)),
                ],
                out_specs=pl.BlockSpec((part, WIDE), lambda i: (0, 0)),
                out_shape=jax.ShapeDtypeStruct((part, WIDE), WIRE),
                compiler_params=params(),
                name="group_total",
            )(entries[-1], states)
    entering = pl.pallas_call(
        prefix_kernel,
        out_shape=jax.ShapeDtypeStruct((GROUP, part, WIDE), WIRE),
        compiler_params=params(),
        name="group_prefix",
    )(*entries, states)
    arrived = lax.all_to_all(entering, "stream", 0, 0, tiled=True, axis_index_groups=near)

    updated = pl.pallas_call(
        update_kernel,
        out_specs=outer,
        out_shape=jax.ShapeDtypeStruct((rows, width), bf16),
        scratch_shapes=[pltpu.VMEM((rows, width), bf16), pltpu.SemaphoreType.DMA((blocks,))],
        compiler_params=params(),
        name="update",
    )(inverse, residual, gain, arrived.reshape(width, WIDE))
    return updated[None, None, None]


def solution(mesh):
    return jax.shard_map(
        on_device,
        mesh=mesh,
        in_specs=(
            P("stream", "gy", "gz", None, None),
            P("stream", "gy", "gz", None, None),
            P("stream", "gy", "gz", None, None, None),
            P("stream", "gy", "gz", None, None),
            P("stream", "gy", "gz", None, None),
        ),
        out_specs=P("stream", "gy", "gz", None, None),
        check_vma=False,
    )
```

time: 107 us -> 78 us (0.73)
  the two profiles are of different devices: /device:TPU:24 before, /device:TPU:392 now
where the time goes in v2:
time: 78 us; the launch traced here: 77.6 us
  blocking collectives  27.1 us (35%)
  waiting for transfers between devices  21.8 us (28%)
  starting transfers between devices  16.9 us (22%)
  Pallas kernels  9.19 us (12%)
  local copies, waits for them, and re-layouts  2.48 us (3%)
    ppermute x3, waiting for transfers between devices, on_device(): entries.append(lax.ppermute(total, 'stream', pairs))  17.9 us
    all_to_all x1, blocking collectives, on_device(): lax.all_to_all(sent, 'stream', 0, 0, tiled=True, axis_index_groups=near)  16.4 us
    ppermute x5, starting transfers between devices, shifted(): return lax.ppermute(value, axis, pairs)  14.2 us
    all_to_all x1, blocking collectives, on_device(): lax.all_to_all(entering, 'stream', 0, 0, tiled=True, axis_index_groups=near)  10.8 us
    ppermute x5, waiting for transfers between devices, shifted(): return lax.ppermute(value, axis, pairs)  3.89 us
    ppermute x3, starting transfers between devices, on_device(): entries.append(lax.ppermute(total, 'stream', pairs))  2.62 us
    unnamed x11, local copies, waits for them, and re-layouts  2.48 us
    pallas_call x1, Pallas kernels, on_device(): pl.pallas_call(update_kernel, out_specs=outer, out_shape=jax.ShapeDtypeSt...  2.31 us
  transfers between devices with their start and end apart: 8, of which 2 were waited for; matrix products, arithmetic and copies ran while one was open for 0% of the time, Pallas kernels for 1%

profile of v2, /device:TPU:392, one launch (start us, length us, event | category | flops | bytes accessed | tf_op | source)
XLA Modules:
  0.0 77.6 jit_solution(14533658111724064633)
XLA Ops:
  0.0 1.3 %copy-done.2 = bf16[1,1,1,625,768]{4,3,2,1,0:T(8,128)(2,1)S(1)} copy-done((bf16[1,1,1,625,768]{4,3,2,1,0:T(8,128)(2,1)S(1)}, bf16[1,1,1,625,768]{4,3,2,1,0:T(8,128)(2,1)}, u32[]{:S(2)}) %copy-start.2) | copy-done | bytes 960024
  1.3 1.7 %face_traces.1 = (bf16[128,768]{1,0:T(8,128)(2,1)S(1)}, bf16[128,768]{1,0:T(8,128)(2,1)S(1)}, bf16[128,768]{1,0:T(8,128)(2,1)S(1)}, bf16[128,768]{1,0:T(8,128)(2,1)S(1)}, bf16[128,768]{1,0:T(8,128)(2,1)S(1)}) custom-call(bf16[625,768]{1,0:T(8,128)(2,1)S(1)} %bitcast.12), custom_call_target="tpu_custom_call" | custom-call | tf_op jit(solution)/shard_map/face_traces/pallas_call | solution.py:182
  3.0 0.0 copy-start.1
  3.0 3.7 %collective-permute-start = (bf16[128,768]{1,0:T(8,128)(2,1)S(1)}, bf16[128,768]{1,0:T(8,128)(2,1)S(1)}, u32[]{:S(2)}, u32[]{:S(2)}) collective-permute-start(bf16[128,768]{1,0:T(8,128)(2,1)S(1)} %get-tuple-element.19), channel_id=1, source_target_pairs={{16,0},{32,16},{48,32},{64,48},{80,64},{96,80},{112,96},{128,112},... | collective-permute-start | bytes 589832 | tf_op jit(solution)/shard_map/ppermute | solution.py:194
  6.7 3.5 %collective-permute-start.1 = (bf16[128,768]{1,0:T(8,128)(2,1)S(1)}, bf16[128,768]{1,0:T(8,128)(2,1)S(1)}, u32[]{:S(2)}, u32[]{:S(2)}) collective-permute-start(bf16[128,768]{1,0:T(8,128)(2,1)S(1)} %get-tuple-element.20), channel_id=1, source_target_pairs={{0,4},{4,8},{8,12},{1,5},{5,9},{9,13},{2,6},{6,10},{10,14},{3,7},{... | collective-permute-start | bytes 589832 | tf_op jit(solution)/shard_map/ppermute | solution.py:194
  10.2 2.4 %collective-permute-start.2 = (bf16[128,768]{1,0:T(8,128)(2,1)S(1)}, bf16[128,768]{1,0:T(8,128)(2,1)S(1)}, u32[]{:S(2)}, u32[]{:S(2)}) collective-permute-start(bf16[128,768]{1,0:T(8,128)(2,1)S(1)} %get-tuple-element.21), channel_id=1, source_target_pairs={{4,0},{8,4},{12,8},{5,1},{9,5},{13,9},{6,2},{10,6},{14,10},{7,3},{... | collective-permute-start | bytes 589832 | tf_op jit(solution)/shard_map/ppermute | solution.py:194
  12.6 3.4 %collective-permute-start.3 = (bf16[128,768]{1,0:T(8,128)(2,1)S(1)}, bf16[128,768]{1,0:T(8,128)(2,1)S(1)}, u32[]{:S(2)}, u32[]{:S(2)}) collective-permute-start(bf16[128,768]{1,0:T(8,128)(2,1)S(1)} %get-tuple-element.22), channel_id=1, source_target_pairs={{0,1},{1,2},{2,3},{4,5},{5,6},{6,7},{8,9},{9,10},{10,11},{12,13},{... | collective-permute-start | bytes 589832 | tf_op jit(solution)/shard_map/ppermute | solution.py:194
  16.0 1.3 %collective-permute-start.4 = (bf16[128,768]{1,0:T(8,128)(2,1)S(1)}, bf16[128,768]{1,0:T(8,128)(2,1)S(1)}, u32[]{:S(2)}, u32[]{:S(2)}) collective-permute-start(bf16[128,768]{1,0:T(8,128)(2,1)S(1)} %get-tuple-element.23), channel_id=1, source_target_pairs={{1,0},{2,1},{3,2},{5,4},{6,5},{7,6},{9,8},{10,9},{11,10},{13,12},{... | collective-permute-start | bytes 589832 | tf_op jit(solution)/shard_map/ppermute | solution.py:194
  17.3 0.0 copy-start.3
  17.3 1.2 %copy-done.3 = bf16[1,1,1,6,625,125]{5,4,3,2,1,0:T(8,128)(2,1)S(1)} copy-done((bf16[1,1,1,6,625,125]{5,4,3,2,1,0:T(8,128)(2,1)S(1)}, bf16[1,1,1,6,625,125]{5,4,3,2,1,0:T(8,128)(2,1)}, u32[]{:S(2)}) %copy-start.3) | copy-done | bytes 937524
  18.5 1.1 %element_maps.1 = (bf16[625,640]{1,0:T(8,128)(2,1)S(1)}, bf16[625,384]{1,0:T(8,128)(2,1)S(1)}, bf16[128,625]{1,0:T(8,128)(2,1)S(1)}, f32[128,128]{1,0:T(8,128)S(1)}) custom-call(bf16[625,625]{1,0:T(8,128)(2,1)S(1)} %bitcast.9, bf16[6,625,125]{2,1,0:T(8,128)(2,1)S(1)} %bitcast.13, s32[6,125]{1,0:T(8,128)S(1)} %bitcast.15), custom_call_target="tpu_custom_call" | custom-call | tf_op jit(solution)/shard_map/element_maps/pallas_call | solution.py:199
  19.7 3.9 %collective-permute-done.4.t5 = bf16[128,768]{1,0:T(8,128)(2,1)S(1)} collective-permute-done((bf16[128,768]{1,0:T(8,128)(2,1)S(1)}, bf16[128,768]{1,0:T(8,128)(2,1)S(1)}, u32[]{:S(2)}, u32[]{:S(2)}) %collective-permute-start.4) | collective-permute-done | bytes 196640 | tf_op jit(solution)/shard_map/ppermute | solution.py:194
  23.6 1.8 %residual_offset.1 = (bf16[625,768]{1,0:T(8,128)(2,1)S(1)}, s16[8,224,128]{2,1,0:T(8,128)(2,1)S(1)}) custom-call(bf16[625,768]{1,0:T(8,128)(2,1)S(1)} %bitcast.11, bf16[625,640]{1,0:T(8,128)(2,1)S(1)} %get-tuple-element.18.couple, bf16[128,768]{1,0:T(8,128)(2,1)S(1)} %collective-permute-done.t1, bf16[128,768]{1,0:T(8,128)(2,1)S(1)} %collective-permute-done.1.t2, ...), custom_call_target="tpu_custom_call" | custom-call | tf_op jit(solution)/shard_map/residual_offset/pallas_call | solution.py:211
  25.3 16.4 %all_to_all.10.received = s16[8,224,128]{2,1,0:T(8,128)(2,1)S(1)} all-to-all(s16[8,224,128]{2,1,0:T(8,128)(2,1)S(1)} %get-tuple-element.28), channel_id=1, replica_groups={{0,16,32,48,64,80,96,112},{128,144,160,176,192,208,224,240},{256,272,28..., dimensions={0} | all-to-all | bytes 917504 | tf_op jit(solution)/shard_map/all_to_all | solution.py:221
  41.7 1.1 %group_scan.1 = (f32[8,224,128]{2,1,0:T(8,128)S(1)}, s16[96,128]{1,0:T(8,128)(2,1)S(1)}) custom-call(s16[8,224,128]{2,1,0:T(8,128)(2,1)S(1)} %all_to_all.10.received), custom_call_target="tpu_custom_call" | custom-call | tf_op jit(solution)/shard_map/group_scan/pallas_call | solution.py:222
  42.8 0.7 collective-permute-start.5
  43.5 0.3 group_total.2
  43.9 0.7 collective-permute-start.6
  44.5 0.3 group_total.3
  44.9 1.3 %collective-permute-start.7 = (s16[96,128]{1,0:T(8,128)(2,1)S(1)}, s16[96,128]{1,0:T(8,128)(2,1)S(1)}, u32[]{:S(2)}, u32[]{:S(2)}) collective-permute-start(s16[96,128]{1,0:T(8,128)(2,1)S(1)} %group_total.3), channel_id=1, source_target_pairs={{256,384},{272,400},{288,416},{304,432},{320,448},{336,464},{352,4... | collective-permute-start | bytes 73736 | tf_op jit(solution)/shard_map/ppermute | solution.py:235
  46.2 17.9 %collective-permute-done.7.refs_2_ = s16[96,128]{1,0:T(8,128)(2,1)S(1)} collective-permute-done((s16[96,128]{1,0:T(8,128)(2,1)S(1)}, s16[96,128]{1,0:T(8,128)(2,1)S(1)}, u32[]{:S(2)}, u32[]{:S(2)}) %collective-permute-start.7) | collective-permute-done | bytes 24608 | tf_op jit(solution)/shard_map/ppermute | solution.py:235
  64.0 0.5 group_prefix.1
  64.6 10.8 %all_to_all.11 = s16[8,96,128]{2,1,0:T(8,128)(2,1)S(1)} all-to-all(s16[8,96,128]{2,1,0:T(8,128)(2,1)S(1)} %group_prefix.1), channel_id=1, replica_groups={{0,16,32,48,64,80,96,112},{128,144,160,176,192,208,224,240},{256,272,28..., dimensions={0} | all-to-all | bytes 393216 | tf_op jit(solution)/shard_map/all_to_all | solution.py:255
  75.3 2.3 %update.1 = bf16[625,768]{1,0:T(8,128)(2,1)} custom-call(bf16[625,625]{1,0:T(8,128)(2,1)S(1)} %bitcast.10, bf16[625,768]{1,0:T(8,128)(2,1)S(1)} %get-tuple-element.26.residual, bf16[625,384]{1,0:T(8,128)(2,1)S(1)} %get-tuple-element.27.gain, s16[768,128]{1,0:T(8,128)(2,1)S(1)} %bitcast.14), custom_call_target="tpu_custom_call" | custom-call | tf_op jit(solution)/shard_map/update/pallas_call | solution.py:257
  (13 shorter events, 0.0 us)
Async XLA Ops:
  0.0 17.3 %copy-start = (bf16[1,1,1,625,625]{4,3,2,1,0:T(8,128)(2,1)S(1)}, bf16[1,1,1,625,625]{4,3,2,1,0:T(8,128)(2,1)}, u32[]{:S(2)}) copy-start(bf16[1,1,1,625,625]{4,3,2,1,0:T(8,128)(2,1)} %param.6) | copy-start | bytes 2343754
  0.0 1.3 %copy-start.2 = (bf16[1,1,1,625,768]{4,3,2,1,0:T(8,128)(2,1)S(1)}, bf16[1,1,1,625,768]{4,3,2,1,0:T(8,128)(2,1)}, u32[]{:S(2)}) copy-start(bf16[1,1,1,625,768]{4,3,2,1,0:T(8,128)(2,1)} %param.8) | copy-start | bytes 2880004
  1.3 16.0 %copy-start.4 = (s32[1,1,1,6,125]{4,2,3,1,0:T(1,128)S(1)}, s32[1,1,1,6,125]{4,2,3,1,0:T(1,128)}, u32[]{:S(2)}) copy-start(s32[1,1,1,6,125]{4,2,3,1,0:T(1,128)} %param.9) | copy-start | bytes 9004
  3.0 20.6 %copy-start.1 = (bf16[1,1,1,625,768]{4,3,2,1,0:T(8,128)(2,1)S(1)}, bf16[1,1,1,625,768]{4,3,2,1,0:T(8,128)(2,1)}, u32[]{:S(2)}) copy-start(bf16[1,1,1,625,768]{4,3,2,1,0:T(8,128)(2,1)} %param.5) | copy-start | bytes 2880004
  3.0 16.6 %collective-permute-start = (bf16[128,768]{1,0:T(8,128)(2,1)S(1)}, bf16[128,768]{1,0:T(8,128)(2,1)S(1)}, u32[]{:S(2)}, u32[]{:S(2)}) collective-permute-start(bf16[128,768]{1,0:T(8,128)(2,1)S(1)} %get-tuple-element.19), channel_id=1, source_target_pairs={{16,0},{32,16},{48,32},{64,48},{80,64},{96,80},{112,96},{128,112},... | collective-permute-start | bytes 589832 | tf_op jit(solution)/shard_map/ppermute | solution.py:194
  6.7 12.9 %collective-permute-start.1 = (bf16[128,768]{1,0:T(8,128)(2,1)S(1)}, bf16[128,768]{1,0:T(8,128)(2,1)S(1)}, u32[]{:S(2)}, u32[]{:S(2)}) collective-permute-start(bf16[128,768]{1,0:T(8,128)(2,1)S(1)} %get-tuple-element.20), channel_id=1, source_target_pairs={{0,4},{4,8},{8,12},{1,5},{5,9},{9,13},{2,6},{6,10},{10,14},{3,7},{... | collective-permute-start | bytes 589832 | tf_op jit(solution)/shard_map/ppermute | solution.py:194
  10.2 9.5 %collective-permute-start.2 = (bf16[128,768]{1,0:T(8,128)(2,1)S(1)}, bf16[128,768]{1,0:T(8,128)(2,1)S(1)}, u32[]{:S(2)}, u32[]{:S(2)}) collective-permute-start(bf16[128,768]{1,0:T(8,128)(2,1)S(1)} %get-tuple-element.21), channel_id=1, source_target_pairs={{4,0},{8,4},{12,8},{5,1},{9,5},{13,9},{6,2},{10,6},{14,10},{7,3},{... | collective-permute-start | bytes 589832 | tf_op jit(solution)/shard_map/ppermute | solution.py:194
  12.6 7.1 %collective-permute-start.3 = (bf16[128,768]{1,0:T(8,128)(2,1)S(1)}, bf16[128,768]{1,0:T(8,128)(2,1)S(1)}, u32[]{:S(2)}, u32[]{:S(2)}) collective-permute-start(bf16[128,768]{1,0:T(8,128)(2,1)S(1)} %get-tuple-element.22), channel_id=1, source_target_pairs={{0,1},{1,2},{2,3},{4,5},{5,6},{6,7},{8,9},{9,10},{10,11},{12,13},{... | collective-permute-start | bytes 589832 | tf_op jit(solution)/shard_map/ppermute | solution.py:194
  16.0 7.6 %collective-permute-start.4 = (bf16[128,768]{1,0:T(8,128)(2,1)S(1)}, bf16[128,768]{1,0:T(8,128)(2,1)S(1)}, u32[]{:S(2)}, u32[]{:S(2)}) collective-permute-start(bf16[128,768]{1,0:T(8,128)(2,1)S(1)} %get-tuple-element.23), channel_id=1, source_target_pairs={{1,0},{2,1},{3,2},{5,4},{6,5},{7,6},{9,8},{10,9},{11,10},{13,12},{... | collective-permute-start | bytes 589832 | tf_op jit(solution)/shard_map/ppermute | solution.py:194
  17.3 1.2 %copy-start.3 = (bf16[1,1,1,6,625,125]{5,4,3,2,1,0:T(8,128)(2,1)S(1)}, bf16[1,1,1,6,625,125]{5,4,3,2,1,0:T(8,128)(2,1)}, u32[]{:S(2)}) copy-start(bf16[1,1,1,6,625,125]{5,4,3,2,1,0:T(8,128)(2,1)} %param.7) | copy-start | bytes 2812504
  42.8 0.7 collective-permute-start.5
  43.9 0.7 collective-permute-start.6
  44.9 19.2 %collective-permute-start.7 = (s16[96,128]{1,0:T(8,128)(2,1)S(1)}, s16[96,128]{1,0:T(8,128)(2,1)S(1)}, u32[]{:S(2)}, u32[]{:S(2)}) collective-permute-start(s16[96,128]{1,0:T(8,128)(2,1)S(1)} %group_total.3), channel_id=1, source_target_pairs={{256,384},{272,400},{288,416},{304,432},{320,448},{336,464},{352,4... | collective-permute-start | bytes 73736 | tf_op jit(solution)/shard_map/ppermute | solution.py:235

commit v3 on v2

v3 whole, which is shorter than its diff:
```python
import jax
import jax.numpy as jnp
from jax import lax
from jax.experimental import pallas as pl
from jax.experimental.pallas import tpu as pltpu
from jax.sharding import PartitionSpec as P

NODE = 5
TRACE = 125
WIDE = 128
TALL = 640
FACES = 5
GROUP = 8
f32, bf16 = jnp.float32, jnp.bfloat16
WIRE = jnp.int16
GRANT = 40 * 1024 * 1024


def params():
    return pltpu.CompilerParams(vmem_limit_bytes=GRANT)


def dot(left, right, contract=(1, 0)):
    dims = (((contract[0],), (contract[1],)), ((), ()))
    return lax.dot_general(left, right, dims, preferred_element_type=f32)


def halves(value):
    high = value.astype(bf16)
    return high, (value - high.astype(f32)).astype(bf16)


def split_left(value):
    high, low = halves(value)
    return jnp.concatenate([high, low, high], axis=1)


def split_right(value, axis):
    high, low = halves(value)
    return jnp.concatenate([high, high, low], axis=axis)


def coded(value):
    lane = lax.broadcasted_iota(jnp.int32, value.shape, 1)
    top = jnp.max(jnp.abs(value), axis=1, keepdims=True)
    power = jnp.minimum(jnp.ceil(jnp.log2(jnp.maximum(top, 1e-30))), 127.0)
    fraction = jnp.round(value * jnp.exp2(13.9 - power))
    return jnp.where(lane == WIDE - 1, power, fraction).astype(jnp.int32).astype(WIRE)


def decoded(block):
    value = block.astype(jnp.int32).astype(f32)
    lane = lax.broadcasted_iota(jnp.int32, value.shape, 1)
    power = value[:, WIDE - 1 :]
    return jnp.where(lane == WIDE - 1, 0.0, value * jnp.exp2(power - 13.9))


def trace_rows(which, side):
    at = lax.broadcasted_iota(jnp.int32, (WIDE, 1), 0)
    var = (at * 41) >> 10
    rest = at - 25 * var
    slow = (rest * 13) >> 6
    fast = rest - 5 * slow
    place = [side, slow, fast]
    if which == 1:
        place = [slow, side, fast]
    if which == 2:
        place = [slow, fast, side]
    row = var * 125 + place[0] * 25 + place[1] * 5 + place[2]
    row = jnp.where(at < TRACE, row, -1)
    column = lax.broadcasted_iota(jnp.int32, (WIDE, 625), 1)
    return (row == column).astype(f32).astype(bf16)


def traces_kernel(core, guess, *outs):
    last = NODE - 1
    ahead = last * (1 - core[0])
    sent = ((0, 0), (1, ahead), (2, ahead), (1, last - ahead), (2, last - ahead))
    for (which, side), out in zip(sent, outs):
        out[...] = dot(trace_rows(which, side), guess[...]).astype(bf16)


def maps_kernel(core, inverse, coupling, order, couple_out, left_out, inverse_out, map_out):
    node = lax.broadcasted_iota(jnp.int32, (WIDE, TRACE), 0)

    def permuted(face):
        pick = (node == order[face]).astype(f32).astype(bf16)
        return dot(coupling[face], pick, (1, 1)).astype(bf16)

    turn = core[0]
    for at, face in enumerate((1, 2 + turn, 4 + turn, 3 - turn, 5 - turn)):
        couple_out[:, at * WIDE : (at + 1) * WIDE] = permuted(face)
    first = permuted(0)
    left_out[...] = jnp.zeros(left_out.shape, bf16)
    left_out[:, : inverse.shape[1]] = inverse[...]
    left_out[:, TALL:] = split_left(-dot(inverse[...], first))
    picked = dot(trace_rows(0, NODE - 1), inverse[...]).astype(bf16)
    inverse_out[...] = picked
    map_out[...] = -dot(picked, first).T


def partial_kernel(right_side, couple, t1, t2, t3, t4, out):
    traces = jnp.concatenate([t[...] for t in (t1, t2, t3, t4)], axis=0)
    out[...] = right_side[...].astype(f32) - dot(couple[:, : 4 * WIDE], traces)


def offset_kernel(partial, couple, t5, inverse, maps, residual_out, send_out):
    count, rows, _ = send_out.shape
    part = rows - WIDE
    step = coded(maps[...])
    for start in range(0, count, count // 2):
        cut = slice(start * part, (start + count // 2) * part)
        pulled = dot(couple[:, 4 * WIDE :], t5[:, cut])
        residual = (partial[:, cut] - pulled).astype(bf16)
        padding = jnp.zeros((residual_out.shape[0] - residual.shape[0], residual.shape[1]), bf16)
        residual_out[:, cut] = jnp.concatenate([residual, padding], axis=0)
        offset = coded(dot(inverse[...], residual).T)
        for at in range(count // 2):
            send_out[start + at, :part, :] = offset[at * part : (at + 1) * part]
            send_out[start + at, part:, :] = step


def scan_kernel(received, states_out, total_out, both_out):
    count, rows, _ = received.shape
    part = rows - WIDE
    state = decoded(received[0])
    for at in range(1, count):
        states_out[at - 1] = state
        step = decoded(received[at])
        moved = dot(split_left(state), split_right(step[part:], 0))
        state = jnp.concatenate([moved[:part] + step[:part], moved[part:]], axis=0)
    whole = coded(state)
    total_out[...] = whole[:part]
    both_out[...] = whole


def passed(entering, state):
    part = entering.shape[0]
    return state[:part] + dot(split_left(entering), split_right(state[part:], 0))


def pair_kernel(group, own, above, below, out):
    part = out.shape[0]
    first = group[0] == 0
    mine = decoded(own[...])
    state = jnp.where(first, decoded(above[...]), mine)
    entering = jnp.where(first, mine[:part], decoded(below[...]))
    out[...] = coded(passed(entering, state))


def prefix_kernel(group, first, pair, third, states, out):
    count, part, _ = out.shape
    entering = decoded(pair[...])
    later = passed(entering, decoded(third[...]))
    entering = jnp.where(group[0] == 3, later, entering) + decoded(first[...])
    out[0] = coded(entering)
    left = split_left(entering)
    for at in range(1, count):
        state = states[at - 1]
        moved = dot(left, split_right(state[part:], 0))
        out[at] = coded(state[:part] + moved)


def update_kernel(left, residual, arrived, out, held, sems):
    block = WIDE * 2
    copies = []
    for at, start in enumerate(range(0, held.shape[1], block)):
        cut = slice(start, start + block)
        entering = split_right(decoded(arrived[cut, :]).T, 0)
        right = jnp.concatenate([residual[:, cut], entering], axis=0)
        held[:, cut] = dot(left[...], right).astype(bf16)
        copies.append(pltpu.make_async_copy(held.at[:, cut], out.at[:, cut], sems.at[at]))
        copies[-1].start()
    for copy in copies:
        copy.wait()


def on_device(right_side, inverse, coupling, initial_guess, face_order):
    rows, width = right_side.shape[-2:]
    right_side, inverse, guess = right_side[0, 0, 0], inverse[0, 0, 0], initial_guess[0, 0, 0]
    coupling, order = coupling[0, 0, 0], face_order[0, 0, 0]
    count = lax.axis_size("stream")
    assert count == 4 * GROUP
    part = width // GROUP
    near = [[g * GROUP + i for i in range(GROUP)] for g in range(4)]

    outer = pl.BlockSpec(memory_space=pltpu.HBM)
    blocks = width // (2 * WIDE)

    scalar = pl.BlockSpec(memory_space=pltpu.SMEM)
    inner = pl.BlockSpec(memory_space=pltpu.VMEM)
    place = lax.axis_index("stream").astype(jnp.int32)
    core, group = (place & 1).reshape(1), (place >> 3).reshape(1)
    assert GROUP == 8 and lax.axis_size("gy") == lax.axis_size("gz")

    traces = pl.pallas_call(
        traces_kernel,
        in_specs=[scalar, inner],
        out_shape=[jax.ShapeDtypeStruct((WIDE, width), bf16)] * FACES,
        compiler_params=params(),
        cost_estimate=pl.CostEstimate(flops=8 * 10**9, bytes_accessed=2 * rows * width, transcendentals=0),
        name="face_traces",
    )(core, guess)

    size = lax.axis_size("gy")

    def upstream(value):
        return lax.ppermute(value, "stream", [(i, i - 1) for i in range(1, count)])

    def sideways(value, axis, first):
        steps = [first if i % 2 == 0 else -first for i in range(count)]
        pairs = [
            (i * size + j, i * size + j + steps[i])
            for i in range(count)
            for j in range(size)
            if 0 <= j + steps[i] < size
        ]
        return lax.ppermute(value, ("stream", axis), pairs)

    halos = [upstream(traces[0])]
    for at, (axis, first) in enumerate((("gy", 1), ("gz", 1), ("gy", -1), ("gz", -1))):
        halos.append(sideways(traces[1 + at], axis, first))

    couple, left, picked, maps = pl.pallas_call(
        maps_kernel,
        in_specs=[scalar, inner, inner, inner],
        out_shape=[
            jax.ShapeDtypeStruct((rows, FACES * WIDE), bf16),
            jax.ShapeDtypeStruct((rows, TALL + 3 * WIDE), bf16),
            jax.ShapeDtypeStruct((WIDE, rows), bf16),
            jax.ShapeDtypeStruct((WIDE, WIDE), f32),
        ],
        compiler_params=params(),
        name="element_maps",
    )(core, inverse, coupling, order.reshape(6, 1, TRACE))

    partial = pl.pallas_call(
        partial_kernel,
        out_shape=jax.ShapeDtypeStruct((rows, width), f32),
        cost_estimate=pl.CostEstimate(
            flops=8 * WIDE * rows * width, bytes_accessed=6 * rows * width, transcendentals=0
        ),
        compiler_params=params(),
        name="partial_residual",
    )(right_side, couple, *halos[:4])
    residual, sent = pl.pallas_call(
        offset_kernel,
        out_shape=[
            jax.ShapeDtypeStruct((TALL, width), bf16),
            jax.ShapeDtypeStruct((GROUP, part + WIDE, WIDE), WIRE),
        ],
        compiler_params=params(),
        name="residual_offset",
    )(partial, couple, halos[4], picked, maps)

    received = lax.all_to_all(sent, "stream", 0, 0, tiled=True, axis_index_groups=near)
    states, total, both = pl.pallas_call(
        scan_kernel,
        out_shape=[
            jax.ShapeDtypeStruct((GROUP - 1, part + WIDE, WIDE), f32),
            jax.ShapeDtypeStruct((part, WIDE), WIRE),
            jax.ShapeDtypeStruct((part + WIDE, WIDE), WIRE),
        ],
        compiler_params=params(),
        name="group_scan",
    )(received)

    def between(value, *pairs):
        moves = [(a * GROUP + i, b * GROUP + i) for a, b in pairs for i in range(GROUP)]
        return lax.ppermute(value, "stream", moves)

    above = between(both, (1, 0))
    first = between(total, (0, 1))
    third = between(both, (2, 3))
    pair = pl.pallas_call(
        pair_kernel,
        in_specs=[scalar] + [inner] * 3,
        out_shape=jax.ShapeDtypeStruct((part, WIDE), WIRE),
        compiler_params=params(),
        name="pair_total",
    )(group, both, above, first)
    pair = between(pair, (1, 2), (0, 3))
    entering = pl.pallas_call(
        prefix_kernel,
        in_specs=[scalar] + [inner] * 4,
        out_shape=jax.ShapeDtypeStruct((GROUP, part, WIDE), WIRE),
        compiler_params=params(),
        name="group_prefix",
    )(group, first, pair, third, states)
    arrived = lax.all_to_all(entering, "stream", 0, 0, tiled=True, axis_index_groups=near)

    updated = pl.pallas_call(
        update_kernel,
        out_specs=outer,
        out_shape=jax.ShapeDtypeStruct((rows, width), bf16),
        scratch_shapes=[pltpu.VMEM((rows, width), bf16), pltpu.SemaphoreType.DMA((blocks,))],
        compiler_params=params(),
        name="update",
    )(left, residual, arrived.reshape(width, WIDE))
    return updated[None, None, None]


def solution(mesh):
    return jax.shard_map(
        on_device,
        mesh=mesh,
        in_specs=(
            P("stream", "gy", "gz", None, None),
            P("stream", "gy", "gz", None, None),
            P("stream", "gy", "gz", None, None, None),
            P("stream", "gy", "gz", None, None),
            P("stream", "gy", "gz", None, None),
        ),
        out_specs=P("stream", "gy", "gz", None, None),
        check_vma=False,
    )
```

time: 78 us -> 72.9 us (0.935)
  the two profiles are of different devices: /device:TPU:392 before, /device:TPU:24 now
where the time goes in v3:
time: 72.9 us; the launch traced here: 72.5 us
  blocking collectives  31 us (43%)
  starting transfers between devices  24.3 us (33%)
  Pallas kernels  8.05 us (11%)
  waiting for transfers between devices  7.75 us (11%)
  local copies, waits for them, and re-layouts  1.21 us (2%)
    all_to_all x1, blocking collectives, on_device(): lax.all_to_all(sent, 'stream', 0, 0, tiled=True, axis_index_groups=near)  20.3 us
    ppermute x4, starting transfers between devices, between(): return lax.ppermute(value, 'stream', moves)  12.3 us
    all_to_all x1, blocking collectives, on_device(): lax.all_to_all(entering, 'stream', 0, 0, tiled=True, axis_index_groups=near)  10.7 us
    ppermute x4, starting transfers between devices, sideways(): return lax.ppermute(value, ('stream', axis), pairs)  10.6 us
    ppermute x4, waiting for transfers between devices, sideways(): return lax.ppermute(value, ('stream', axis), pairs)  4.29 us
    ppermute x4, waiting for transfers between devices, between(): return lax.ppermute(value, 'stream', moves)  3.45 us
    pallas_call x1, Pallas kernels, on_device(): pl.pallas_call(update_kernel, out_specs=outer, out_shape=jax.ShapeDtypeSt...  2.07 us
  transfers between devices with their start and end apart: 9, of which 5 were waited for; matrix products, arithmetic and copies ran while one was open for 0% of the time, Pallas kernels for 3%

profile of v3, /device:TPU:24, one launch (start us, length us, event | category | flops | bytes accessed | tf_op | source)
XLA Modules:
  0.0 72.5 jit_solution(15190662132448335276)
XLA Ops:
  0.0 1.2 %copy-done.4 = bf16[1,1,1,625,768]{4,3,2,1,0:T(8,128)(2,1)S(1)} copy-done((bf16[1,1,1,625,768]{4,3,2,1,0:T(8,128)(2,1)S(1)}, bf16[1,1,1,625,768]{4,3,2,1,0:T(8,128)(2,1)}, u32[]{:S(2)}) %copy-start.4) | copy-done | bytes 960024
  1.2 0.9 %face_traces.1 = (bf16[128,768]{1,0:T(8,128)(2,1)S(1)}, bf16[128,768]{1,0:T(8,128)(2,1)S(1)}, bf16[128,768]{1,0:T(8,128)(2,1)S(1)}, bf16[128,768]{1,0:T(8,128)(2,1)S(1)}, bf16[128,768]{1,0:T(8,128)(2,1)S(1)}) custom-call(s32[1]{0:T(128)} %bitcast.core, bf16[625,768]{1,0:T(8,128)(2,1)S(1)} %bitcast.14), custom_call_target="tpu_custom_call" | custom-call | flops 8000000000 | bytes 960000 | tf_op jit(solution)/shard_map/face_traces/pallas_call | solution.py:196
  2.2 1.4 %collective-permute-start = (bf16[128,768]{1,0:T(8,128)(2,1)S(1)}, bf16[128,768]{1,0:T(8,128)(2,1)S(1)}, u32[]{:S(2)}, u32[]{:S(2)}) collective-permute-start(bf16[128,768]{1,0:T(8,128)(2,1)S(1)} %get-tuple-element.21), channel_id=1, source_target_pairs={{16,0},{32,16},{48,32},{64,48},{80,64},{96,80},{112,96},{128,112},... | collective-permute-start | bytes 589832 | tf_op jit(solution)/shard_map/ppermute | solution.py:208
  3.6 1.3 %collective-permute-start.1 = (bf16[128,768]{1,0:T(8,128)(2,1)S(1)}, bf16[128,768]{1,0:T(8,128)(2,1)S(1)}, u32[]{:S(2)}, u32[]{:S(2)}) collective-permute-start(bf16[128,768]{1,0:T(8,128)(2,1)S(1)} %get-tuple-element.22), channel_id=1, source_target_pairs={{0,4},{4,8},{8,12},{20,16},{24,20},{28,24},{32,36},{36,40},{40,44}... | collective-permute-start | bytes 589832 | tf_op jit(solution)/shard_map/ppermute | solution.py:218
  4.9 3.4 %collective-permute-start.2 = (bf16[128,768]{1,0:T(8,128)(2,1)S(1)}, bf16[128,768]{1,0:T(8,128)(2,1)S(1)}, u32[]{:S(2)}, u32[]{:S(2)}) collective-permute-start(bf16[128,768]{1,0:T(8,128)(2,1)S(1)} %get-tuple-element.23), channel_id=1, source_target_pairs={{0,1},{1,2},{2,3},{17,16},{18,17},{19,18},{32,33},{33,34},{34,35},... | collective-permute-start | bytes 589832 | tf_op jit(solution)/shard_map/ppermute | solution.py:218
  8.3 4.6 %collective-permute-start.3 = (bf16[128,768]{1,0:T(8,128)(2,1)S(1)}, bf16[128,768]{1,0:T(8,128)(2,1)S(1)}, u32[]{:S(2)}, u32[]{:S(2)}) collective-permute-start(bf16[128,768]{1,0:T(8,128)(2,1)S(1)} %get-tuple-element.24), channel_id=1, source_target_pairs={{4,0},{8,4},{12,8},{16,20},{20,24},{24,28},{36,32},{40,36},{44,40}... | collective-permute-start | bytes 589832 | tf_op jit(solution)/shard_map/ppermute | solution.py:218
  12.9 1.3 %collective-permute-start.4 = (bf16[128,768]{1,0:T(8,128)(2,1)S(1)}, bf16[128,768]{1,0:T(8,128)(2,1)S(1)}, u32[]{:S(2)}, u32[]{:S(2)}) collective-permute-start(bf16[128,768]{1,0:T(8,128)(2,1)S(1)} %get-tuple-element.25), channel_id=1, source_target_pairs={{1,0},{2,1},{3,2},{16,17},{17,18},{18,19},{33,32},{34,33},{35,34},... | collective-permute-start | bytes 589832 | tf_op jit(solution)/shard_map/ppermute | solution.py:218
  14.2 1.2 %element_maps.1 = (bf16[625,640]{1,0:T(8,128)(2,1)S(1)}, bf16[625,1024]{1,0:T(8,128)(2,1)S(1)}, bf16[128,625]{1,0:T(8,128)(2,1)S(1)}, f32[128,128]{1,0:T(8,128)S(1)}) custom-call(s32[1]{0:T(128)} %bitcast.core, bf16[625,625]{1,0:T(8,128)(2,1)S(1)} %bitcast.11, bf16[6,625,125]{2,1,0:T(8,128)(2,1)S(1)} %bitcast.9, s32[6,1,125]{2,1,0:T(1,128)S(1)} %bitcast.13), custom_call_target="tpu_custom_call" | custom-call | tf_op jit(solution)/shard_map/element_maps/pallas_call | solution.py:224
  15.5 0.6 collective-permute-done.3.t4
  16.0 0.7 partial_residual.1.partial
  16.7 3.7 %collective-permute-done.4.t5 = bf16[128,768]{1,0:T(8,128)(2,1)S(1)} collective-permute-done((bf16[128,768]{1,0:T(8,128)(2,1)S(1)}, bf16[128,768]{1,0:T(8,128)(2,1)S(1)}, u32[]{:S(2)}, u32[]{:S(2)}) %collective-permute-start.4) | collective-permute-done | bytes 196640 | tf_op jit(solution)/shard_map/ppermute | solution.py:218
  20.4 1.0 %residual_offset.1 = (bf16[640,768]{1,0:T(8,128)(2,1)S(1)}, s16[8,224,128]{2,1,0:T(8,128)(2,1)S(1)}) custom-call(f32[625,768]{1,0:T(8,128)S(1)} %partial_residual.1.partial, bf16[625,640]{1,0:T(8,128)(2,1)S(1)} %get-tuple-element.20.couple, bf16[128,768]{1,0:T(8,128)(2,1)S(1)} %collective-permute-done.4.t5, bf16[128,625]{1,0:T(8,128)(2,1)S(1)} %get-tuple-element.26.inverse, ...), custom_call_target="tpu_custom_call" | custom-call | tf_op jit(solution)/shard_map/residual_offset/pallas_call | solution.py:246
  21.4 20.3 %all_to_all.10.received = s16[8,224,128]{2,1,0:T(8,128)(2,1)S(1)} all-to-all(s16[8,224,128]{2,1,0:T(8,128)(2,1)S(1)} %get-tuple-element.29), channel_id=1, replica_groups={{0,16,32,48,64,80,96,112},{128,144,160,176,192,208,224,240},{256,272,28..., dimensions={0} | all-to-all | bytes 917504 | tf_op jit(solution)/shard_map/all_to_all | solution.py:256
  41.7 1.2 %group_scan.1 = (f32[7,224,128]{2,1,0:T(8,128)S(1)}, s16[96,128]{1,0:T(8,128)(2,1)S(1)}, s16[224,128]{1,0:T(8,128)(2,1)S(1)}) custom-call(s16[8,224,128]{2,1,0:T(8,128)(2,1)S(1)} %all_to_all.10.received), custom_call_target="tpu_custom_call" | custom-call | tf_op jit(solution)/shard_map/group_scan/pallas_call | solution.py:257
  42.9 1.3 %collective-permute-start.6 = (s16[224,128]{1,0:T(8,128)(2,1)S(1)}, s16[224,128]{1,0:T(8,128)(2,1)S(1)}, u32[]{:S(2)}, u32[]{:S(2)}) collective-permute-start(s16[224,128]{1,0:T(8,128)(2,1)S(1)} %get-tuple-element.31.own), channel_id=1, source_target_pairs={{128,0},{144,16},{160,32},{176,48},{192,64},{208,80},{224,96},{240... | collective-permute-start | bytes 172040 | tf_op jit(solution)/shard_map/ppermute | solution.py:270
  44.2 0.7 collective-permute-start.8
  44.9 9.1 %collective-permute-start.5 = (s16[96,128]{1,0:T(8,128)(2,1)S(1)}, s16[96,128]{1,0:T(8,128)(2,1)S(1)}, u32[]{:S(2)}, u32[]{:S(2)}) collective-permute-start(s16[96,128]{1,0:T(8,128)(2,1)S(1)} %get-tuple-element.30), channel_id=1, source_target_pairs={{0,128},{16,144},{32,160},{48,176},{64,192},{80,208},{96,224},{112... | collective-permute-start | bytes 73736 | tf_op jit(solution)/shard_map/ppermute | solution.py:270
  54.0 1.5 %collective-permute-done.5.below.first = s16[96,128]{1,0:T(8,128)(2,1)S(1)} collective-permute-done((s16[96,128]{1,0:T(8,128)(2,1)S(1)}, s16[96,128]{1,0:T(8,128)(2,1)S(1)}, u32[]{:S(2)}, u32[]{:S(2)}) %collective-permute-start.5) | collective-permute-done | bytes 24608 | tf_op jit(solution)/shard_map/ppermute | solution.py:270
  55.5 0.5 collective-permute-done.6.above
  56.3 1.3 %collective-permute-start.7 = (s16[96,128]{1,0:T(8,128)(2,1)S(1)}, s16[96,128]{1,0:T(8,128)(2,1)S(1)}, u32[]{:S(2)}, u32[]{:S(2)}) collective-permute-start(s16[96,128]{1,0:T(8,128)(2,1)S(1)} %pair_total.1), channel_id=1, source_target_pairs={{128,256},{144,272},{160,288},{176,304},{192,320},{208,336},{224,3... | collective-permute-start | bytes 73736 | tf_op jit(solution)/shard_map/ppermute | solution.py:270
  57.6 1.5 %collective-permute-done.7.pair = s16[96,128]{1,0:T(8,128)(2,1)S(1)} collective-permute-done((s16[96,128]{1,0:T(8,128)(2,1)S(1)}, s16[96,128]{1,0:T(8,128)(2,1)S(1)}, u32[]{:S(2)}, u32[]{:S(2)}) %collective-permute-start.7) | collective-permute-done | bytes 24608 | tf_op jit(solution)/shard_map/ppermute | solution.py:270
  59.1 0.6 group_prefix.1
  59.7 10.7 %all_to_all.11 = s16[8,96,128]{2,1,0:T(8,128)(2,1)S(1)} all-to-all(s16[8,96,128]{2,1,0:T(8,128)(2,1)S(1)} %group_prefix.1), channel_id=1, replica_groups={{0,16,32,48,64,80,96,112},{128,144,160,176,192,208,224,240},{256,272,28..., dimensions={0} | all-to-all | bytes 393216 | tf_op jit(solution)/shard_map/all_to_all | solution.py:290
  70.5 2.1 %update.1 = bf16[625,768]{1,0:T(8,128)(2,1)} custom-call(bf16[625,1024]{1,0:T(8,128)(2,1)S(1)} %get-tuple-element.19.left, bf16[640,768]{1,0:T(8,128)(2,1)S(1)} %get-tuple-element.28.residual, s16[768,128]{1,0:T(8,128)(2,1)S(1)} %bitcast.12), custom_call_target="tpu_custom_call" | custom-call | tf_op jit(solution)/shard_map/update/pallas_call | solution.py:292
  (14 shorter events, 0.4 us)
Async XLA Ops:
  0.0 1.2 %copy-start.4 = (bf16[1,1,1,625,768]{4,3,2,1,0:T(8,128)(2,1)S(1)}, bf16[1,1,1,625,768]{4,3,2,1,0:T(8,128)(2,1)}, u32[]{:S(2)}) copy-start(bf16[1,1,1,625,768]{4,3,2,1,0:T(8,128)(2,1)} %param.8) | copy-start | bytes 2880004
  1.2 13.0 %copy-start = (bf16[1,1,1,6,625,125]{5,4,3,2,1,0:T(8,128)(2,1)S(1)}, bf16[1,1,1,6,625,125]{5,4,3,2,1,0:T(8,128)(2,1)}, u32[]{:S(2)}) copy-start(bf16[1,1,1,6,625,125]{5,4,3,2,1,0:T(8,128)(2,1)} %param.7) | copy-start | bytes 2812504
  1.2 13.0 %copy-start.2 = (bf16[1,1,1,625,625]{4,3,2,1,0:T(8,128)(2,1)S(1)}, bf16[1,1,1,625,625]{4,3,2,1,0:T(8,128)(2,1)}, u32[]{:S(2)}) copy-start(bf16[1,1,1,625,625]{4,3,2,1,0:T(8,128)(2,1)} %param.6) | copy-start | bytes 2343754
  1.2 13.0 %copy-start.3 = (s32[1,1,1,6,125]{4,2,3,1,0:T(1,128)S(1)}, s32[1,1,1,6,125]{4,2,3,1,0:T(1,128)}, u32[]{:S(2)}) copy-start(s32[1,1,1,6,125]{4,2,3,1,0:T(1,128)} %param.9) | copy-start | bytes 9004
  2.1 13.9 %copy-start.1 = (bf16[1,1,1,625,768]{4,3,2,1,0:T(8,128)(2,1)S(1)}, bf16[1,1,1,625,768]{4,3,2,1,0:T(8,128)(2,1)}, u32[]{:S(2)}) copy-start(bf16[1,1,1,625,768]{4,3,2,1,0:T(8,128)(2,1)} %param.5) | copy-start | bytes 2880004
  2.2 13.3 %collective-permute-start = (bf16[128,768]{1,0:T(8,128)(2,1)S(1)}, bf16[128,768]{1,0:T(8,128)(2,1)S(1)}, u32[]{:S(2)}, u32[]{:S(2)}) collective-permute-start(bf16[128,768]{1,0:T(8,128)(2,1)S(1)} %get-tuple-element.21), channel_id=1, source_target_pairs={{16,0},{32,16},{48,32},{64,48},{80,64},{96,80},{112,96},{128,112},... | collective-permute-start | bytes 589832 | tf_op jit(solution)/shard_map/ppermute | solution.py:208
  3.6 11.8 %collective-permute-start.1 = (bf16[128,768]{1,0:T(8,128)(2,1)S(1)}, bf16[128,768]{1,0:T(8,128)(2,1)S(1)}, u32[]{:S(2)}, u32[]{:S(2)}) collective-permute-start(bf16[128,768]{1,0:T(8,128)(2,1)S(1)} %get-tuple-element.22), channel_id=1, source_target_pairs={{0,4},{4,8},{8,12},{20,16},{24,20},{28,24},{32,36},{36,40},{40,44}... | collective-permute-start | bytes 589832 | tf_op jit(solution)/shard_map/ppermute | solution.py:218
  4.9 10.6 %collective-permute-start.2 = (bf16[128,768]{1,0:T(8,128)(2,1)S(1)}, bf16[128,768]{1,0:T(8,128)(2,1)S(1)}, u32[]{:S(2)}, u32[]{:S(2)}) collective-permute-start(bf16[128,768]{1,0:T(8,128)(2,1)S(1)} %get-tuple-element.23), channel_id=1, source_target_pairs={{0,1},{1,2},{2,3},{17,16},{18,17},{19,18},{32,33},{33,34},{34,35},... | collective-permute-start | bytes 589832 | tf_op jit(solution)/shard_map/ppermute | solution.py:218
  8.3 7.7 %collective-permute-start.3 = (bf16[128,768]{1,0:T(8,128)(2,1)S(1)}, bf16[128,768]{1,0:T(8,128)(2,1)S(1)}, u32[]{:S(2)}, u32[]{:S(2)}) collective-permute-start(bf16[128,768]{1,0:T(8,128)(2,1)S(1)} %get-tuple-element.24), channel_id=1, source_target_pairs={{4,0},{8,4},{12,8},{16,20},{20,24},{24,28},{36,32},{40,36},{44,40}... | collective-permute-start | bytes 589832 | tf_op jit(solution)/shard_map/ppermute | solution.py:218
  12.9 7.6 %collective-permute-start.4 = (bf16[128,768]{1,0:T(8,128)(2,1)S(1)}, bf16[128,768]{1,0:T(8,128)(2,1)S(1)}, u32[]{:S(2)}, u32[]{:S(2)}) collective-permute-start(bf16[128,768]{1,0:T(8,128)(2,1)S(1)} %get-tuple-element.25), channel_id=1, source_target_pairs={{1,0},{2,1},{3,2},{16,17},{17,18},{18,19},{33,32},{34,33},{35,34},... | collective-permute-start | bytes 589832 | tf_op jit(solution)/shard_map/ppermute | solution.py:218
  42.9 13.0 %collective-permute-start.6 = (s16[224,128]{1,0:T(8,128)(2,1)S(1)}, s16[224,128]{1,0:T(8,128)(2,1)S(1)}, u32[]{:S(2)}, u32[]{:S(2)}) collective-permute-start(s16[224,128]{1,0:T(8,128)(2,1)S(1)} %get-tuple-element.31.own), channel_id=1, source_target_pairs={{128,0},{144,16},{160,32},{176,48},{192,64},{208,80},{224,96},{240... | collective-permute-start | bytes 172040 | tf_op jit(solution)/shard_map/ppermute | solution.py:270
  44.2 13.4 %collective-permute-start.8 = (s16[224,128]{1,0:T(8,128)(2,1)S(1)}, s16[224,128]{1,0:T(8,128)(2,1)S(1)}, u32[]{:S(2)}, u32[]{:S(2)}) collective-permute-start(s16[224,128]{1,0:T(8,128)(2,1)S(1)} %get-tuple-element.31.own), channel_id=1, source_target_pairs={{256,384},{272,400},{288,416},{304,432},{320,448},{336,464},{352,4... | collective-permute-start | bytes 172040 | tf_op jit(solution)/shard_map/ppermute | solution.py:270
  44.9 10.6 %collective-permute-start.5 = (s16[96,128]{1,0:T(8,128)(2,1)S(1)}, s16[96,128]{1,0:T(8,128)(2,1)S(1)}, u32[]{:S(2)}, u32[]{:S(2)}) collective-permute-start(s16[96,128]{1,0:T(8,128)(2,1)S(1)} %get-tuple-element.30), channel_id=1, source_target_pairs={{0,128},{16,144},{32,160},{48,176},{64,192},{80,208},{96,224},{112... | collective-permute-start | bytes 73736 | tf_op jit(solution)/shard_map/ppermute | solution.py:270
  56.3 2.8 %collective-permute-start.7 = (s16[96,128]{1,0:T(8,128)(2,1)S(1)}, s16[96,128]{1,0:T(8,128)(2,1)S(1)}, u32[]{:S(2)}, u32[]{:S(2)}) collective-permute-start(s16[96,128]{1,0:T(8,128)(2,1)S(1)} %pair_total.1), channel_id=1, source_target_pairs={{128,256},{144,272},{160,288},{176,304},{192,320},{208,336},{224,3... | collective-permute-start | bytes 73736 | tf_op jit(solution)/shard_map/ppermute | solution.py:270

commit v4 on v3

--- a/solution.py
+++ b/solution.py
@@ -74,8 +74,8 @@
 
 def traces_kernel(core, guess, *outs):
     last = NODE - 1
-    ahead = last * (1 - core[0])
-    sent = ((0, 0), (1, ahead), (2, ahead), (1, last - ahead), (2, last - ahead))
+    y, z = last * (1 - core[0]), last * (core[0])
+    sent = ((0, 0), (1, y), (2, z), (1, last - y), (2, last - z))
     for (which, side), out in zip(sent, outs):
         out[...] = dot(trace_rows(which, side), guess[...]).astype(bf16)
 
@@ -88,7 +88,7 @@
         return dot(coupling[face], pick, (1, 1)).astype(bf16)
 
     turn = core[0]
-    for at, face in enumerate((1, 2 + turn, 4 + turn, 3 - turn, 5 - turn)):
+    for at, face in enumerate((2 + turn, 5 - turn, 1, 3 - turn, 4 + turn)):
         couple_out[:, at * WIDE : (at + 1) * WIDE] = permuted(face)
     first = permuted(0)
     left_out[...] = jnp.zeros(left_out.shape, bf16)
@@ -96,7 +96,7 @@
     left_out[:, TALL:] = split_left(-dot(inverse[...], first))
     picked = dot(trace_rows(0, NODE - 1), inverse[...]).astype(bf16)
     inverse_out[...] = picked
-    map_out[...] = -dot(picked, first).T
+    map_out[...] = coded(-dot(picked, first).T)
 
 
 def partial_kernel(right_side, couple, t1, t2, t3, t4, out):
@@ -104,31 +104,46 @@
     out[...] = right_side[...].astype(f32) - dot(couple[:, : 4 * WIDE], traces)
 
 
-def offset_kernel(partial, couple, t5, inverse, maps, residual_out, send_out):
-    count, rows, _ = send_out.shape
-    part = rows - WIDE
-    step = coded(maps[...])
-    for start in range(0, count, count // 2):
-        cut = slice(start * part, (start + count // 2) * part)
+def offset_kernel(partial, couple, t5, inverse, residual_out, offset_out):
+    block = offset_out.shape[0] // 2
+    for start in (0, block):
+        cut = slice(start, start + block)
         pulled = dot(couple[:, 4 * WIDE :], t5[:, cut])
         residual = (partial[:, cut] - pulled).astype(bf16)
-        padding = jnp.zeros((residual_out.shape[0] - residual.shape[0], residual.shape[1]), bf16)
+        padding = jnp.zeros((residual_out.shape[0] - residual.shape[0], block), bf16)
         residual_out[:, cut] = jnp.concatenate([residual, padding], axis=0)
-        offset = coded(dot(inverse[...], residual).T)
-        for at in range(count // 2):
-            send_out[start + at, :part, :] = offset[at * part : (at + 1) * part]
-            send_out[start + at, part:, :] = step
+        offset_out[cut, :] = coded(dot(inverse[...], residual).T)
+
+
+def merge_kernel(core, offsets, maps, send_out):
+    count, rows, _ = send_out.shape
+    half = rows - WIDE // 2
+    last = split_right(decoded(maps[1]), 0)
+    merged = decoded(offsets[1]) + dot(split_left(decoded(offsets[0])), last)
+    step = dot(split_left(decoded(maps[0])), last)
+    first = core[0] == 0
+    step = coded(jnp.where(first, step[: WIDE // 2], step[WIDE // 2 :]))
+    for at in range(count):
+        low = merged[2 * at * half : (2 * at + 1) * half]
+        high = merged[(2 * at + 1) * half : (2 * at + 2) * half]
+        send_out[at, :half, :] = coded(jnp.where(first, low, high))
+        send_out[at, half:, :] = step
 
 
 def scan_kernel(received, states_out, total_out, both_out):
     count, rows, _ = received.shape
-    part = rows - WIDE
-    state = decoded(received[0])
-    for at in range(1, count):
+    half = rows - WIDE // 2
+    part = 2 * half
+    steps = []
+    for at in range(0, count, 2):
+        low, high = decoded(received[at]), decoded(received[at + 1])
+        steps.append((low[:half], high[:half], low[half:], high[half:]))
+    state = jnp.concatenate(steps[0], axis=0)
+    for at in range(1, count // 2):
         states_out[at - 1] = state
-        step = decoded(received[at])
-        moved = dot(split_left(state), split_right(step[part:], 0))
-        state = jnp.concatenate([moved[:part] + step[:part], moved[part:]], axis=0)
+        moved = dot(split_left(state), split_right(jnp.concatenate(steps[at][2:], axis=0), 0))
+        offset = jnp.concatenate(steps[at][:2], axis=0)
+        state = jnp.concatenate([moved[:part] + offset, moved[part:]], axis=0)
     whole = coded(state)
     total_out[...] = whole[:part]
     both_out[...] = whole
@@ -153,21 +168,27 @@
     entering = decoded(pair[...])
     later = passed(entering, decoded(third[...]))
     entering = jnp.where(group[0] == 3, later, entering) + decoded(first[...])
-    out[0] = coded(entering)
     left = split_left(entering)
-    for at in range(1, count):
-        state = states[at - 1]
-        moved = dot(left, split_right(state[part:], 0))
-        out[at] = coded(state[:part] + moved)
-
-
-def update_kernel(left, residual, arrived, out, held, sems):
+    for at in range(0, count, 2):
+        value = entering
+        if at > 0:
+            state = states[at // 2 - 1]
+            value = state[:part] + dot(left, split_right(state[part:], 0))
+        value = coded(value)
+        out[at] = value
+        out[at + 1] = value
+
+
+def update_kernel(core, left, residual, arrived, offsets, maps, out, held, sems):
     block = WIDE * 2
     copies = []
+    step = split_right(decoded(maps[0]), 0)
     for at, start in enumerate(range(0, held.shape[1], block)):
         cut = slice(start, start + block)
-        entering = split_right(decoded(arrived[cut, :]).T, 0)
-        right = jnp.concatenate([residual[:, cut], entering], axis=0)
+        entering = decoded(arrived[cut, :])
+        later = decoded(offsets[0, cut, :]) + dot(split_left(entering), step)
+        entering = jnp.where(core[0] == 0, entering, later)
+        right = jnp.concatenate([residual[:, cut], split_right(entering.T, 0)], axis=0)
         held[:, cut] = dot(left[...], right).astype(bf16)
         copies.append(pltpu.make_async_copy(held.at[:, cut], out.at[:, cut], sems.at[at]))
         copies[-1].start()
@@ -182,6 +203,7 @@
     count = lax.axis_size("stream")
     assert count == 4 * GROUP
     part = width // GROUP
+    chips = [[i, i + 1] for i in range(0, count, 2)]
     near = [[g * GROUP + i for i in range(GROUP)] for g in range(4)]
 
     outer = pl.BlockSpec(memory_space=pltpu.HBM)
@@ -218,7 +240,7 @@
         return lax.ppermute(value, ("stream", axis), pairs)
 
     halos = [upstream(traces[0])]
-    for at, (axis, first) in enumerate((("gy", 1), ("gz", 1), ("gy", -1), ("gz", -1))):
+    for at, (axis, first) in enumerate((("gy", 1), ("gz", -1), ("gy", -1), ("gz", 1))):
         halos.append(sideways(traces[1 + at], axis, first))
 
     couple, left, picked, maps = pl.pallas_call(
@@ -228,7 +250,7 @@
             jax.ShapeDtypeStruct((rows, FACES * WIDE), bf16),
             jax.ShapeDtypeStruct((rows, TALL + 3 * WIDE), bf16),
             jax.ShapeDtypeStruct((WIDE, rows), bf16),
-            jax.ShapeDtypeStruct((WIDE, WIDE), f32),
+            jax.ShapeDtypeStruct((WIDE, WIDE), WIRE),
         ],
         compiler_params=params(),
         name="element_maps",
@@ -242,22 +264,30 @@
         ),
         compiler_params=params(),
         name="partial_residual",
-    )(right_side, couple, *halos[:4])
-    residual, sent = pl.pallas_call(
+    )(right_side, couple, *(halos[at] for at in (1, 2, 0, 3)))
+    maps = lax.all_gather(maps, "stream", axis_index_groups=chips)
+    residual, offset = pl.pallas_call(
         offset_kernel,
         out_shape=[
             jax.ShapeDtypeStruct((TALL, width), bf16),
-            jax.ShapeDtypeStruct((GROUP, part + WIDE, WIDE), WIRE),
+            jax.ShapeDtypeStruct((width, WIDE), WIRE),
         ],
         compiler_params=params(),
         name="residual_offset",
-    )(partial, couple, halos[4], picked, maps)
-
+    )(partial, couple, halos[4], picked)
+    offsets = lax.all_gather(offset, "stream", axis_index_groups=chips)
+    sent = pl.pallas_call(
+        merge_kernel,
+        in_specs=[scalar, inner, inner],
+        out_shape=jax.ShapeDtypeStruct((GROUP, (part + WIDE) // 2, WIDE), WIRE),
+        compiler_params=params(),
+        name="chip_merge",
+    )(core, offsets, maps)
     received = lax.all_to_all(sent, "stream", 0, 0, tiled=True, axis_index_groups=near)
     states, total, both = pl.pallas_call(
         scan_kernel,
         out_shape=[
-            jax.ShapeDtypeStruct((GROUP - 1, part + WIDE, WIDE), f32),
+            jax.ShapeDtypeStruct((GROUP // 2 - 1, part + WIDE, WIDE), f32),
             jax.ShapeDtypeStruct((part, WIDE), WIRE),
             jax.ShapeDtypeStruct((part + WIDE, WIDE), WIRE),
         ],
@@ -291,12 +321,13 @@
 
     updated = pl.pallas_call(
         update_kernel,
+        in_specs=[scalar] + [inner] * 5,
         out_specs=outer,
         out_shape=jax.ShapeDtypeStruct((rows, width), bf16),
         scratch_shapes=[pltpu.VMEM((rows, width), bf16), pltpu.SemaphoreType.DMA((blocks,))],
         compiler_params=params(),
         name="update",
-    )(left, residual, arrived.reshape(width, WIDE))
+    )(core, left, residual, arrived.reshape(width, WIDE), offsets, maps)
     return updated[None, None, None]
 
 

time: 72.9 us -> 69.5 us (0.953)
  waiting for transfers between devices: 7.75 us -> 3.23 us
  starting transfers between devices: 24.3 us -> 25.5 us
  blocking collectives: 31 us -> 30 us
    all_to_all x1, blocking collectives: 20.3 us -> 15.4 us  [on_device(): lax.all_to_all(sent, 'stream', 0, 0, tiled=True, axis_index_groups=near)]
    ppermute x4, waiting for transfers between devices: 4.29 us -> 0.01 us  [sideways(): return lax.ppermute(value, ('stream', axis), pairs)]
    all_gather x0 -> x2, blocking collectives: none -> 3.94 us  [the longest x1 2.09 us: on_device(): offsets = lax.all_gather(offset, 'stream', axis_index_groups=chips)]
    ppermute x4, starting transfers between devices: 10.6 us -> 11.8 us  [sideways(): return lax.ppermute(value, ('stream', axis), pairs)]
    pallas_call x2 -> x3, Pallas kernels: 3.25 us -> 3.58 us  [the longest x1 2.32 us: on_device(): pl.pallas_call(update_kernel, in_specs=[scalar] + [inner] * 5, out_specs=...]
  transfers between devices with their start and end apart: 9 -> 9, of which waited for: 5 -> 3; matrix products, arithmetic and copies ran while one was open for 0% -> 0% of each run, Pallas kernels for 3% -> 3%
where the time goes in v4:
time: 69.5 us; the launch traced here: 68.5 us
  blocking collectives  30 us (43%)
  starting transfers between devices  25.5 us (37%)
  Pallas kernels  8.38 us (12%)
  waiting for transfers between devices  3.23 us (5%)
  local copies, waits for them, and re-layouts  1.21 us (2%)
    all_to_all x1, blocking collectives, on_device(): lax.all_to_all(sent, 'stream', 0, 0, tiled=True, axis_index_groups=near)  15.4 us
    ppermute x4, starting transfers between devices, between(): return lax.ppermute(value, 'stream', moves)  12.3 us
    ppermute x4, starting transfers between devices, sideways(): return lax.ppermute(value, ('stream', axis), pairs)  11.8 us
    all_to_all x1, blocking collectives, on_device(): lax.all_to_all(entering, 'stream', 0, 0, tiled=True, axis_index_groups=near)  10.7 us
    ppermute x4, waiting for transfers between devices, between(): return lax.ppermute(value, 'stream', moves)  3.22 us
    pallas_call x1, Pallas kernels, on_device(): pl.pallas_call(update_kernel, in_specs=[scalar] + [inner] * 5, out_specs=...  2.32 us
    all_gather x1, blocking collectives, on_device(): offsets = lax.all_gather(offset, 'stream', axis_index_groups=chips)  2.09 us
    all_gather x1, blocking collectives, on_device(): maps = lax.all_gather(maps, 'stream', axis_index_groups=chips)  1.85 us
  transfers between devices with their start and end apart: 9, of which 3 were waited for; matrix products, arithmetic and copies ran while one was open for 0% of the time, Pallas kernels for 3%

profile of v4, /device:TPU:24, one launch (start us, length us, event | category | flops | bytes accessed | tf_op | source)
XLA Modules:
  0.0 68.5 jit_solution(716744765987159243)
XLA Ops:
  0.0 1.2 %copy-done.4 = bf16[1,1,1,625,768]{4,3,2,1,0:T(8,128)(2,1)S(1)} copy-done((bf16[1,1,1,625,768]{4,3,2,1,0:T(8,128)(2,1)S(1)}, bf16[1,1,1,625,768]{4,3,2,1,0:T(8,128)(2,1)}, u32[]{:S(2)}) %copy-start.4) | copy-done | bytes 960024
  1.2 0.9 %face_traces.1 = (bf16[128,768]{1,0:T(8,128)(2,1)S(1)}, bf16[128,768]{1,0:T(8,128)(2,1)S(1)}, bf16[128,768]{1,0:T(8,128)(2,1)S(1)}, bf16[128,768]{1,0:T(8,128)(2,1)S(1)}, bf16[128,768]{1,0:T(8,128)(2,1)S(1)}) custom-call(s32[1]{0:T(128)} %bitcast.core, bf16[625,768]{1,0:T(8,128)(2,1)S(1)} %bitcast.20), custom_call_target="tpu_custom_call" | custom-call | flops 8000000000 | bytes 960000 | tf_op jit(solution)/shard_map/face_traces/pallas_call | solution.py:218
  2.2 1.4 %collective-permute-start = (bf16[128,768]{1,0:T(8,128)(2,1)S(1)}, bf16[128,768]{1,0:T(8,128)(2,1)S(1)}, u32[]{:S(2)}, u32[]{:S(2)}) collective-permute-start(bf16[128,768]{1,0:T(8,128)(2,1)S(1)} %get-tuple-element.21), channel_id=1, source_target_pairs={{0,4},{4,8},{8,12},{20,16},{24,20},{28,24},{32,36},{36,40},{40,44}... | collective-permute-start | bytes 589832 | tf_op jit(solution)/shard_map/ppermute | solution.py:240
  3.6 1.3 %collective-permute-start.1 = (bf16[128,768]{1,0:T(8,128)(2,1)S(1)}, bf16[128,768]{1,0:T(8,128)(2,1)S(1)}, u32[]{:S(2)}, u32[]{:S(2)}) collective-permute-start(bf16[128,768]{1,0:T(8,128)(2,1)S(1)} %get-tuple-element.22), channel_id=1, source_target_pairs={{1,0},{2,1},{3,2},{16,17},{17,18},{18,19},{33,32},{34,33},{35,34},... | collective-permute-start | bytes 589832 | tf_op jit(solution)/shard_map/ppermute | solution.py:240
  4.9 1.3 %collective-permute-start.2 = (bf16[128,768]{1,0:T(8,128)(2,1)S(1)}, bf16[128,768]{1,0:T(8,128)(2,1)S(1)}, u32[]{:S(2)}, u32[]{:S(2)}) collective-permute-start(bf16[128,768]{1,0:T(8,128)(2,1)S(1)} %get-tuple-element.23), channel_id=1, source_target_pairs={{16,0},{32,16},{48,32},{64,48},{80,64},{96,80},{112,96},{128,112},... | collective-permute-start | bytes 589832 | tf_op jit(solution)/shard_map/ppermute | solution.py:230
  6.2 4.6 %collective-permute-start.3 = (bf16[128,768]{1,0:T(8,128)(2,1)S(1)}, bf16[128,768]{1,0:T(8,128)(2,1)S(1)}, u32[]{:S(2)}, u32[]{:S(2)}) collective-permute-start(bf16[128,768]{1,0:T(8,128)(2,1)S(1)} %get-tuple-element.24), channel_id=1, source_target_pairs={{4,0},{8,4},{12,8},{16,20},{20,24},{24,28},{36,32},{40,36},{44,40}... | collective-permute-start | bytes 589832 | tf_op jit(solution)/shard_map/ppermute | solution.py:240
  10.8 4.6 %collective-permute-start.4 = (bf16[128,768]{1,0:T(8,128)(2,1)S(1)}, bf16[128,768]{1,0:T(8,128)(2,1)S(1)}, u32[]{:S(2)}, u32[]{:S(2)}) collective-permute-start(bf16[128,768]{1,0:T(8,128)(2,1)S(1)} %get-tuple-element.25), channel_id=1, source_target_pairs={{0,1},{1,2},{2,3},{17,16},{18,17},{19,18},{32,33},{33,34},{34,35},... | collective-permute-start | bytes 589832 | tf_op jit(solution)/shard_map/ppermute | solution.py:240
  15.4 1.3 %element_maps.1 = (bf16[625,640]{1,0:T(8,128)(2,1)S(1)}, bf16[625,1024]{1,0:T(8,128)(2,1)S(1)}, bf16[128,625]{1,0:T(8,128)(2,1)S(1)}, s16[128,128]{1,0:T(8,128)(2,1)S(1)}) custom-call(s32[1]{0:T(128)} %bitcast.core, bf16[625,625]{1,0:T(8,128)(2,1)S(1)} %bitcast.15, bf16[6,625,125]{2,1,0:T(8,128)(2,1)S(1)} %bitcast.13, s32[6,1,125]{2,1,0:T(1,128)S(1)} %bitcast.19), custom_call_target="tpu_custom_call" | custom-call | tf_op jit(solution)/shard_map/element_maps/pallas_call | solution.py:246
  16.7 1.9 %all-gather.1 = s16[256,128]{1,0:T(8,128)(2,1)S(1)} all-gather(s16[128,128]{1,0:T(8,128)(2,1)S(1)} %get-tuple-element.29), channel_id=3, replica_groups={{0,16},{32,48},{64,80},{96,112},{128,144},{160,176},{192,208},{224,240}..., dimensions={0}, use_global_device_ids=true | all-gather | bytes 98304 | tf_op jit(solution)/shard_map/all_gather | solution.py:268
  18.6 0.7 %partial_residual.1.partial = f32[625,768]{1,0:T(8,128)S(1)} custom-call(bf16[625,768]{1,0:T(8,128)(2,1)S(1)} %bitcast.14, bf16[625,640]{1,0:T(8,128)(2,1)S(1)} %get-tuple-element.20.couple, bf16[128,768]{1,0:T(8,128)(2,1)S(1)} %collective-permute-done.t1, bf16[128,768]{1,0:T(8,128)(2,1)S(1)} %collective-permute-done.1.t2, ...), custom_call_target="tpu_custom_call" | custom-call | flops 491520000 | bytes 2880000 | tf_op jit(solution)/shard_map/partial_residual/pallas_call | solution.py:259
  19.3 1.0 %residual_offset.1 = (bf16[640,768]{1,0:T(8,128)(2,1)S(1)}, s16[768,128]{1,0:T(8,128)(2,1)S(1)}) custom-call(f32[625,768]{1,0:T(8,128)S(1)} %partial_residual.1.partial, bf16[625,640]{1,0:T(8,128)(2,1)S(1)} %get-tuple-element.20.couple, bf16[128,768]{1,0:T(8,128)(2,1)S(1)} %collective-permute-done.4.t5, bf16[128,625]{1,0:T(8,128)(2,1)S(1)} %get-tuple-element.26.inverse), custom_call_target="tpu_custom_call" | custom-call | tf_op jit(solution)/shard_map/residual_offset/pallas_call | solution.py:269
  20.2 2.1 %all-gather = s16[1536,128]{1,0:T(8,128)(2,1)S(1)} all-gather(s16[768,128]{1,0:T(8,128)(2,1)S(1)} %get-tuple-element.28), channel_id=2, replica_groups={{0,16},{32,48},{64,80},{96,112},{128,144},{160,176},{192,208},{224,240}..., dimensions={0}, use_global_device_ids=true | all-gather | bytes 589824 | tf_op jit(solution)/shard_map/all_gather | solution.py:278
  22.3 0.6 chip_merge.1
  22.9 15.4 %all_to_all.10.received = s16[8,112,128]{2,1,0:T(8,128)(2,1)S(1)} all-to-all(s16[8,112,128]{2,1,0:T(8,128)(2,1)S(1)} %chip_merge.1), channel_id=1, replica_groups={{0,16,32,48,64,80,96,112},{128,144,160,176,192,208,224,240},{256,272,28..., dimensions={0} | all-to-all | bytes 458752 | tf_op jit(solution)/shard_map/all_to_all | solution.py:286
  38.3 0.7 group_scan.1
  39.0 1.3 %collective-permute-start.6 = (s16[224,128]{1,0:T(8,128)(2,1)S(1)}, s16[224,128]{1,0:T(8,128)(2,1)S(1)}, u32[]{:S(2)}, u32[]{:S(2)}) collective-permute-start(s16[224,128]{1,0:T(8,128)(2,1)S(1)} %get-tuple-element.31.own), channel_id=1, source_target_pairs={{128,0},{144,16},{160,32},{176,48},{192,64},{208,80},{224,96},{240... | collective-permute-start | bytes 172040 | tf_op jit(solution)/shard_map/ppermute | solution.py:300
  40.3 0.7 collective-permute-start.8
  41.0 9.1 %collective-permute-start.5 = (s16[96,128]{1,0:T(8,128)(2,1)S(1)}, s16[96,128]{1,0:T(8,128)(2,1)S(1)}, u32[]{:S(2)}, u32[]{:S(2)}) collective-permute-start(s16[96,128]{1,0:T(8,128)(2,1)S(1)} %get-tuple-element.30), channel_id=1, source_target_pairs={{0,128},{16,144},{32,160},{48,176},{64,192},{80,208},{96,224},{112... | collective-permute-start | bytes 73736 | tf_op jit(solution)/shard_map/ppermute | solution.py:300
  50.1 1.5 %collective-permute-done.5.below.first = s16[96,128]{1,0:T(8,128)(2,1)S(1)} collective-permute-done((s16[96,128]{1,0:T(8,128)(2,1)S(1)}, s16[96,128]{1,0:T(8,128)(2,1)S(1)}, u32[]{:S(2)}, u32[]{:S(2)}) %collective-permute-start.5) | collective-permute-done | bytes 24608 | tf_op jit(solution)/shard_map/ppermute | solution.py:300
  52.2 1.3 %collective-permute-start.7 = (s16[96,128]{1,0:T(8,128)(2,1)S(1)}, s16[96,128]{1,0:T(8,128)(2,1)S(1)}, u32[]{:S(2)}, u32[]{:S(2)}) collective-permute-start(s16[96,128]{1,0:T(8,128)(2,1)S(1)} %pair_total.1), channel_id=1, source_target_pairs={{128,256},{144,272},{160,288},{176,304},{192,320},{208,336},{224,3... | collective-permute-start | bytes 73736 | tf_op jit(solution)/shard_map/ppermute | solution.py:300
  53.5 1.5 %collective-permute-done.7.pair = s16[96,128]{1,0:T(8,128)(2,1)S(1)} collective-permute-done((s16[96,128]{1,0:T(8,128)(2,1)S(1)}, s16[96,128]{1,0:T(8,128)(2,1)S(1)}, u32[]{:S(2)}, u32[]{:S(2)}) %collective-permute-start.7) | collective-permute-done | bytes 24608 | tf_op jit(solution)/shard_map/ppermute | solution.py:300
  55.0 0.5 group_prefix.1
  55.5 10.7 %all_to_all.11 = s16[8,96,128]{2,1,0:T(8,128)(2,1)S(1)} all-to-all(s16[8,96,128]{2,1,0:T(8,128)(2,1)S(1)} %group_prefix.1), channel_id=1, replica_groups={{0,16,32,48,64,80,96,112},{128,144,160,176,192,208,224,240},{256,272,28..., dimensions={0} | all-to-all | bytes 393216 | tf_op jit(solution)/shard_map/all_to_all | solution.py:320
  66.2 2.3 %update.1 = bf16[625,768]{1,0:T(8,128)(2,1)} custom-call(s32[1]{0:T(128)} %bitcast.core, bf16[625,1024]{1,0:T(8,128)(2,1)S(1)} %get-tuple-element.19.left, bf16[640,768]{1,0:T(8,128)(2,1)S(1)} %get-tuple-element.27.residual, s16[768,128]{1,0:T(8,128)(2,1)S(1)} %bitcast.16, s16[2,768,128]{2,1,0:T(8,128)(2,1)S(1)} %bitcast.12, s16[2,128,128]{2,1,0:T(8,128)(2,1)S(1)} %bitcast.18), custom_call_target="tpu_custom_call" | custom-call | tf_op jit(solution)/shard_map/update/pallas_call | solution.py:322
  (17 shorter events, 0.6 us)
Async XLA Ops:
  0.0 1.2 %copy-start.4 = (bf16[1,1,1,625,768]{4,3,2,1,0:T(8,128)(2,1)S(1)}, bf16[1,1,1,625,768]{4,3,2,1,0:T(8,128)(2,1)}, u32[]{:S(2)}) copy-start(bf16[1,1,1,625,768]{4,3,2,1,0:T(8,128)(2,1)} %param.8) | copy-start | bytes 2880004
  1.2 14.1 %copy-start = (bf16[1,1,1,6,625,125]{5,4,3,2,1,0:T(8,128)(2,1)S(1)}, bf16[1,1,1,6,625,125]{5,4,3,2,1,0:T(8,128)(2,1)}, u32[]{:S(2)}) copy-start(bf16[1,1,1,6,625,125]{5,4,3,2,1,0:T(8,128)(2,1)} %param.7) | copy-start | bytes 2812504
  1.2 14.1 %copy-start.2 = (bf16[1,1,1,625,625]{4,3,2,1,0:T(8,128)(2,1)S(1)}, bf16[1,1,1,625,625]{4,3,2,1,0:T(8,128)(2,1)}, u32[]{:S(2)}) copy-start(bf16[1,1,1,625,625]{4,3,2,1,0:T(8,128)(2,1)} %param.6) | copy-start | bytes 2343754
  1.2 14.1 %copy-start.3 = (s32[1,1,1,6,125]{4,2,3,1,0:T(1,128)S(1)}, s32[1,1,1,6,125]{4,2,3,1,0:T(1,128)}, u32[]{:S(2)}) copy-start(s32[1,1,1,6,125]{4,2,3,1,0:T(1,128)} %param.9) | copy-start | bytes 9004
  2.1 16.4 %copy-start.1 = (bf16[1,1,1,625,768]{4,3,2,1,0:T(8,128)(2,1)S(1)}, bf16[1,1,1,625,768]{4,3,2,1,0:T(8,128)(2,1)}, u32[]{:S(2)}) copy-start(bf16[1,1,1,625,768]{4,3,2,1,0:T(8,128)(2,1)} %param.5) | copy-start | bytes 2880004
  2.2 16.4 %collective-permute-start = (bf16[128,768]{1,0:T(8,128)(2,1)S(1)}, bf16[128,768]{1,0:T(8,128)(2,1)S(1)}, u32[]{:S(2)}, u32[]{:S(2)}) collective-permute-start(bf16[128,768]{1,0:T(8,128)(2,1)S(1)} %get-tuple-element.21), channel_id=1, source_target_pairs={{0,4},{4,8},{8,12},{20,16},{24,20},{28,24},{32,36},{36,40},{40,44}... | collective-permute-start | bytes 589832 | tf_op jit(solution)/shard_map/ppermute | solution.py:240
  3.6 14.9 %collective-permute-start.1 = (bf16[128,768]{1,0:T(8,128)(2,1)S(1)}, bf16[128,768]{1,0:T(8,128)(2,1)S(1)}, u32[]{:S(2)}, u32[]{:S(2)}) collective-permute-start(bf16[128,768]{1,0:T(8,128)(2,1)S(1)} %get-tuple-element.22), channel_id=1, source_target_pairs={{1,0},{2,1},{3,2},{16,17},{17,18},{18,19},{33,32},{34,33},{35,34},... | collective-permute-start | bytes 589832 | tf_op jit(solution)/shard_map/ppermute | solution.py:240
  4.9 13.6 %collective-permute-start.2 = (bf16[128,768]{1,0:T(8,128)(2,1)S(1)}, bf16[128,768]{1,0:T(8,128)(2,1)S(1)}, u32[]{:S(2)}, u32[]{:S(2)}) collective-permute-start(bf16[128,768]{1,0:T(8,128)(2,1)S(1)} %get-tuple-element.23), channel_id=1, source_target_pairs={{16,0},{32,16},{48,32},{64,48},{80,64},{96,80},{112,96},{128,112},... | collective-permute-start | bytes 589832 | tf_op jit(solution)/shard_map/ppermute | solution.py:230
  6.2 12.3 %collective-permute-start.3 = (bf16[128,768]{1,0:T(8,128)(2,1)S(1)}, bf16[128,768]{1,0:T(8,128)(2,1)S(1)}, u32[]{:S(2)}, u32[]{:S(2)}) collective-permute-start(bf16[128,768]{1,0:T(8,128)(2,1)S(1)} %get-tuple-element.24), channel_id=1, source_target_pairs={{4,0},{8,4},{12,8},{16,20},{20,24},{24,28},{36,32},{40,36},{44,40}... | collective-permute-start | bytes 589832 | tf_op jit(solution)/shard_map/ppermute | solution.py:240
  10.8 8.5 %collective-permute-start.4 = (bf16[128,768]{1,0:T(8,128)(2,1)S(1)}, bf16[128,768]{1,0:T(8,128)(2,1)S(1)}, u32[]{:S(2)}, u32[]{:S(2)}) collective-permute-start(bf16[128,768]{1,0:T(8,128)(2,1)S(1)} %get-tuple-element.25), channel_id=1, source_target_pairs={{0,1},{1,2},{2,3},{17,16},{18,17},{19,18},{32,33},{33,34},{34,35},... | collective-permute-start | bytes 589832 | tf_op jit(solution)/shard_map/ppermute | solution.py:240
  39.0 12.8 %collective-permute-start.6 = (s16[224,128]{1,0:T(8,128)(2,1)S(1)}, s16[224,128]{1,0:T(8,128)(2,1)S(1)}, u32[]{:S(2)}, u32[]{:S(2)}) collective-permute-start(s16[224,128]{1,0:T(8,128)(2,1)S(1)} %get-tuple-element.31.own), channel_id=1, source_target_pairs={{128,0},{144,16},{160,32},{176,48},{192,64},{208,80},{224,96},{240... | collective-permute-start | bytes 172040 | tf_op jit(solution)/shard_map/ppermute | solution.py:300
  40.3 13.2 %collective-permute-start.8 = (s16[224,128]{1,0:T(8,128)(2,1)S(1)}, s16[224,128]{1,0:T(8,128)(2,1)S(1)}, u32[]{:S(2)}, u32[]{:S(2)}) collective-permute-start(s16[224,128]{1,0:T(8,128)(2,1)S(1)} %get-tuple-element.31.own), channel_id=1, source_target_pairs={{256,384},{272,400},{288,416},{304,432},{320,448},{336,464},{352,4... | collective-permute-start | bytes 172040 | tf_op jit(solution)/shard_map/ppermute | solution.py:300
  41.0 10.6 %collective-permute-start.5 = (s16[96,128]{1,0:T(8,128)(2,1)S(1)}, s16[96,128]{1,0:T(8,128)(2,1)S(1)}, u32[]{:S(2)}, u32[]{:S(2)}) collective-permute-start(s16[96,128]{1,0:T(8,128)(2,1)S(1)} %get-tuple-element.30), channel_id=1, source_target_pairs={{0,128},{16,144},{32,160},{48,176},{64,192},{80,208},{96,224},{112... | collective-permute-start | bytes 73736 | tf_op jit(solution)/shard_map/ppermute | solution.py:300
  52.2 2.8 %collective-permute-start.7 = (s16[96,128]{1,0:T(8,128)(2,1)S(1)}, s16[96,128]{1,0:T(8,128)(2,1)S(1)}, u32[]{:S(2)}, u32[]{:S(2)}) collective-permute-start(s16[96,128]{1,0:T(8,128)(2,1)S(1)} %pair_total.1), channel_id=1, source_target_pairs={{128,256},{144,272},{160,288},{176,304},{192,320},{208,336},{224,3... | collective-permute-start | bytes 73736 | tf_op jit(solution)/shard_map/ppermute | solution.py:300

commit v5 on v4

--- a/solution.py
+++ b/solution.py
@@ -105,28 +105,28 @@
 
 
 def offset_kernel(partial, couple, t5, inverse, residual_out, offset_out):
-    block = offset_out.shape[0] // 2
-    for start in (0, block):
-        cut = slice(start, start + block)
-        pulled = dot(couple[:, 4 * WIDE :], t5[:, cut])
-        residual = (partial[:, cut] - pulled).astype(bf16)
-        padding = jnp.zeros((residual_out.shape[0] - residual.shape[0], block), bf16)
-        residual_out[:, cut] = jnp.concatenate([residual, padding], axis=0)
-        offset_out[cut, :] = coded(dot(inverse[...], residual).T)
+    pulled = dot(couple[:, 4 * WIDE :], t5[...])
+    residual = (partial[...] - pulled).astype(bf16)
+    rows, width = residual.shape
+    padding = jnp.zeros((residual_out.shape[0] - rows, width), bf16)
+    residual_out[...] = jnp.concatenate([residual, padding], axis=0)
+    offset_out[...] = coded(dot(inverse[...], residual).T)
 
 
 def merge_kernel(core, offsets, maps, send_out):
     count, rows, _ = send_out.shape
     half = rows - WIDE // 2
     last = split_right(decoded(maps[1]), 0)
-    merged = decoded(offsets[1]) + dot(split_left(decoded(offsets[0])), last)
     step = dot(split_left(decoded(maps[0])), last)
-    first = core[0] == 0
-    step = coded(jnp.where(first, step[: WIDE // 2], step[WIDE // 2 :]))
+    step = coded(jnp.where(core[0] == 0, step[: WIDE // 2], step[WIDE // 2 :]))
+
+    def mine(which):
+        starts = (pl.multiple_of((2 * at + core[0]) * half, 16) for at in range(count))
+        return jnp.concatenate([offsets[which, pl.ds(start, half), :] for start in starts], axis=0)
+
+    merged = coded(decoded(mine(1)) + dot(split_left(decoded(mine(0))), last))
     for at in range(count):
-        low = merged[2 * at * half : (2 * at + 1) * half]
-        high = merged[(2 * at + 1) * half : (2 * at + 2) * half]
-        send_out[at, :half, :] = coded(jnp.where(first, low, high))
+        send_out[at, :half, :] = merged[at * half : (at + 1) * half]
         send_out[at, half:, :] = step
 
 
@@ -163,7 +163,7 @@
     out[...] = coded(passed(entering, state))
 
 
-def prefix_kernel(group, first, pair, third, states, out):
+def prefix_kernel(group, first, pair, third, states, solved, out):
     count, part, _ = out.shape
     entering = decoded(pair[...])
     later = passed(entering, decoded(third[...]))
@@ -179,17 +179,24 @@
         out[at + 1] = value
 
 
-def update_kernel(core, left, residual, arrived, offsets, maps, out, held, sems):
-    block = WIDE * 2
+def solve_kernel(core, left, residual, offsets, maps, solved_out, gain_out):
+    later = core[0] == 1
+    offset = jnp.where(later, decoded(offsets[0]), 0.0)
+    right = jnp.concatenate([residual[...], split_right(offset.T, 0)], axis=0)
+    solved_out[...] = dot(left[...], right)
+    gain = left[:, TALL:]
+    own = gain[:, :WIDE].astype(f32) + gain[:, WIDE : 2 * WIDE].astype(f32)
+    through = dot(gain, split_right(decoded(maps[0]).T, 0))
+    gain_out[...] = split_left(jnp.where(later, through, own))
+
+
+def update_kernel(solved, gain, arrived, out, held, sems):
+    block = held.shape[1] // sems.shape[0]
     copies = []
-    step = split_right(decoded(maps[0]), 0)
-    for at, start in enumerate(range(0, held.shape[1], block)):
-        cut = slice(start, start + block)
-        entering = decoded(arrived[cut, :])
-        later = decoded(offsets[0, cut, :]) + dot(split_left(entering), step)
-        entering = jnp.where(core[0] == 0, entering, later)
-        right = jnp.concatenate([residual[:, cut], split_right(entering.T, 0)], axis=0)
-        held[:, cut] = dot(left[...], right).astype(bf16)
+    for at in range(sems.shape[0]):
+        cut = slice(at * block, (at + 1) * block)
+        moved = dot(gain[...], split_right(decoded(arrived[cut, :]).T, 0))
+        held[:, cut] = (solved[:, cut] + moved).astype(bf16)
         copies.append(pltpu.make_async_copy(held.at[:, cut], out.at[:, cut], sems.at[at]))
         copies[-1].start()
     for copy in copies:
@@ -207,7 +214,6 @@
     near = [[g * GROUP + i for i in range(GROUP)] for g in range(4)]
 
     outer = pl.BlockSpec(memory_space=pltpu.HBM)
-    blocks = width // (2 * WIDE)
 
     scalar = pl.BlockSpec(memory_space=pltpu.SMEM)
     inner = pl.BlockSpec(memory_space=pltpu.VMEM)
@@ -302,6 +308,19 @@
     above = between(both, (1, 0))
     first = between(total, (0, 1))
     third = between(both, (2, 3))
+    solved, gain = pl.pallas_call(
+        solve_kernel,
+        in_specs=[scalar] + [inner] * 4,
+        out_shape=[
+            jax.ShapeDtypeStruct((rows, width), f32),
+            jax.ShapeDtypeStruct((rows, 3 * WIDE), bf16),
+        ],
+        cost_estimate=pl.CostEstimate(
+            flops=2 * rows * 1024 * width, bytes_accessed=4 * rows * width, transcendentals=0
+        ),
+        compiler_params=params(),
+        name="solve",
+    )(core, left, residual, offsets, maps)
     pair = pl.pallas_call(
         pair_kernel,
         in_specs=[scalar] + [inner] * 3,
@@ -312,22 +331,22 @@
     pair = between(pair, (1, 2), (0, 3))
     entering = pl.pallas_call(
         prefix_kernel,
-        in_specs=[scalar] + [inner] * 4,
+        in_specs=[scalar] + [inner] * 5,
         out_shape=jax.ShapeDtypeStruct((GROUP, part, WIDE), WIRE),
         compiler_params=params(),
         name="group_prefix",
-    )(group, first, pair, third, states)
+    )(group, first, pair, third, states, solved)
     arrived = lax.all_to_all(entering, "stream", 0, 0, tiled=True, axis_index_groups=near)
 
     updated = pl.pallas_call(
         update_kernel,
-        in_specs=[scalar] + [inner] * 5,
+        in_specs=[inner] * 3,
         out_specs=outer,
         out_shape=jax.ShapeDtypeStruct((rows, width), bf16),
-        scratch_shapes=[pltpu.VMEM((rows, width), bf16), pltpu.SemaphoreType.DMA((blocks,))],
+        scratch_shapes=[pltpu.VMEM((rows, width), bf16), pltpu.SemaphoreType.DMA((3,))],
         compiler_params=params(),
         name="update",
-    )(core, left, residual, arrived.reshape(width, WIDE), offsets, maps)
+    )(solved, gain, arrived.reshape(width, WIDE))
     return updated[None, None, None]
 
 

time: 69.5 us -> 68.6 us (0.987)
  waiting for transfers between devices: 3.23 us -> 1.87 us
    ppermute x4, waiting for transfers between devices: 3.22 us -> 1.86 us  [between(): return lax.ppermute(value, 'stream', moves)]
    pallas_call x2 -> x3, Pallas kernels: 2.84 us -> 3.62 us  [the longest x1 1.72 us: on_device(): pl.pallas_call(update_kernel, in_specs=[inner] * 3, out_specs=outer, out_...]
  transfers between devices with their start and end apart: 9 -> 9, of which waited for: 3 -> 3; matrix products, arithmetic and copies ran while one was open for 0% -> 0% of each run, Pallas kernels for 3% -> 6%
where the time goes in v5:
time: 68.6 us; the launch traced here: 67.7 us
  blocking collectives  30 us (44%)
  starting transfers between devices  25.5 us (37%)
  Pallas kernels  8.91 us (13%)
  waiting for transfers between devices  1.87 us (3%)
  local copies, waits for them, and re-layouts  1.21 us (2%)
    all_to_all x1, blocking collectives, on_device(): lax.all_to_all(sent, 'stream', 0, 0, tiled=True, axis_index_groups=near)  15.4 us
    ppermute x4, starting transfers between devices, between(): return lax.ppermute(value, 'stream', moves)  12.3 us
    ppermute x4, starting transfers between devices, sideways(): return lax.ppermute(value, ('stream', axis), pairs)  11.8 us
    all_to_all x1, blocking collectives, on_device(): lax.all_to_all(entering, 'stream', 0, 0, tiled=True, axis_index_groups=near)  10.7 us
    all_gather x1, blocking collectives, on_device(): offsets = lax.all_gather(offset, 'stream', axis_index_groups=chips)  2.09 us
    ppermute x4, waiting for transfers between devices, between(): return lax.ppermute(value, 'stream', moves)  1.86 us
    all_gather x1, blocking collectives, on_device(): maps = lax.all_gather(maps, 'stream', axis_index_groups=chips)  1.85 us
    pallas_call x1, Pallas kernels, on_device(): pl.pallas_call(update_kernel, in_specs=[inner] * 3, out_specs=outer, out_...  1.72 us
  transfers between devices with their start and end apart: 9, of which 3 were waited for; matrix products, arithmetic and copies ran while one was open for 0% of the time, Pallas kernels for 6%

profile of v5, /device:TPU:24, one launch (start us, length us, event | category | flops | bytes accessed | tf_op | source)
XLA Modules:
  0.0 67.7 jit_solution(370315416245584627)
XLA Ops:
  0.0 1.2 %copy-done.4 = bf16[1,1,1,625,768]{4,3,2,1,0:T(8,128)(2,1)S(1)} copy-done((bf16[1,1,1,625,768]{4,3,2,1,0:T(8,128)(2,1)S(1)}, bf16[1,1,1,625,768]{4,3,2,1,0:T(8,128)(2,1)}, u32[]{:S(2)}) %copy-start.4) | copy-done | bytes 960024
  1.2 0.9 %face_traces.1 = (bf16[128,768]{1,0:T(8,128)(2,1)S(1)}, bf16[128,768]{1,0:T(8,128)(2,1)S(1)}, bf16[128,768]{1,0:T(8,128)(2,1)S(1)}, bf16[128,768]{1,0:T(8,128)(2,1)S(1)}, bf16[128,768]{1,0:T(8,128)(2,1)S(1)}) custom-call(s32[1]{0:T(128)} %bitcast.core, bf16[625,768]{1,0:T(8,128)(2,1)S(1)} %bitcast.20), custom_call_target="tpu_custom_call" | custom-call | flops 8000000000 | bytes 960000 | tf_op jit(solution)/shard_map/face_traces/pallas_call | solution.py:224
  2.2 1.4 %collective-permute-start = (bf16[128,768]{1,0:T(8,128)(2,1)S(1)}, bf16[128,768]{1,0:T(8,128)(2,1)S(1)}, u32[]{:S(2)}, u32[]{:S(2)}) collective-permute-start(bf16[128,768]{1,0:T(8,128)(2,1)S(1)} %get-tuple-element.23), channel_id=1, source_target_pairs={{0,4},{4,8},{8,12},{20,16},{24,20},{28,24},{32,36},{36,40},{40,44}... | collective-permute-start | bytes 589832 | tf_op jit(solution)/shard_map/ppermute | solution.py:246
  3.6 1.3 %collective-permute-start.1 = (bf16[128,768]{1,0:T(8,128)(2,1)S(1)}, bf16[128,768]{1,0:T(8,128)(2,1)S(1)}, u32[]{:S(2)}, u32[]{:S(2)}) collective-permute-start(bf16[128,768]{1,0:T(8,128)(2,1)S(1)} %get-tuple-element.24), channel_id=1, source_target_pairs={{1,0},{2,1},{3,2},{16,17},{17,18},{18,19},{33,32},{34,33},{35,34},... | collective-permute-start | bytes 589832 | tf_op jit(solution)/shard_map/ppermute | solution.py:246
  4.9 1.3 %collective-permute-start.2 = (bf16[128,768]{1,0:T(8,128)(2,1)S(1)}, bf16[128,768]{1,0:T(8,128)(2,1)S(1)}, u32[]{:S(2)}, u32[]{:S(2)}) collective-permute-start(bf16[128,768]{1,0:T(8,128)(2,1)S(1)} %get-tuple-element.25), channel_id=1, source_target_pairs={{16,0},{32,16},{48,32},{64,48},{80,64},{96,80},{112,96},{128,112},... | collective-permute-start | bytes 589832 | tf_op jit(solution)/shard_map/ppermute | solution.py:236
  6.2 4.6 %collective-permute-start.3 = (bf16[128,768]{1,0:T(8,128)(2,1)S(1)}, bf16[128,768]{1,0:T(8,128)(2,1)S(1)}, u32[]{:S(2)}, u32[]{:S(2)}) collective-permute-start(bf16[128,768]{1,0:T(8,128)(2,1)S(1)} %get-tuple-element.26), channel_id=1, source_target_pairs={{4,0},{8,4},{12,8},{16,20},{20,24},{24,28},{36,32},{40,36},{44,40}... | collective-permute-start | bytes 589832 | tf_op jit(solution)/shard_map/ppermute | solution.py:246
  10.8 4.6 %collective-permute-start.4 = (bf16[128,768]{1,0:T(8,128)(2,1)S(1)}, bf16[128,768]{1,0:T(8,128)(2,1)S(1)}, u32[]{:S(2)}, u32[]{:S(2)}) collective-permute-start(bf16[128,768]{1,0:T(8,128)(2,1)S(1)} %get-tuple-element.27), channel_id=1, source_target_pairs={{0,1},{1,2},{2,3},{17,16},{18,17},{19,18},{32,33},{33,34},{34,35},... | collective-permute-start | bytes 589832 | tf_op jit(solution)/shard_map/ppermute | solution.py:246
  15.4 1.3 %element_maps.1 = (bf16[625,640]{1,0:T(8,128)(2,1)S(1)}, bf16[625,1024]{1,0:T(8,128)(2,1)S(1)}, bf16[128,625]{1,0:T(8,128)(2,1)S(1)}, s16[128,128]{1,0:T(8,128)(2,1)S(1)}) custom-call(s32[1]{0:T(128)} %bitcast.core, bf16[625,625]{1,0:T(8,128)(2,1)S(1)} %bitcast.15, bf16[6,625,125]{2,1,0:T(8,128)(2,1)S(1)} %bitcast.13, s32[6,1,125]{2,1,0:T(1,128)S(1)} %bitcast.19), custom_call_target="tpu_custom_call" | custom-call | tf_op jit(solution)/shard_map/element_maps/pallas_call | solution.py:252
  16.7 1.9 %all-gather.1 = s16[256,128]{1,0:T(8,128)(2,1)S(1)} all-gather(s16[128,128]{1,0:T(8,128)(2,1)S(1)} %get-tuple-element.31), channel_id=3, replica_groups={{0,16},{32,48},{64,80},{96,112},{128,144},{160,176},{192,208},{224,240}..., dimensions={0}, use_global_device_ids=true | all-gather | bytes 98304 | tf_op jit(solution)/shard_map/all_gather | solution.py:274
  18.6 0.7 %partial_residual.1.partial = f32[625,768]{1,0:T(8,128)S(1)} custom-call(bf16[625,768]{1,0:T(8,128)(2,1)S(1)} %bitcast.14, bf16[625,640]{1,0:T(8,128)(2,1)S(1)} %get-tuple-element.22.couple, bf16[128,768]{1,0:T(8,128)(2,1)S(1)} %collective-permute-done.t1, bf16[128,768]{1,0:T(8,128)(2,1)S(1)} %collective-permute-done.1.t2, ...), custom_call_target="tpu_custom_call" | custom-call | flops 491520000 | bytes 2880000 | tf_op jit(solution)/shard_map/partial_residual/pallas_call | solution.py:265
  19.3 0.9 %residual_offset.1 = (bf16[640,768]{1,0:T(8,128)(2,1)S(1)}, s16[768,128]{1,0:T(8,128)(2,1)S(1)}) custom-call(f32[625,768]{1,0:T(8,128)S(1)} %partial_residual.1.partial, bf16[625,640]{1,0:T(8,128)(2,1)S(1)} %get-tuple-element.22.couple, bf16[128,768]{1,0:T(8,128)(2,1)S(1)} %collective-permute-done.4.t5, bf16[128,625]{1,0:T(8,128)(2,1)S(1)} %get-tuple-element.28.inverse), custom_call_target="tpu_custom_call" | custom-call | tf_op jit(solution)/shard_map/residual_offset/pallas_call | solution.py:275
  20.1 2.1 %all-gather = s16[1536,128]{1,0:T(8,128)(2,1)S(1)} all-gather(s16[768,128]{1,0:T(8,128)(2,1)S(1)} %get-tuple-element.30), channel_id=2, replica_groups={{0,16},{32,48},{64,80},{96,112},{128,144},{160,176},{192,208},{224,240}..., dimensions={0}, use_global_device_ids=true | all-gather | bytes 589824 | tf_op jit(solution)/shard_map/all_gather | solution.py:284
  22.7 15.4 %all_to_all.10.received = s16[8,112,128]{2,1,0:T(8,128)(2,1)S(1)} all-to-all(s16[8,112,128]{2,1,0:T(8,128)(2,1)S(1)} %chip_merge.1), channel_id=1, replica_groups={{0,16,32,48,64,80,96,112},{128,144,160,176,192,208,224,240},{256,272,28..., dimensions={0} | all-to-all | bytes 458752 | tf_op jit(solution)/shard_map/all_to_all | solution.py:292
  38.1 0.7 group_scan.1
  38.7 1.3 %collective-permute-start.6 = (s16[224,128]{1,0:T(8,128)(2,1)S(1)}, s16[224,128]{1,0:T(8,128)(2,1)S(1)}, u32[]{:S(2)}, u32[]{:S(2)}) collective-permute-start(s16[224,128]{1,0:T(8,128)(2,1)S(1)} %get-tuple-element.35.own), channel_id=1, source_target_pairs={{128,0},{144,16},{160,32},{176,48},{192,64},{208,80},{224,96},{240... | collective-permute-start | bytes 172040 | tf_op jit(solution)/shard_map/ppermute | solution.py:306
  40.0 9.1 %collective-permute-start.5 = (s16[96,128]{1,0:T(8,128)(2,1)S(1)}, s16[96,128]{1,0:T(8,128)(2,1)S(1)}, u32[]{:S(2)}, u32[]{:S(2)}) collective-permute-start(s16[96,128]{1,0:T(8,128)(2,1)S(1)} %get-tuple-element.34), channel_id=1, source_target_pairs={{0,128},{16,144},{32,160},{48,176},{64,192},{80,208},{96,224},{112... | collective-permute-start | bytes 73736 | tf_op jit(solution)/shard_map/ppermute | solution.py:306
  49.1 0.7 collective-permute-start.8
  49.8 0.8 %collective-permute-done.5.below.first = s16[96,128]{1,0:T(8,128)(2,1)S(1)} collective-permute-done((s16[96,128]{1,0:T(8,128)(2,1)S(1)}, s16[96,128]{1,0:T(8,128)(2,1)S(1)}, u32[]{:S(2)}, u32[]{:S(2)}) %collective-permute-start.5) | collective-permute-done | bytes 24608 | tf_op jit(solution)/shard_map/ppermute | solution.py:306
  50.6 0.9 %collective-permute-done.6.above = s16[224,128]{1,0:T(8,128)(2,1)S(1)} collective-permute-done((s16[224,128]{1,0:T(8,128)(2,1)S(1)}, s16[224,128]{1,0:T(8,128)(2,1)S(1)}, u32[]{:S(2)}, u32[]{:S(2)}) %collective-permute-start.6) | collective-permute-done | bytes 57376 | tf_op jit(solution)/shard_map/ppermute | solution.py:306
  51.9 1.3 %collective-permute-start.7 = (s16[96,128]{1,0:T(8,128)(2,1)S(1)}, s16[96,128]{1,0:T(8,128)(2,1)S(1)}, u32[]{:S(2)}, u32[]{:S(2)}) collective-permute-start(s16[96,128]{1,0:T(8,128)(2,1)S(1)} %pair_total.1), channel_id=1, source_target_pairs={{128,256},{144,272},{160,288},{176,304},{192,320},{208,336},{224,3... | collective-permute-start | bytes 73736 | tf_op jit(solution)/shard_map/ppermute | solution.py:306
  53.2 1.4 %solve.1 = (f32[625,768]{1,0:T(8,128)S(1)}, bf16[625,384]{1,0:T(8,128)(2,1)S(1)}) custom-call(s32[1]{0:T(128)} %bitcast.core, bf16[625,1024]{1,0:T(8,128)(2,1)S(1)} %get-tuple-element.21.left, bf16[640,768]{1,0:T(8,128)(2,1)S(1)} %get-tuple-element.29.residual, s16[2,768,128]{2,1,0:T(8,128)(2,1)S(1)} %bitcast.12, s16[2,128,128]{2,1,0:T(8,128)(2,1)S(1)} %bitcast.18), custom_call_target="tpu_custom_call" | custom-call | flops 983040000 | bytes 1920000 | tf_op jit(solution)/shard_map/solve/pallas_call | solution.py:311
  54.7 0.5 group_prefix.1
  55.3 10.7 %all_to_all.11 = s16[8,96,128]{2,1,0:T(8,128)(2,1)S(1)} all-to-all(s16[8,96,128]{2,1,0:T(8,128)(2,1)S(1)} %group_prefix.1), channel_id=1, replica_groups={{0,16,32,48,64,80,96,112},{128,144,160,176,192,208,224,240},{256,272,28..., dimensions={0} | all-to-all | bytes 393216 | tf_op jit(solution)/shard_map/all_to_all | solution.py:339
  66.0 1.7 %update.1 = bf16[625,768]{1,0:T(8,128)(2,1)} custom-call(f32[625,768]{1,0:T(8,128)S(1)} %get-tuple-element.32.solved, bf16[625,384]{1,0:T(8,128)(2,1)S(1)} %get-tuple-element.33.gain, s16[768,128]{1,0:T(8,128)(2,1)S(1)} %bitcast.16), custom_call_target="tpu_custom_call" | custom-call | tf_op jit(solution)/shard_map/update/pallas_call | solution.py:341
  (18 shorter events, 1.0 us)
Async XLA Ops:
  0.0 1.2 %copy-start.4 = (bf16[1,1,1,625,768]{4,3,2,1,0:T(8,128)(2,1)S(1)}, bf16[1,1,1,625,768]{4,3,2,1,0:T(8,128)(2,1)}, u32[]{:S(2)}) copy-start(bf16[1,1,1,625,768]{4,3,2,1,0:T(8,128)(2,1)} %param.8) | copy-start | bytes 2880004
  1.2 14.1 %copy-start = (bf16[1,1,1,6,625,125]{5,4,3,2,1,0:T(8,128)(2,1)S(1)}, bf16[1,1,1,6,625,125]{5,4,3,2,1,0:T(8,128)(2,1)}, u32[]{:S(2)}) copy-start(bf16[1,1,1,6,625,125]{5,4,3,2,1,0:T(8,128)(2,1)} %param.7) | copy-start | bytes 2812504
  1.2 14.1 %copy-start.2 = (bf16[1,1,1,625,625]{4,3,2,1,0:T(8,128)(2,1)S(1)}, bf16[1,1,1,625,625]{4,3,2,1,0:T(8,128)(2,1)}, u32[]{:S(2)}) copy-start(bf16[1,1,1,625,625]{4,3,2,1,0:T(8,128)(2,1)} %param.6) | copy-start | bytes 2343754
  1.2 14.1 %copy-start.3 = (s32[1,1,1,6,125]{4,2,3,1,0:T(1,128)S(1)}, s32[1,1,1,6,125]{4,2,3,1,0:T(1,128)}, u32[]{:S(2)}) copy-start(s32[1,1,1,6,125]{4,2,3,1,0:T(1,128)} %param.9) | copy-start | bytes 9004
  2.1 16.4 %copy-start.1 = (bf16[1,1,1,625,768]{4,3,2,1,0:T(8,128)(2,1)S(1)}, bf16[1,1,1,625,768]{4,3,2,1,0:T(8,128)(2,1)}, u32[]{:S(2)}) copy-start(bf16[1,1,1,625,768]{4,3,2,1,0:T(8,128)(2,1)} %param.5) | copy-start | bytes 2880004
  2.2 16.4 %collective-permute-start = (bf16[128,768]{1,0:T(8,128)(2,1)S(1)}, bf16[128,768]{1,0:T(8,128)(2,1)S(1)}, u32[]{:S(2)}, u32[]{:S(2)}) collective-permute-start(bf16[128,768]{1,0:T(8,128)(2,1)S(1)} %get-tuple-element.23), channel_id=1, source_target_pairs={{0,4},{4,8},{8,12},{20,16},{24,20},{28,24},{32,36},{36,40},{40,44}... | collective-permute-start | bytes 589832 | tf_op jit(solution)/shard_map/ppermute | solution.py:246
  3.6 14.9 %collective-permute-start.1 = (bf16[128,768]{1,0:T(8,128)(2,1)S(1)}, bf16[128,768]{1,0:T(8,128)(2,1)S(1)}, u32[]{:S(2)}, u32[]{:S(2)}) collective-permute-start(bf16[128,768]{1,0:T(8,128)(2,1)S(1)} %get-tuple-element.24), channel_id=1, source_target_pairs={{1,0},{2,1},{3,2},{16,17},{17,18},{18,19},{33,32},{34,33},{35,34},... | collective-permute-start | bytes 589832 | tf_op jit(solution)/shard_map/ppermute | solution.py:246
  4.9 13.6 %collective-permute-start.2 = (bf16[128,768]{1,0:T(8,128)(2,1)S(1)}, bf16[128,768]{1,0:T(8,128)(2,1)S(1)}, u32[]{:S(2)}, u32[]{:S(2)}) collective-permute-start(bf16[128,768]{1,0:T(8,128)(2,1)S(1)} %get-tuple-element.25), channel_id=1, source_target_pairs={{16,0},{32,16},{48,32},{64,48},{80,64},{96,80},{112,96},{128,112},... | collective-permute-start | bytes 589832 | tf_op jit(solution)/shard_map/ppermute | solution.py:236
  6.2 12.3 %collective-permute-start.3 = (bf16[128,768]{1,0:T(8,128)(2,1)S(1)}, bf16[128,768]{1,0:T(8,128)(2,1)S(1)}, u32[]{:S(2)}, u32[]{:S(2)}) collective-permute-start(bf16[128,768]{1,0:T(8,128)(2,1)S(1)} %get-tuple-element.26), channel_id=1, source_target_pairs={{4,0},{8,4},{12,8},{16,20},{20,24},{24,28},{36,32},{40,36},{44,40}... | collective-permute-start | bytes 589832 | tf_op jit(solution)/shard_map/ppermute | solution.py:246
  10.8 8.5 %collective-permute-start.4 = (bf16[128,768]{1,0:T(8,128)(2,1)S(1)}, bf16[128,768]{1,0:T(8,128)(2,1)S(1)}, u32[]{:S(2)}, u32[]{:S(2)}) collective-permute-start(bf16[128,768]{1,0:T(8,128)(2,1)S(1)} %get-tuple-element.27), channel_id=1, source_target_pairs={{0,1},{1,2},{2,3},{17,16},{18,17},{19,18},{32,33},{33,34},{34,35},... | collective-permute-start | bytes 589832 | tf_op jit(solution)/shard_map/ppermute | solution.py:246
  38.7 12.8 %collective-permute-start.6 = (s16[224,128]{1,0:T(8,128)(2,1)S(1)}, s16[224,128]{1,0:T(8,128)(2,1)S(1)}, u32[]{:S(2)}, u32[]{:S(2)}) collective-permute-start(s16[224,128]{1,0:T(8,128)(2,1)S(1)} %get-tuple-element.35.own), channel_id=1, source_target_pairs={{128,0},{144,16},{160,32},{176,48},{192,64},{208,80},{224,96},{240... | collective-permute-start | bytes 172040 | tf_op jit(solution)/shard_map/ppermute | solution.py:306
  40.0 10.6 %collective-permute-start.5 = (s16[96,128]{1,0:T(8,128)(2,1)S(1)}, s16[96,128]{1,0:T(8,128)(2,1)S(1)}, u32[]{:S(2)}, u32[]{:S(2)}) collective-permute-start(s16[96,128]{1,0:T(8,128)(2,1)S(1)} %get-tuple-element.34), channel_id=1, source_target_pairs={{0,128},{16,144},{32,160},{48,176},{64,192},{80,208},{96,224},{112... | collective-permute-start | bytes 73736 | tf_op jit(solution)/shard_map/ppermute | solution.py:306
  49.1 5.5 %collective-permute-start.8 = (s16[224,128]{1,0:T(8,128)(2,1)S(1)}, s16[224,128]{1,0:T(8,128)(2,1)S(1)}, u32[]{:S(2)}, u32[]{:S(2)}) collective-permute-start(s16[224,128]{1,0:T(8,128)(2,1)S(1)} %get-tuple-element.35.own), channel_id=1, source_target_pairs={{256,384},{272,400},{288,416},{304,432},{320,448},{336,464},{352,4... | collective-permute-start | bytes 172040 | tf_op jit(solution)/shard_map/ppermute | solution.py:306
  51.9 2.8 %collective-permute-start.7 = (s16[96,128]{1,0:T(8,128)(2,1)S(1)}, s16[96,128]{1,0:T(8,128)(2,1)S(1)}, u32[]{:S(2)}, u32[]{:S(2)}) collective-permute-start(s16[96,128]{1,0:T(8,128)(2,1)S(1)} %pair_total.1), channel_id=1, source_target_pairs={{128,256},{144,272},{160,288},{176,304},{192,320},{208,336},{224,3... | collective-permute-start | bytes 73736 | tf_op jit(solution)/shard_map/ppermute | solution.py:306

commit v6 on v5

--- a/solution.py
+++ b/solution.py
@@ -104,20 +104,22 @@
     out[...] = right_side[...].astype(f32) - dot(couple[:, : 4 * WIDE], traces)
 
 
-def offset_kernel(partial, couple, t5, inverse, residual_out, offset_out):
+def offset_kernel(partial, couple, t5, inverse, maps, residual_out, offset_out):
     pulled = dot(couple[:, 4 * WIDE :], t5[...])
     residual = (partial[...] - pulled).astype(bf16)
     rows, width = residual.shape
     padding = jnp.zeros((residual_out.shape[0] - rows, width), bf16)
     residual_out[...] = jnp.concatenate([residual, padding], axis=0)
-    offset_out[...] = coded(dot(inverse[...], residual).T)
-
-
-def merge_kernel(core, offsets, maps, send_out):
+    offset_out[:width, :] = coded(dot(inverse[...], residual).T)
+    offset_out[width:, :] = maps[...]
+
+
+def merge_kernel(core, offsets, send_out):
     count, rows, _ = send_out.shape
     half = rows - WIDE // 2
-    last = split_right(decoded(maps[1]), 0)
-    step = dot(split_left(decoded(maps[0])), last)
+    width = 2 * count * half
+    last = split_right(decoded(offsets[1, width:, :]), 0)
+    step = dot(split_left(decoded(offsets[0, width:, :])), last)
     step = coded(jnp.where(core[0] == 0, step[: WIDE // 2], step[WIDE // 2 :]))
 
     def mine(which):
@@ -179,14 +181,15 @@
         out[at + 1] = value
 
 
-def solve_kernel(core, left, residual, offsets, maps, solved_out, gain_out):
+def solve_kernel(core, left, residual, offsets, solved_out, gain_out):
     later = core[0] == 1
-    offset = jnp.where(later, decoded(offsets[0]), 0.0)
+    width = residual.shape[1]
+    offset = jnp.where(later, decoded(offsets[0, :width, :]), 0.0)
     right = jnp.concatenate([residual[...], split_right(offset.T, 0)], axis=0)
     solved_out[...] = dot(left[...], right)
     gain = left[:, TALL:]
     own = gain[:, :WIDE].astype(f32) + gain[:, WIDE : 2 * WIDE].astype(f32)
-    through = dot(gain, split_right(decoded(maps[0]).T, 0))
+    through = dot(gain, split_right(decoded(offsets[0, width:, :]).T, 0))
     gain_out[...] = split_left(jnp.where(later, through, own))
 
 
@@ -271,24 +274,23 @@
         compiler_params=params(),
         name="partial_residual",
     )(right_side, couple, *(halos[at] for at in (1, 2, 0, 3)))
-    maps = lax.all_gather(maps, "stream", axis_index_groups=chips)
     residual, offset = pl.pallas_call(
         offset_kernel,
         out_shape=[
             jax.ShapeDtypeStruct((TALL, width), bf16),
-            jax.ShapeDtypeStruct((width, WIDE), WIRE),
+            jax.ShapeDtypeStruct((width + WIDE, WIDE), WIRE),
         ],
         compiler_params=params(),
         name="residual_offset",
-    )(partial, couple, halos[4], picked)
+    )(partial, couple, halos[4], picked, maps)
     offsets = lax.all_gather(offset, "stream", axis_index_groups=chips)
     sent = pl.pallas_call(
         merge_kernel,
-        in_specs=[scalar, inner, inner],
+        in_specs=[scalar, inner],
         out_shape=jax.ShapeDtypeStruct((GROUP, (part + WIDE) // 2, WIDE), WIRE),
         compiler_params=params(),
         name="chip_merge",
-    )(core, offsets, maps)
+    )(core, offsets)
     received = lax.all_to_all(sent, "stream", 0, 0, tiled=True, axis_index_groups=near)
     states, total, both = pl.pallas_call(
         scan_kernel,
@@ -310,7 +312,7 @@
     third = between(both, (2, 3))
     solved, gain = pl.pallas_call(
         solve_kernel,
-        in_specs=[scalar] + [inner] * 4,
+        in_specs=[scalar] + [inner] * 3,
         out_shape=[
             jax.ShapeDtypeStruct((rows, width), f32),
             jax.ShapeDtypeStruct((rows, 3 * WIDE), bf16),
@@ -320,7 +322,7 @@
         ),
         compiler_params=params(),
         name="solve",
-    )(core, left, residual, offsets, maps)
+    )(core, left, residual, offsets)
     pair = pl.pallas_call(
         pair_kernel,
         in_specs=[scalar] + [inner] * 3,

time: 68.6 us -> 68.7 us (level)
  the two profiles are of different devices: /device:TPU:24 before, /device:TPU:30 now
where the time goes in v6:
time: 68.7 us; the launch traced here: 68.3 us
  blocking collectives  28.2 us (41%)
  starting transfers between devices  23.7 us (34%)
  Pallas kernels  8.91 us (13%)
  waiting for transfers between devices  6.05 us (9%)
  local copies, waits for them, and re-layouts  1.21 us (2%)
    all_to_all x1, blocking collectives, on_device(): lax.all_to_all(sent, 'stream', 0, 0, tiled=True, axis_index_groups=near)  15.4 us
    ppermute x4, starting transfers between devices, between(): return lax.ppermute(value, 'stream', moves)  12.3 us
    all_to_all x1, blocking collectives, on_device(): lax.all_to_all(entering, 'stream', 0, 0, tiled=True, axis_index_groups=near)  10.7 us
    ppermute x4, starting transfers between devices, sideways(): return lax.ppermute(value, ('stream', axis), pairs)  10 us
    ppermute x4, waiting for transfers between devices, sideways(): return lax.ppermute(value, ('stream', axis), pairs)  4.2 us
    all_gather x1, blocking collectives, on_device(): offsets = lax.all_gather(offset, 'stream', axis_index_groups=chips)  2.13 us
    ppermute x4, waiting for transfers between devices, between(): return lax.ppermute(value, 'stream', moves)  1.85 us
    pallas_call x1, Pallas kernels, on_device(): pl.pallas_call(update_kernel, in_specs=[inner] * 3, out_specs=outer, out_...  1.72 us
  transfers between devices with their start and end apart: 9, of which 5 were waited for; matrix products, arithmetic and copies ran while one was open for 0% of the time, Pallas kernels for 5%

profile of v6, /device:TPU:30, one launch (start us, length us, event | category | flops | bytes accessed | tf_op | source)
XLA Modules:
  0.0 68.3 jit_solution(7385664528310527332)
XLA Ops:
  0.0 1.2 %copy-done.4 = bf16[1,1,1,625,768]{4,3,2,1,0:T(8,128)(2,1)S(1)} copy-done((bf16[1,1,1,625,768]{4,3,2,1,0:T(8,128)(2,1)S(1)}, bf16[1,1,1,625,768]{4,3,2,1,0:T(8,128)(2,1)}, u32[]{:S(2)}) %copy-start.4) | copy-done | bytes 960024
  1.2 0.9 %face_traces.1 = (bf16[128,768]{1,0:T(8,128)(2,1)S(1)}, bf16[128,768]{1,0:T(8,128)(2,1)S(1)}, bf16[128,768]{1,0:T(8,128)(2,1)S(1)}, bf16[128,768]{1,0:T(8,128)(2,1)S(1)}, bf16[128,768]{1,0:T(8,128)(2,1)S(1)}) custom-call(s32[1]{0:T(128)} %bitcast.core, bf16[625,768]{1,0:T(8,128)(2,1)S(1)} %bitcast.17), custom_call_target="tpu_custom_call" | custom-call | flops 8000000000 | bytes 960000 | tf_op jit(solution)/shard_map/face_traces/pallas_call | solution.py:227
  2.2 1.4 %collective-permute-start = (bf16[128,768]{1,0:T(8,128)(2,1)S(1)}, bf16[128,768]{1,0:T(8,128)(2,1)S(1)}, u32[]{:S(2)}, u32[]{:S(2)}) collective-permute-start(bf16[128,768]{1,0:T(8,128)(2,1)S(1)} %get-tuple-element.23), channel_id=1, source_target_pairs={{0,4},{4,8},{8,12},{20,16},{24,20},{28,24},{32,36},{36,40},{40,44}... | collective-permute-start | bytes 589832 | tf_op jit(solution)/shard_map/ppermute | solution.py:249
  3.6 2.7 %collective-permute-start.1 = (bf16[128,768]{1,0:T(8,128)(2,1)S(1)}, bf16[128,768]{1,0:T(8,128)(2,1)S(1)}, u32[]{:S(2)}, u32[]{:S(2)}) collective-permute-start(bf16[128,768]{1,0:T(8,128)(2,1)S(1)} %get-tuple-element.24), channel_id=1, source_target_pairs={{1,0},{2,1},{3,2},{16,17},{17,18},{18,19},{33,32},{34,33},{35,34},... | collective-permute-start | bytes 589832 | tf_op jit(solution)/shard_map/ppermute | solution.py:249
  6.3 1.3 %collective-permute-start.2 = (bf16[128,768]{1,0:T(8,128)(2,1)S(1)}, bf16[128,768]{1,0:T(8,128)(2,1)S(1)}, u32[]{:S(2)}, u32[]{:S(2)}) collective-permute-start(bf16[128,768]{1,0:T(8,128)(2,1)S(1)} %get-tuple-element.25), channel_id=1, source_target_pairs={{16,0},{32,16},{48,32},{64,48},{80,64},{96,80},{112,96},{128,112},... | collective-permute-start | bytes 589832 | tf_op jit(solution)/shard_map/ppermute | solution.py:239
  7.6 4.6 %collective-permute-start.3 = (bf16[128,768]{1,0:T(8,128)(2,1)S(1)}, bf16[128,768]{1,0:T(8,128)(2,1)S(1)}, u32[]{:S(2)}, u32[]{:S(2)}) collective-permute-start(bf16[128,768]{1,0:T(8,128)(2,1)S(1)} %get-tuple-element.26), channel_id=1, source_target_pairs={{4,0},{8,4},{12,8},{16,20},{20,24},{24,28},{36,32},{40,36},{44,40}... | collective-permute-start | bytes 589832 | tf_op jit(solution)/shard_map/ppermute | solution.py:249
  12.2 1.3 %collective-permute-start.4 = (bf16[128,768]{1,0:T(8,128)(2,1)S(1)}, bf16[128,768]{1,0:T(8,128)(2,1)S(1)}, u32[]{:S(2)}, u32[]{:S(2)}) collective-permute-start(bf16[128,768]{1,0:T(8,128)(2,1)S(1)} %get-tuple-element.27), channel_id=1, source_target_pairs={{0,1},{1,2},{2,3},{17,16},{18,17},{19,18},{32,33},{33,34},{34,35},... | collective-permute-start | bytes 589832 | tf_op jit(solution)/shard_map/ppermute | solution.py:249
  13.5 1.3 %element_maps.1 = (bf16[625,640]{1,0:T(8,128)(2,1)S(1)}, bf16[625,1024]{1,0:T(8,128)(2,1)S(1)}, bf16[128,625]{1,0:T(8,128)(2,1)S(1)}, s16[128,128]{1,0:T(8,128)(2,1)S(1)}) custom-call(s32[1]{0:T(128)} %bitcast.core, bf16[625,625]{1,0:T(8,128)(2,1)S(1)} %bitcast.14, bf16[6,625,125]{2,1,0:T(8,128)(2,1)S(1)} %bitcast.12, s32[6,1,125]{2,1,0:T(1,128)S(1)} %bitcast.16), custom_call_target="tpu_custom_call" | custom-call | tf_op jit(solution)/shard_map/element_maps/pallas_call | solution.py:255
  15.4 0.7 %partial_residual.1.partial = f32[625,768]{1,0:T(8,128)S(1)} custom-call(bf16[625,768]{1,0:T(8,128)(2,1)S(1)} %bitcast.13, bf16[625,640]{1,0:T(8,128)(2,1)S(1)} %get-tuple-element.22.couple, bf16[128,768]{1,0:T(8,128)(2,1)S(1)} %collective-permute-done.t1, bf16[128,768]{1,0:T(8,128)(2,1)S(1)} %collective-permute-done.1.t2, ...), custom_call_target="tpu_custom_call" | custom-call | flops 491520000 | bytes 2880000 | tf_op jit(solution)/shard_map/partial_residual/pallas_call | solution.py:268
  16.1 3.7 %collective-permute-done.4.t5 = bf16[128,768]{1,0:T(8,128)(2,1)S(1)} collective-permute-done((bf16[128,768]{1,0:T(8,128)(2,1)S(1)}, bf16[128,768]{1,0:T(8,128)(2,1)S(1)}, u32[]{:S(2)}, u32[]{:S(2)}) %collective-permute-start.4) | collective-permute-done | bytes 196640 | tf_op jit(solution)/shard_map/ppermute | solution.py:249
  19.8 0.9 %residual_offset.1 = (bf16[640,768]{1,0:T(8,128)(2,1)S(1)}, s16[896,128]{1,0:T(8,128)(2,1)S(1)}) custom-call(f32[625,768]{1,0:T(8,128)S(1)} %partial_residual.1.partial, bf16[625,640]{1,0:T(8,128)(2,1)S(1)} %get-tuple-element.22.couple, bf16[128,768]{1,0:T(8,128)(2,1)S(1)} %collective-permute-done.4.t5, bf16[128,625]{1,0:T(8,128)(2,1)S(1)} %get-tuple-element.28.inverse, ...), custom_call_target="tpu_custom_call" | custom-call | tf_op jit(solution)/shard_map/residual_offset/pallas_call | solution.py:277
  20.6 2.1 %all-gather = s16[1792,128]{1,0:T(8,128)(2,1)S(1)} all-gather(s16[896,128]{1,0:T(8,128)(2,1)S(1)} %get-tuple-element.31), channel_id=2, replica_groups={{0,16},{32,48},{64,80},{96,112},{128,144},{160,176},{192,208},{224,240}..., dimensions={0}, use_global_device_ids=true | all-gather | bytes 688128 | tf_op jit(solution)/shard_map/all_gather | solution.py:286
  23.3 15.4 %all_to_all.10.received = s16[8,112,128]{2,1,0:T(8,128)(2,1)S(1)} all-to-all(s16[8,112,128]{2,1,0:T(8,128)(2,1)S(1)} %chip_merge.1), channel_id=1, replica_groups={{0,16,32,48,64,80,96,112},{128,144,160,176,192,208,224,240},{256,272,28..., dimensions={0} | all-to-all | bytes 458752 | tf_op jit(solution)/shard_map/all_to_all | solution.py:294
  38.6 0.7 group_scan.1
  39.3 1.3 %collective-permute-start.6 = (s16[224,128]{1,0:T(8,128)(2,1)S(1)}, s16[224,128]{1,0:T(8,128)(2,1)S(1)}, u32[]{:S(2)}, u32[]{:S(2)}) collective-permute-start(s16[224,128]{1,0:T(8,128)(2,1)S(1)} %get-tuple-element.35.own), channel_id=1, source_target_pairs={{128,0},{144,16},{160,32},{176,48},{192,64},{208,80},{224,96},{240... | collective-permute-start | bytes 172040 | tf_op jit(solution)/shard_map/ppermute | solution.py:308
  40.6 9.1 %collective-permute-start.5 = (s16[96,128]{1,0:T(8,128)(2,1)S(1)}, s16[96,128]{1,0:T(8,128)(2,1)S(1)}, u32[]{:S(2)}, u32[]{:S(2)}) collective-permute-start(s16[96,128]{1,0:T(8,128)(2,1)S(1)} %get-tuple-element.34), channel_id=1, source_target_pairs={{0,128},{16,144},{32,160},{48,176},{64,192},{80,208},{96,224},{112... | collective-permute-start | bytes 73736 | tf_op jit(solution)/shard_map/ppermute | solution.py:308
  49.7 0.7 collective-permute-start.8
  50.4 0.8 %collective-permute-done.5.below.first = s16[96,128]{1,0:T(8,128)(2,1)S(1)} collective-permute-done((s16[96,128]{1,0:T(8,128)(2,1)S(1)}, s16[96,128]{1,0:T(8,128)(2,1)S(1)}, u32[]{:S(2)}, u32[]{:S(2)}) %collective-permute-start.5) | collective-permute-done | bytes 24608 | tf_op jit(solution)/shard_map/ppermute | solution.py:308
  51.2 0.9 %collective-permute-done.6.above = s16[224,128]{1,0:T(8,128)(2,1)S(1)} collective-permute-done((s16[224,128]{1,0:T(8,128)(2,1)S(1)}, s16[224,128]{1,0:T(8,128)(2,1)S(1)}, u32[]{:S(2)}, u32[]{:S(2)}) %collective-permute-start.6) | collective-permute-done | bytes 57376 | tf_op jit(solution)/shard_map/ppermute | solution.py:308
  52.5 1.3 %collective-permute-start.7 = (s16[96,128]{1,0:T(8,128)(2,1)S(1)}, s16[96,128]{1,0:T(8,128)(2,1)S(1)}, u32[]{:S(2)}, u32[]{:S(2)}) collective-permute-start(s16[96,128]{1,0:T(8,128)(2,1)S(1)} %pair_total.1), channel_id=1, source_target_pairs={{128,256},{144,272},{160,288},{176,304},{192,320},{208,336},{224,3... | collective-permute-start | bytes 73736 | tf_op jit(solution)/shard_map/ppermute | solution.py:308
  53.8 1.4 %solve.1 = (f32[625,768]{1,0:T(8,128)S(1)}, bf16[625,384]{1,0:T(8,128)(2,1)S(1)}) custom-call(s32[1]{0:T(128)} %bitcast.core, bf16[625,1024]{1,0:T(8,128)(2,1)S(1)} %get-tuple-element.21.left, bf16[640,768]{1,0:T(8,128)(2,1)S(1)} %get-tuple-element.30.residual, s16[2,896,128]{2,1,0:T(8,128)(2,1)S(1)} %bitcast.11), custom_call_target="tpu_custom_call" | custom-call | flops 983040000 | bytes 1920000 | tf_op jit(solution)/shard_map/solve/pallas_call | solution.py:313
  55.3 0.5 group_prefix.1
  55.8 10.7 %all_to_all.11 = s16[8,96,128]{2,1,0:T(8,128)(2,1)S(1)} all-to-all(s16[8,96,128]{2,1,0:T(8,128)(2,1)S(1)} %group_prefix.1), channel_id=1, replica_groups={{0,16,32,48,64,80,96,112},{128,144,160,176,192,208,224,240},{256,272,28..., dimensions={0} | all-to-all | bytes 393216 | tf_op jit(solution)/shard_map/all_to_all | solution.py:341
  66.5 1.7 %update.1 = bf16[625,768]{1,0:T(8,128)(2,1)} custom-call(f32[625,768]{1,0:T(8,128)S(1)} %get-tuple-element.32.solved, bf16[625,384]{1,0:T(8,128)(2,1)S(1)} %get-tuple-element.33.gain, s16[768,128]{1,0:T(8,128)(2,1)S(1)} %bitcast.15), custom_call_target="tpu_custom_call" | custom-call | tf_op jit(solution)/shard_map/update/pallas_call | solution.py:343
  (17 shorter events, 1.5 us)
Async XLA Ops:
  0.0 1.2 %copy-start.4 = (bf16[1,1,1,625,768]{4,3,2,1,0:T(8,128)(2,1)S(1)}, bf16[1,1,1,625,768]{4,3,2,1,0:T(8,128)(2,1)}, u32[]{:S(2)}) copy-start(bf16[1,1,1,625,768]{4,3,2,1,0:T(8,128)(2,1)} %param.8) | copy-start | bytes 2880004
  1.2 12.3 %copy-start = (bf16[1,1,1,6,625,125]{5,4,3,2,1,0:T(8,128)(2,1)S(1)}, bf16[1,1,1,6,625,125]{5,4,3,2,1,0:T(8,128)(2,1)}, u32[]{:S(2)}) copy-start(bf16[1,1,1,6,625,125]{5,4,3,2,1,0:T(8,128)(2,1)} %param.7) | copy-start | bytes 2812504
  1.2 12.3 %copy-start.2 = (bf16[1,1,1,625,625]{4,3,2,1,0:T(8,128)(2,1)S(1)}, bf16[1,1,1,625,625]{4,3,2,1,0:T(8,128)(2,1)}, u32[]{:S(2)}) copy-start(bf16[1,1,1,625,625]{4,3,2,1,0:T(8,128)(2,1)} %param.6) | copy-start | bytes 2343754
  1.2 12.3 %copy-start.3 = (s32[1,1,1,6,125]{4,2,3,1,0:T(1,128)S(1)}, s32[1,1,1,6,125]{4,2,3,1,0:T(1,128)}, u32[]{:S(2)}) copy-start(s32[1,1,1,6,125]{4,2,3,1,0:T(1,128)} %param.9) | copy-start | bytes 9004
  2.2 13.2 %copy-start.1 = (bf16[1,1,1,625,768]{4,3,2,1,0:T(8,128)(2,1)S(1)}, bf16[1,1,1,625,768]{4,3,2,1,0:T(8,128)(2,1)}, u32[]{:S(2)}) copy-start(bf16[1,1,1,625,768]{4,3,2,1,0:T(8,128)(2,1)} %param.5) | copy-start | bytes 2880004
  2.2 12.7 %collective-permute-start = (bf16[128,768]{1,0:T(8,128)(2,1)S(1)}, bf16[128,768]{1,0:T(8,128)(2,1)S(1)}, u32[]{:S(2)}, u32[]{:S(2)}) collective-permute-start(bf16[128,768]{1,0:T(8,128)(2,1)S(1)} %get-tuple-element.23), channel_id=1, source_target_pairs={{0,4},{4,8},{8,12},{20,16},{24,20},{28,24},{32,36},{36,40},{40,44}... | collective-permute-start | bytes 589832 | tf_op jit(solution)/shard_map/ppermute | solution.py:249
  3.6 11.3 %collective-permute-start.1 = (bf16[128,768]{1,0:T(8,128)(2,1)S(1)}, bf16[128,768]{1,0:T(8,128)(2,1)S(1)}, u32[]{:S(2)}, u32[]{:S(2)}) collective-permute-start(bf16[128,768]{1,0:T(8,128)(2,1)S(1)} %get-tuple-element.24), channel_id=1, source_target_pairs={{1,0},{2,1},{3,2},{16,17},{17,18},{18,19},{33,32},{34,33},{35,34},... | collective-permute-start | bytes 589832 | tf_op jit(solution)/shard_map/ppermute | solution.py:249
  6.3 8.5 %collective-permute-start.2 = (bf16[128,768]{1,0:T(8,128)(2,1)S(1)}, bf16[128,768]{1,0:T(8,128)(2,1)S(1)}, u32[]{:S(2)}, u32[]{:S(2)}) collective-permute-start(bf16[128,768]{1,0:T(8,128)(2,1)S(1)} %get-tuple-element.25), channel_id=1, source_target_pairs={{16,0},{32,16},{48,32},{64,48},{80,64},{96,80},{112,96},{128,112},... | collective-permute-start | bytes 589832 | tf_op jit(solution)/shard_map/ppermute | solution.py:239
  7.6 7.7 %collective-permute-start.3 = (bf16[128,768]{1,0:T(8,128)(2,1)S(1)}, bf16[128,768]{1,0:T(8,128)(2,1)S(1)}, u32[]{:S(2)}, u32[]{:S(2)}) collective-permute-start(bf16[128,768]{1,0:T(8,128)(2,1)S(1)} %get-tuple-element.26), channel_id=1, source_target_pairs={{4,0},{8,4},{12,8},{16,20},{20,24},{24,28},{36,32},{40,36},{44,40}... | collective-permute-start | bytes 589832 | tf_op jit(solution)/shard_map/ppermute | solution.py:249
  12.2 7.6 %collective-permute-start.4 = (bf16[128,768]{1,0:T(8,128)(2,1)S(1)}, bf16[128,768]{1,0:T(8,128)(2,1)S(1)}, u32[]{:S(2)}, u32[]{:S(2)}) collective-permute-start(bf16[128,768]{1,0:T(8,128)(2,1)S(1)} %get-tuple-element.27), channel_id=1, source_target_pairs={{0,1},{1,2},{2,3},{17,16},{18,17},{19,18},{32,33},{33,34},{34,35},... | collective-permute-start | bytes 589832 | tf_op jit(solution)/shard_map/ppermute | solution.py:249
  39.3 12.8 %collective-permute-start.6 = (s16[224,128]{1,0:T(8,128)(2,1)S(1)}, s16[224,128]{1,0:T(8,128)(2,1)S(1)}, u32[]{:S(2)}, u32[]{:S(2)}) collective-permute-start(s16[224,128]{1,0:T(8,128)(2,1)S(1)} %get-tuple-element.35.own), channel_id=1, source_target_pairs={{128,0},{144,16},{160,32},{176,48},{192,64},{208,80},{224,96},{240... | collective-permute-start | bytes 172040 | tf_op jit(solution)/shard_map/ppermute | solution.py:308
  40.6 10.6 %collective-permute-start.5 = (s16[96,128]{1,0:T(8,128)(2,1)S(1)}, s16[96,128]{1,0:T(8,128)(2,1)S(1)}, u32[]{:S(2)}, u32[]{:S(2)}) collective-permute-start(s16[96,128]{1,0:T(8,128)(2,1)S(1)} %get-tuple-element.34), channel_id=1, source_target_pairs={{0,128},{16,144},{32,160},{48,176},{64,192},{80,208},{96,224},{112... | collective-permute-start | bytes 73736 | tf_op jit(solution)/shard_map/ppermute | solution.py:308
  49.7 5.5 %collective-permute-start.8 = (s16[224,128]{1,0:T(8,128)(2,1)S(1)}, s16[224,128]{1,0:T(8,128)(2,1)S(1)}, u32[]{:S(2)}, u32[]{:S(2)}) collective-permute-start(s16[224,128]{1,0:T(8,128)(2,1)S(1)} %get-tuple-element.35.own), channel_id=1, source_target_pairs={{256,384},{272,400},{288,416},{304,432},{320,448},{336,464},{352,4... | collective-permute-start | bytes 172040 | tf_op jit(solution)/shard_map/ppermute | solution.py:308
  52.5 2.8 %collective-permute-start.7 = (s16[96,128]{1,0:T(8,128)(2,1)S(1)}, s16[96,128]{1,0:T(8,128)(2,1)S(1)}, u32[]{:S(2)}, u32[]{:S(2)}) collective-permute-start(s16[96,128]{1,0:T(8,128)(2,1)S(1)} %pair_total.1), channel_id=1, source_target_pairs={{128,256},{144,272},{160,288},{176,304},{192,320},{208,336},{224,3... | collective-permute-start | bytes 73736 | tf_op jit(solution)/shard_map/ppermute | solution.py:308

commit v7 on v6

--- a/solution.py
+++ b/solution.py
@@ -88,7 +88,7 @@
         return dot(coupling[face], pick, (1, 1)).astype(bf16)
 
     turn = core[0]
-    for at, face in enumerate((2 + turn, 5 - turn, 1, 3 - turn, 4 + turn)):
+    for at, face in enumerate((1, 2 + turn, 5 - turn, 3 - turn, 4 + turn)):
         couple_out[:, at * WIDE : (at + 1) * WIDE] = permuted(face)
     first = permuted(0)
     left_out[...] = jnp.zeros(left_out.shape, bf16)
@@ -273,7 +273,7 @@
         ),
         compiler_params=params(),
         name="partial_residual",
-    )(right_side, couple, *(halos[at] for at in (1, 2, 0, 3)))
+    )(right_side, couple, *(halos[at] for at in (0, 1, 2, 3)))
     residual, offset = pl.pallas_call(
         offset_kernel,
         out_shape=[

time: 68.7 us -> 68.6 us (level)
  the two profiles are of different devices: /device:TPU:30 before, /device:TPU:14 now
where the time goes in v7:
time: 68.6 us; the launch traced here: 68.3 us
  blocking collectives  28.2 us (41%)
  starting transfers between devices  23.7 us (35%)
  Pallas kernels  8.9 us (13%)
  waiting for transfers between devices  6.04 us (9%)
  local copies, waits for them, and re-layouts  1.21 us (2%)
    all_to_all x1, blocking collectives, on_device(): lax.all_to_all(sent, 'stream', 0, 0, tiled=True, axis_index_groups=near)  15.4 us
    ppermute x4, starting transfers between devices, between(): return lax.ppermute(value, 'stream', moves)  12.3 us
    all_to_all x1, blocking collectives, on_device(): lax.all_to_all(entering, 'stream', 0, 0, tiled=True, axis_index_groups=near)  10.7 us
    ppermute x4, starting transfers between devices, sideways(): return lax.ppermute(value, ('stream', axis), pairs)  9.89 us
    ppermute x4, waiting for transfers between devices, sideways(): return lax.ppermute(value, ('stream', axis), pairs)  4.2 us
    all_gather x1, blocking collectives, on_device(): offsets = lax.all_gather(offset, 'stream', axis_index_groups=chips)  2.13 us
    ppermute x4, waiting for transfers between devices, between(): return lax.ppermute(value, 'stream', moves)  1.84 us
    pallas_call x1, Pallas kernels, on_device(): pl.pallas_call(update_kernel, in_specs=[inner] * 3, out_specs=outer, out_...  1.72 us
  transfers between devices with their start and end apart: 9, of which 5 were waited for; matrix products, arithmetic and copies ran while one was open for 0% of the time, Pallas kernels for 5%

profile of v7, /device:TPU:14, one launch (start us, length us, event | category | flops | bytes accessed | tf_op | source)
XLA Modules:
  0.0 68.3 jit_solution(2393381619161541513)
XLA Ops:
  0.0 1.2 %copy-done.4 = bf16[1,1,1,625,768]{4,3,2,1,0:T(8,128)(2,1)S(1)} copy-done((bf16[1,1,1,625,768]{4,3,2,1,0:T(8,128)(2,1)S(1)}, bf16[1,1,1,625,768]{4,3,2,1,0:T(8,128)(2,1)}, u32[]{:S(2)}) %copy-start.4) | copy-done | bytes 960024
  1.2 0.9 %face_traces.1 = (bf16[128,768]{1,0:T(8,128)(2,1)S(1)}, bf16[128,768]{1,0:T(8,128)(2,1)S(1)}, bf16[128,768]{1,0:T(8,128)(2,1)S(1)}, bf16[128,768]{1,0:T(8,128)(2,1)S(1)}, bf16[128,768]{1,0:T(8,128)(2,1)S(1)}) custom-call(s32[1]{0:T(128)} %bitcast.core, bf16[625,768]{1,0:T(8,128)(2,1)S(1)} %bitcast.17), custom_call_target="tpu_custom_call" | custom-call | flops 8000000000 | bytes 960000 | tf_op jit(solution)/shard_map/face_traces/pallas_call | solution.py:227
  2.2 1.4 %collective-permute-start = (bf16[128,768]{1,0:T(8,128)(2,1)S(1)}, bf16[128,768]{1,0:T(8,128)(2,1)S(1)}, u32[]{:S(2)}, u32[]{:S(2)}) collective-permute-start(bf16[128,768]{1,0:T(8,128)(2,1)S(1)} %get-tuple-element.23), channel_id=1, source_target_pairs={{16,0},{32,16},{48,32},{64,48},{80,64},{96,80},{112,96},{128,112},... | collective-permute-start | bytes 589832 | tf_op jit(solution)/shard_map/ppermute | solution.py:239
  3.6 3.5 %collective-permute-start.1 = (bf16[128,768]{1,0:T(8,128)(2,1)S(1)}, bf16[128,768]{1,0:T(8,128)(2,1)S(1)}, u32[]{:S(2)}, u32[]{:S(2)}) collective-permute-start(bf16[128,768]{1,0:T(8,128)(2,1)S(1)} %get-tuple-element.24), channel_id=1, source_target_pairs={{0,4},{4,8},{8,12},{20,16},{24,20},{28,24},{32,36},{36,40},{40,44}... | collective-permute-start | bytes 589832 | tf_op jit(solution)/shard_map/ppermute | solution.py:249
  7.1 2.7 %collective-permute-start.2 = (bf16[128,768]{1,0:T(8,128)(2,1)S(1)}, bf16[128,768]{1,0:T(8,128)(2,1)S(1)}, u32[]{:S(2)}, u32[]{:S(2)}) collective-permute-start(bf16[128,768]{1,0:T(8,128)(2,1)S(1)} %get-tuple-element.25), channel_id=1, source_target_pairs={{1,0},{2,1},{3,2},{16,17},{17,18},{18,19},{33,32},{34,33},{35,34},... | collective-permute-start | bytes 589832 | tf_op jit(solution)/shard_map/ppermute | solution.py:249
  9.8 2.4 %collective-permute-start.3 = (bf16[128,768]{1,0:T(8,128)(2,1)S(1)}, bf16[128,768]{1,0:T(8,128)(2,1)S(1)}, u32[]{:S(2)}, u32[]{:S(2)}) collective-permute-start(bf16[128,768]{1,0:T(8,128)(2,1)S(1)} %get-tuple-element.26), channel_id=1, source_target_pairs={{4,0},{8,4},{12,8},{16,20},{20,24},{24,28},{36,32},{40,36},{44,40}... | collective-permute-start | bytes 589832 | tf_op jit(solution)/shard_map/ppermute | solution.py:249
  12.2 1.3 %collective-permute-start.4 = (bf16[128,768]{1,0:T(8,128)(2,1)S(1)}, bf16[128,768]{1,0:T(8,128)(2,1)S(1)}, u32[]{:S(2)}, u32[]{:S(2)}) collective-permute-start(bf16[128,768]{1,0:T(8,128)(2,1)S(1)} %get-tuple-element.27), channel_id=1, source_target_pairs={{0,1},{1,2},{2,3},{17,16},{18,17},{19,18},{32,33},{33,34},{34,35},... | collective-permute-start | bytes 589832 | tf_op jit(solution)/shard_map/ppermute | solution.py:249
  13.5 1.3 %element_maps.1 = (bf16[625,640]{1,0:T(8,128)(2,1)S(1)}, bf16[625,1024]{1,0:T(8,128)(2,1)S(1)}, bf16[128,625]{1,0:T(8,128)(2,1)S(1)}, s16[128,128]{1,0:T(8,128)(2,1)S(1)}) custom-call(s32[1]{0:T(128)} %bitcast.core, bf16[625,625]{1,0:T(8,128)(2,1)S(1)} %bitcast.14, bf16[6,625,125]{2,1,0:T(8,128)(2,1)S(1)} %bitcast.12, s32[6,1,125]{2,1,0:T(1,128)S(1)} %bitcast.16), custom_call_target="tpu_custom_call" | custom-call | tf_op jit(solution)/shard_map/element_maps/pallas_call | solution.py:255
  14.9 2.5 %collective-permute-done.3.t4 = bf16[128,768]{1,0:T(8,128)(2,1)S(1)} collective-permute-done((bf16[128,768]{1,0:T(8,128)(2,1)S(1)}, bf16[128,768]{1,0:T(8,128)(2,1)S(1)}, u32[]{:S(2)}, u32[]{:S(2)}) %collective-permute-start.3) | collective-permute-done | bytes 196640 | tf_op jit(solution)/shard_map/ppermute | solution.py:249
  17.4 0.7 %partial_residual.1.partial = f32[625,768]{1,0:T(8,128)S(1)} custom-call(bf16[625,768]{1,0:T(8,128)(2,1)S(1)} %bitcast.13, bf16[625,640]{1,0:T(8,128)(2,1)S(1)} %get-tuple-element.22.couple, bf16[128,768]{1,0:T(8,128)(2,1)S(1)} %collective-permute-done.t1, bf16[128,768]{1,0:T(8,128)(2,1)S(1)} %collective-permute-done.1.t2, ...), custom_call_target="tpu_custom_call" | custom-call | flops 491520000 | bytes 2880000 | tf_op jit(solution)/shard_map/partial_residual/pallas_call | solution.py:268
  18.1 1.7 %collective-permute-done.4.t5 = bf16[128,768]{1,0:T(8,128)(2,1)S(1)} collective-permute-done((bf16[128,768]{1,0:T(8,128)(2,1)S(1)}, bf16[128,768]{1,0:T(8,128)(2,1)S(1)}, u32[]{:S(2)}, u32[]{:S(2)}) %collective-permute-start.4) | collective-permute-done | bytes 196640 | tf_op jit(solution)/shard_map/ppermute | solution.py:249
  19.8 0.9 %residual_offset.1 = (bf16[640,768]{1,0:T(8,128)(2,1)S(1)}, s16[896,128]{1,0:T(8,128)(2,1)S(1)}) custom-call(f32[625,768]{1,0:T(8,128)S(1)} %partial_residual.1.partial, bf16[625,640]{1,0:T(8,128)(2,1)S(1)} %get-tuple-element.22.couple, bf16[128,768]{1,0:T(8,128)(2,1)S(1)} %collective-permute-done.4.t5, bf16[128,625]{1,0:T(8,128)(2,1)S(1)} %get-tuple-element.28.inverse, ...), custom_call_target="tpu_custom_call" | custom-call | tf_op jit(solution)/shard_map/residual_offset/pallas_call | solution.py:277
  20.6 2.1 %all-gather = s16[1792,128]{1,0:T(8,128)(2,1)S(1)} all-gather(s16[896,128]{1,0:T(8,128)(2,1)S(1)} %get-tuple-element.31), channel_id=2, replica_groups={{0,16},{32,48},{64,80},{96,112},{128,144},{160,176},{192,208},{224,240}..., dimensions={0}, use_global_device_ids=true | all-gather | bytes 688128 | tf_op jit(solution)/shard_map/all_gather | solution.py:286
  23.3 15.4 %all_to_all.10.received = s16[8,112,128]{2,1,0:T(8,128)(2,1)S(1)} all-to-all(s16[8,112,128]{2,1,0:T(8,128)(2,1)S(1)} %chip_merge.1), channel_id=1, replica_groups={{0,16,32,48,64,80,96,112},{128,144,160,176,192,208,224,240},{256,272,28..., dimensions={0} | all-to-all | bytes 458752 | tf_op jit(solution)/shard_map/all_to_all | solution.py:294
  38.6 0.7 group_scan.1
  39.3 1.3 %collective-permute-start.6 = (s16[224,128]{1,0:T(8,128)(2,1)S(1)}, s16[224,128]{1,0:T(8,128)(2,1)S(1)}, u32[]{:S(2)}, u32[]{:S(2)}) collective-permute-start(s16[224,128]{1,0:T(8,128)(2,1)S(1)} %get-tuple-element.35.own), channel_id=1, source_target_pairs={{128,0},{144,16},{160,32},{176,48},{192,64},{208,80},{224,96},{240... | collective-permute-start | bytes 172040 | tf_op jit(solution)/shard_map/ppermute | solution.py:308
  40.6 9.1 %collective-permute-start.5 = (s16[96,128]{1,0:T(8,128)(2,1)S(1)}, s16[96,128]{1,0:T(8,128)(2,1)S(1)}, u32[]{:S(2)}, u32[]{:S(2)}) collective-permute-start(s16[96,128]{1,0:T(8,128)(2,1)S(1)} %get-tuple-element.34), channel_id=1, source_target_pairs={{0,128},{16,144},{32,160},{48,176},{64,192},{80,208},{96,224},{112... | collective-permute-start | bytes 73736 | tf_op jit(solution)/shard_map/ppermute | solution.py:308
  49.7 0.7 collective-permute-start.8
  50.4 0.8 %collective-permute-done.5.below.first = s16[96,128]{1,0:T(8,128)(2,1)S(1)} collective-permute-done((s16[96,128]{1,0:T(8,128)(2,1)S(1)}, s16[96,128]{1,0:T(8,128)(2,1)S(1)}, u32[]{:S(2)}, u32[]{:S(2)}) %collective-permute-start.5) | collective-permute-done | bytes 24608 | tf_op jit(solution)/shard_map/ppermute | solution.py:308
  51.2 0.9 %collective-permute-done.6.above = s16[224,128]{1,0:T(8,128)(2,1)S(1)} collective-permute-done((s16[224,128]{1,0:T(8,128)(2,1)S(1)}, s16[224,128]{1,0:T(8,128)(2,1)S(1)}, u32[]{:S(2)}, u32[]{:S(2)}) %collective-permute-start.6) | collective-permute-done | bytes 57376 | tf_op jit(solution)/shard_map/ppermute | solution.py:308
  52.5 1.3 %collective-permute-start.7 = (s16[96,128]{1,0:T(8,128)(2,1)S(1)}, s16[96,128]{1,0:T(8,128)(2,1)S(1)}, u32[]{:S(2)}, u32[]{:S(2)}) collective-permute-start(s16[96,128]{1,0:T(8,128)(2,1)S(1)} %pair_total.1), channel_id=1, source_target_pairs={{128,256},{144,272},{160,288},{176,304},{192,320},{208,336},{224,3... | collective-permute-start | bytes 73736 | tf_op jit(solution)/shard_map/ppermute | solution.py:308
  53.8 1.4 %solve.1 = (f32[625,768]{1,0:T(8,128)S(1)}, bf16[625,384]{1,0:T(8,128)(2,1)S(1)}) custom-call(s32[1]{0:T(128)} %bitcast.core, bf16[625,1024]{1,0:T(8,128)(2,1)S(1)} %get-tuple-element.21.left, bf16[640,768]{1,0:T(8,128)(2,1)S(1)} %get-tuple-element.30.residual, s16[2,896,128]{2,1,0:T(8,128)(2,1)S(1)} %bitcast.11), custom_call_target="tpu_custom_call" | custom-call | flops 983040000 | bytes 1920000 | tf_op jit(solution)/shard_map/solve/pallas_call | solution.py:313
  55.8 10.7 %all_to_all.11 = s16[8,96,128]{2,1,0:T(8,128)(2,1)S(1)} all-to-all(s16[8,96,128]{2,1,0:T(8,128)(2,1)S(1)} %group_prefix.1), channel_id=1, replica_groups={{0,16,32,48,64,80,96,112},{128,144,160,176,192,208,224,240},{256,272,28..., dimensions={0} | all-to-all | bytes 393216 | tf_op jit(solution)/shard_map/all_to_all | solution.py:341
  66.5 1.7 %update.1 = bf16[625,768]{1,0:T(8,128)(2,1)} custom-call(f32[625,768]{1,0:T(8,128)S(1)} %get-tuple-element.32.solved, bf16[625,384]{1,0:T(8,128)(2,1)S(1)} %get-tuple-element.33.gain, s16[768,128]{1,0:T(8,128)(2,1)S(1)} %bitcast.15), custom_call_target="tpu_custom_call" | custom-call | tf_op jit(solution)/shard_map/update/pallas_call | solution.py:343
  (17 shorter events, 1.5 us)
Async XLA Ops:
  0.0 1.2 %copy-start.4 = (bf16[1,1,1,625,768]{4,3,2,1,0:T(8,128)(2,1)S(1)}, bf16[1,1,1,625,768]{4,3,2,1,0:T(8,128)(2,1)}, u32[]{:S(2)}) copy-start(bf16[1,1,1,625,768]{4,3,2,1,0:T(8,128)(2,1)} %param.8) | copy-start | bytes 2880004
  1.2 12.3 %copy-start = (bf16[1,1,1,6,625,125]{5,4,3,2,1,0:T(8,128)(2,1)S(1)}, bf16[1,1,1,6,625,125]{5,4,3,2,1,0:T(8,128)(2,1)}, u32[]{:S(2)}) copy-start(bf16[1,1,1,6,625,125]{5,4,3,2,1,0:T(8,128)(2,1)} %param.7) | copy-start | bytes 2812504
  1.2 12.3 %copy-start.2 = (bf16[1,1,1,625,625]{4,3,2,1,0:T(8,128)(2,1)S(1)}, bf16[1,1,1,625,625]{4,3,2,1,0:T(8,128)(2,1)}, u32[]{:S(2)}) copy-start(bf16[1,1,1,625,625]{4,3,2,1,0:T(8,128)(2,1)} %param.6) | copy-start | bytes 2343754
  1.2 12.3 %copy-start.3 = (s32[1,1,1,6,125]{4,2,3,1,0:T(1,128)S(1)}, s32[1,1,1,6,125]{4,2,3,1,0:T(1,128)}, u32[]{:S(2)}) copy-start(s32[1,1,1,6,125]{4,2,3,1,0:T(1,128)} %param.9) | copy-start | bytes 9004
  2.1 15.3 %copy-start.1 = (bf16[1,1,1,625,768]{4,3,2,1,0:T(8,128)(2,1)S(1)}, bf16[1,1,1,625,768]{4,3,2,1,0:T(8,128)(2,1)}, u32[]{:S(2)}) copy-start(bf16[1,1,1,625,768]{4,3,2,1,0:T(8,128)(2,1)} %param.5) | copy-start | bytes 2880004
  2.2 12.7 %collective-permute-start = (bf16[128,768]{1,0:T(8,128)(2,1)S(1)}, bf16[128,768]{1,0:T(8,128)(2,1)S(1)}, u32[]{:S(2)}, u32[]{:S(2)}) collective-permute-start(bf16[128,768]{1,0:T(8,128)(2,1)S(1)} %get-tuple-element.23), channel_id=1, source_target_pairs={{16,0},{32,16},{48,32},{64,48},{80,64},{96,80},{112,96},{128,112},... | collective-permute-start | bytes 589832 | tf_op jit(solution)/shard_map/ppermute | solution.py:239
  3.6 11.3 %collective-permute-start.1 = (bf16[128,768]{1,0:T(8,128)(2,1)S(1)}, bf16[128,768]{1,0:T(8,128)(2,1)S(1)}, u32[]{:S(2)}, u32[]{:S(2)}) collective-permute-start(bf16[128,768]{1,0:T(8,128)(2,1)S(1)} %get-tuple-element.24), channel_id=1, source_target_pairs={{0,4},{4,8},{8,12},{20,16},{24,20},{28,24},{32,36},{36,40},{40,44}... | collective-permute-start | bytes 589832 | tf_op jit(solution)/shard_map/ppermute | solution.py:249
  7.1 7.8 %collective-permute-start.2 = (bf16[128,768]{1,0:T(8,128)(2,1)S(1)}, bf16[128,768]{1,0:T(8,128)(2,1)S(1)}, u32[]{:S(2)}, u32[]{:S(2)}) collective-permute-start(bf16[128,768]{1,0:T(8,128)(2,1)S(1)} %get-tuple-element.25), channel_id=1, source_target_pairs={{1,0},{2,1},{3,2},{16,17},{17,18},{18,19},{33,32},{34,33},{35,34},... | collective-permute-start | bytes 589832 | tf_op jit(solution)/shard_map/ppermute | solution.py:249
  9.8 7.6 %collective-permute-start.3 = (bf16[128,768]{1,0:T(8,128)(2,1)S(1)}, bf16[128,768]{1,0:T(8,128)(2,1)S(1)}, u32[]{:S(2)}, u32[]{:S(2)}) collective-permute-start(bf16[128,768]{1,0:T(8,128)(2,1)S(1)} %get-tuple-element.26), channel_id=1, source_target_pairs={{4,0},{8,4},{12,8},{16,20},{20,24},{24,28},{36,32},{40,36},{44,40}... | collective-permute-start | bytes 589832 | tf_op jit(solution)/shard_map/ppermute | solution.py:249
  12.2 7.6 %collective-permute-start.4 = (bf16[128,768]{1,0:T(8,128)(2,1)S(1)}, bf16[128,768]{1,0:T(8,128)(2,1)S(1)}, u32[]{:S(2)}, u32[]{:S(2)}) collective-permute-start(bf16[128,768]{1,0:T(8,128)(2,1)S(1)} %get-tuple-element.27), channel_id=1, source_target_pairs={{0,1},{1,2},{2,3},{17,16},{18,17},{19,18},{32,33},{33,34},{34,35},... | collective-permute-start | bytes 589832 | tf_op jit(solution)/shard_map/ppermute | solution.py:249
  39.3 12.8 %collective-permute-start.6 = (s16[224,128]{1,0:T(8,128)(2,1)S(1)}, s16[224,128]{1,0:T(8,128)(2,1)S(1)}, u32[]{:S(2)}, u32[]{:S(2)}) collective-permute-start(s16[224,128]{1,0:T(8,128)(2,1)S(1)} %get-tuple-element.35.own), channel_id=1, source_target_pairs={{128,0},{144,16},{160,32},{176,48},{192,64},{208,80},{224,96},{240... | collective-permute-start | bytes 172040 | tf_op jit(solution)/shard_map/ppermute | solution.py:308
  40.6 10.6 %collective-permute-start.5 = (s16[96,128]{1,0:T(8,128)(2,1)S(1)}, s16[96,128]{1,0:T(8,128)(2,1)S(1)}, u32[]{:S(2)}, u32[]{:S(2)}) collective-permute-start(s16[96,128]{1,0:T(8,128)(2,1)S(1)} %get-tuple-element.34), channel_id=1, source_target_pairs={{0,128},{16,144},{32,160},{48,176},{64,192},{80,208},{96,224},{112... | collective-permute-start | bytes 73736 | tf_op jit(solution)/shard_map/ppermute | solution.py:308
  49.7 5.5 %collective-permute-start.8 = (s16[224,128]{1,0:T(8,128)(2,1)S(1)}, s16[224,128]{1,0:T(8,128)(2,1)S(1)}, u32[]{:S(2)}, u32[]{:S(2)}) collective-permute-start(s16[224,128]{1,0:T(8,128)(2,1)S(1)} %get-tuple-element.35.own), channel_id=1, source_target_pairs={{256,384},{272,400},{288,416},{304,432},{320,448},{336,464},{352,4... | collective-permute-start | bytes 172040 | tf_op jit(solution)/shard_map/ppermute | solution.py:308
  52.5 2.8 %collective-permute-start.7 = (s16[96,128]{1,0:T(8,128)(2,1)S(1)}, s16[96,128]{1,0:T(8,128)(2,1)S(1)}, u32[]{:S(2)}, u32[]{:S(2)}) collective-permute-start(s16[96,128]{1,0:T(8,128)(2,1)S(1)} %pair_total.1), channel_id=1, source_target_pairs={{128,256},{144,272},{160,288},{176,304},{192,320},{208,336},{224,3... | collective-permute-start | bytes 73736 | tf_op jit(solution)/shard_map/ppermute | solution.py:308
